TPU v7x, 512 devices: a whole 4x8x8 slice. The times are simulated.
512 devices in a mesh: seq: 64 (over y_lo, z, x), uly: 8 (over y_hi, core).
Axes of the slice: x: 4, y: 8 (y_hi: 4, y_lo: 2; y = y_hi * 2 + y_lo), z: 8, core: 2. Of those that a mesh axis runs over, the one named last changes fastest.
Arguments:
- queries: bfloat16 [2, 32768, 2048], P(None, ('seq', 'uly')), may hold values from -22.5 to 22.5
- keys: bfloat16 [2, 32768, 2048], P(None, ('seq', 'uly')), may hold values from -22.5 to 22.5
- values: bfloat16 [2, 32768, 2048], P(None, ('seq', 'uly')), may hold values from -6 to 6
- query_tan: bfloat16 [2, 32768, 2048], P(None, ('seq', 'uly')), may hold values from -6 to 6
- key_tan: bfloat16 [2, 32768, 2048], P(None, ('seq', 'uly')), may hold values from -6 to 6
- value_tan: bfloat16 [2, 32768, 2048], P(None, ('seq', 'uly')), may hold values from -6 to 6
- weight_out: float32 [2048, 1536], P(None, 'seq'), may hold values from -0.125 to 0.125
- gate: float32 [2, 1536], replicated, may hold values from -5 to 5
- gate_tan: float32 [2, 1536], replicated, may hold values from -5 to 5
- cotangent: bfloat16 [2, 32768, 1536], P(None, ('seq', 'uly')), may hold values from -24 to 24
Outputs:
- mixed: bfloat16 [2, 32768, 1536], P(None, ('seq', 'uly'))
- mixed_tan: bfloat16 [2, 32768, 1536], P(None, ('seq', 'uly'))
- weight_grad: float32 [2048, 1536], P('uly', 'seq')
All inputs are finite; a program needn't handle non-finite values.
Results may differ from a plain program's by a relative error of at most 0.0064.
Values may be sent and summed in bfloat16 or wider, within the bound.
No kernel may reach another device: no remote copies, remote signals or barrier semaphores. Data moves between devices by JAX's collectives and lax.ppermute only.
A program may use at most 64 MiB of HBM per device.

v0:
```python
import jax
import jax.numpy as jnp
from jax import lax
from jax.sharding import PartitionSpec as P

HD = 128


def extended(cells, sides, width):
    for axis, dim in sides:
        count = lax.axis_size(axis)
        ends = count - 1
        head = lax.slice_in_dim(cells, 0, width, axis=dim)
        tail = lax.slice_in_dim(cells, cells.shape[dim] - width, cells.shape[dim], axis=dim)
        cells = jnp.concatenate(
            [
                lax.ppermute(tail, axis, [(i, (i + 1) % count) for i in range(ends)]),
                cells,
                lax.ppermute(head, axis, [((i + 1) % count, i) for i in range(ends)]),
            ],
            axis=dim,
        )
    return cells


def contract(form, left, right):
    return jnp.einsum(form, left, right, preferred_element_type=jnp.float32)


def attend_block(query_blk, key_blk, value_blk, query_tan_blk, key_tan_blk, value_tan_blk, allowed):
    score_scale = HD ** (-0.5)
    scores = contract("sqhd,skhd->shqk", query_blk, key_blk) * score_scale
    scores = jnp.where(allowed, scores, -1e30)
    row_top = jnp.max(scores, axis=-1, keepdims=True)
    exp_terms = jnp.where(allowed, jnp.exp(scores - row_top), 0.0)
    probs_full = exp_terms / jnp.sum(exp_terms, axis=-1, keepdims=True)
    score_tan = (
        contract("sqhd,skhd->shqk", query_tan_blk, key_blk)
        + contract("sqhd,skhd->shqk", query_blk, key_tan_blk)
    ) * score_scale
    probs_tan = probs_full * (score_tan - jnp.sum(probs_full * score_tan, axis=-1, keepdims=True))
    probs_low = probs_full.astype(jnp.bfloat16)
    probs_tan_low = probs_tan.astype(jnp.bfloat16)
    attended = contract("shqk,skhd->sqhd", probs_low, value_blk)
    attended_tan = contract("shqk,skhd->sqhd", probs_tan_low, value_blk) + contract(
        "shqk,skhd->sqhd", probs_low, value_tan_blk
    )
    return (attended.astype(jnp.bfloat16), attended_tan.astype(jnp.bfloat16))


def on_device(
    queries, keys, values, query_tan, key_tan, value_tan, weight_out, gate, gate_tan, cotangent
):
    shard_count = lax.axis_size("seq")
    moved = (
        lax.all_to_all(queries, "uly", split_axis=2, concat_axis=1, tiled=True),
        lax.all_to_all(keys, "uly", split_axis=2, concat_axis=1, tiled=True),
        lax.all_to_all(values, "uly", split_axis=2, concat_axis=1, tiled=True),
        lax.all_to_all(query_tan, "uly", split_axis=2, concat_axis=1, tiled=True),
        lax.all_to_all(key_tan, "uly", split_axis=2, concat_axis=1, tiled=True),
        lax.all_to_all(value_tan, "uly", split_axis=2, concat_axis=1, tiled=True),
    )
    query_here, key_here, value_here, query_tan_here, key_tan_here, value_tan_here = moved
    seq_rows, block_len, local_width = query_here.shape
    radius = block_len // 4
    head_local = local_width // HD
    stacked = jnp.stack([key_here, value_here, key_tan_here, value_tan_here])
    widened = extended(stacked, (("seq", 2),), radius)
    sub_len = 2 * radius
    sub_count = block_len // sub_len
    key_span = 2 * sub_len
    row_ids = jnp.arange(sub_len, dtype=jnp.int32)
    key_ids = jnp.arange(key_span, dtype=jnp.int32)
    nearby = jnp.abs(row_ids[:, None] + radius - key_ids[None, :]) <= radius
    first_pos = lax.axis_index("seq") * block_len
    sub_starts = jnp.arange(sub_count, dtype=jnp.int32) * sub_len
    key_pos = first_pos + sub_starts[:, None] - radius + key_ids[None, :]
    inside = (key_pos >= 0) & (key_pos < block_len * shard_count)
    allowed = nearby[None, None, :, :] & inside[:, None, None, :]

    def split_rows(tensor):
        return tensor.reshape(sub_count, sub_len, head_local, HD)

    def split_keys(tensor):
        return jnp.stack(
            [
                tensor[index * sub_len : index * sub_len + key_span].reshape(
                    key_span, head_local, HD
                )
                for index in range(sub_count)
            ]
        )

    def one_sequence(items):
        query_one, key_one, value_one, query_tan_one, key_tan_one, value_tan_one = items
        return attend_block(
            split_rows(query_one),
            split_keys(key_one),
            split_keys(value_one),
            split_rows(query_tan_one),
            split_keys(key_tan_one),
            split_keys(value_tan_one),
            allowed,
        )

    attended, attended_tan = lax.map(
        one_sequence, (query_here, widened[0], widened[1], query_tan_here, widened[2], widened[3])
    )
    att_head = attended.reshape(seq_rows, block_len, local_width)
    att_head_tan = attended_tan.reshape(seq_rows, block_len, local_width)
    returned = (
        lax.all_to_all(att_head, "uly", split_axis=1, concat_axis=2, tiled=True),
        lax.all_to_all(att_head_tan, "uly", split_axis=1, concat_axis=2, tiled=True),
    )
    token_att, token_att_tan = returned
    seg_len = token_att.shape[1]
    full_width = token_att.shape[2]
    token_rows = seq_rows * seg_len
    flat_att = token_att.reshape(token_rows, full_width)
    flat_att_tan = token_att_tan.reshape(token_rows, full_width)
    out_width = weight_out.shape[1] * shard_count
    shard_piece = lax.all_gather(weight_out.astype(jnp.bfloat16), "seq", axis=1, tiled=True)
    projected = jnp.stack(
        [
            jnp.dot(flat_att, shard_piece, preferred_element_type=jnp.float32),
            jnp.dot(flat_att_tan, shard_piece, preferred_element_type=jnp.float32),
        ]
    )
    projection = projected[0].reshape(seq_rows, seg_len, out_width)
    projection_tan = projected[1].reshape(seq_rows, seg_len, out_width)
    gate_rows = gate[:, None, :]
    mixed = (gate_rows * projection).astype(jnp.bfloat16)
    mixed_tan = (gate_tan[:, None, :] * projection + gate_rows * projection_tan).astype(
        jnp.bfloat16
    )
    weighted = (gate_rows * cotangent.astype(jnp.float32)).astype(jnp.bfloat16)
    partial_grad = jnp.einsum(
        "stf,std->fd",
        att_head,
        lax.all_gather(weighted, "uly", axis=1, tiled=True),
        preferred_element_type=jnp.float32,
    )
    weight_grad = lax.psum_scatter(partial_grad, "seq", scatter_dimension=1, tiled=True)
    return (mixed, mixed_tan, weight_grad)


def solution(mesh):
    return jax.shard_map(
        on_device,
        mesh=mesh,
        in_specs=(
            P(None, ("seq", "uly"), None),
            P(None, ("seq", "uly"), None),
            P(None, ("seq", "uly"), None),
            P(None, ("seq", "uly"), None),
            P(None, ("seq", "uly"), None),
            P(None, ("seq", "uly"), None),
            P(None, "seq"),
            P(),
            P(),
            P(None, ("seq", "uly"), None),
        ),
        out_specs=(P(None, ("seq", "uly"), None), P(None, ("seq", "uly"), None), P("uly", "seq")),
        check_vma=False,
    )
```

profile of v0, /device:TPU:40, one launch (start us, length us, event | category | flops | bytes accessed | tf_op | source)
XLA Modules:
  0.0 756.1 jit_solution(14577524558048879883)
XLA Ops:
  7.2 2.4 copy.74
  9.6 1.5 reshape.154
  11.1 7.2 all-to-all-start.3
  18.3 0.8 copy.71
  19.1 1.5 reshape.156
  20.6 9.0 %all-to-all-done.3 = bf16[8,2,16384]{2,1,0:T(2,128)(2,1)S(1)} async-done(((bf16[8,2,16384]{2,1,0:T(2,128)(2,1)}), bf16[8,2,16384]{2,1,0:T(2,128)(2,1)S(1)}, u32[]{:S(2)}, u32[]{:S(2)}) %all-to-all-start.3) | async-done | bytes 524320 | tf_op jit(solution)/shard_map/all_to_all | solution.py:61
  29.6 10.5 %all-to-all-start.2 = ((bf16[8,2,16384]{2,1,0:T(2,128)(2,1)}), bf16[8,2,16384]{2,1,0:T(2,128)(2,1)S(1)}, u32[]{:S(2)}, u32[]{:S(2)}) async-start(bf16[8,2,16384]{2,1,0:T(2,128)(2,1)} %reshape.156), calls=%async_computation.2 | async-start | bytes 1048576 | tf_op jit(solution)/shard_map/all_to_all | solution.py:60
  40.8 0.8 copy.68
  41.6 1.5 reshape.158
  43.1 10.0 %all-to-all-done.2 = bf16[8,2,16384]{2,1,0:T(2,128)(2,1)S(1)} async-done(((bf16[8,2,16384]{2,1,0:T(2,128)(2,1)}), bf16[8,2,16384]{2,1,0:T(2,128)(2,1)S(1)}, u32[]{:S(2)}, u32[]{:S(2)}) %all-to-all-start.2) | async-done | bytes 524320 | tf_op jit(solution)/shard_map/all_to_all | solution.py:60
  53.1 8.2 %all-to-all-start.1 = ((bf16[8,2,16384]{2,1,0:T(2,128)(2,1)}), bf16[8,2,16384]{2,1,0:T(2,128)(2,1)S(1)}, u32[]{:S(2)}, u32[]{:S(2)}) async-start(bf16[8,2,16384]{2,1,0:T(2,128)(2,1)} %reshape.158), calls=%async_computation.1 | async-start | bytes 1048576 | tf_op jit(solution)/shard_map/all_to_all | solution.py:58
  61.2 0.7 copy.65
  62.0 1.6 reshape.160
  63.5 12.2 %all-to-all-done.1 = bf16[8,2,16384]{2,1,0:T(2,128)(2,1)S(1)} async-done(((bf16[8,2,16384]{2,1,0:T(2,128)(2,1)}), bf16[8,2,16384]{2,1,0:T(2,128)(2,1)S(1)}, u32[]{:S(2)}, u32[]{:S(2)}) %all-to-all-start.1) | async-done | bytes 524320 | tf_op jit(solution)/shard_map/all_to_all | solution.py:58
  75.8 8.8 %all-to-all-start = ((bf16[8,2,16384]{2,1,0:T(2,128)(2,1)}), bf16[8,2,16384]{2,1,0:T(2,128)(2,1)S(1)}, u32[]{:S(2)}, u32[]{:S(2)}) async-start(bf16[8,2,16384]{2,1,0:T(2,128)(2,1)} %reshape.160), calls=%async_computation | async-start | bytes 1048576 | tf_op jit(solution)/shard_map/all_to_all | solution.py:57
  84.6 2.3 copy.77
  87.0 1.5 reshape.162
  88.4 12.5 %all-to-all-done = bf16[8,2,16384]{2,1,0:T(2,128)(2,1)S(1)} async-done(((bf16[8,2,16384]{2,1,0:T(2,128)(2,1)}), bf16[8,2,16384]{2,1,0:T(2,128)(2,1)S(1)}, u32[]{:S(2)}, u32[]{:S(2)}) %all-to-all-start) | async-done | bytes 524320 | tf_op jit(solution)/shard_map/all_to_all | solution.py:57
  100.9 0.8 copy-done.10
  101.7 8.1 %all-to-all-start.4 = ((bf16[8,2,16384]{2,1,0:T(2,128)(2,1)}), bf16[8,2,16384]{2,1,0:T(2,128)(2,1)S(1)}, u32[]{:S(2)}, u32[]{:S(2)}) async-start(bf16[8,2,16384]{2,1,0:T(2,128)(2,1)} %reshape.162), calls=%async_computation.4 | async-start | bytes 1048576 | tf_op jit(solution)/shard_map/all_to_all | solution.py:56
  109.8 2.4 copy.79
  112.2 1.5 reshape.164
  113.7 10.8 %all-to-all-done.4 = bf16[8,2,16384]{2,1,0:T(2,128)(2,1)S(1)} async-done(((bf16[8,2,16384]{2,1,0:T(2,128)(2,1)}), bf16[8,2,16384]{2,1,0:T(2,128)(2,1)S(1)}, u32[]{:S(2)}, u32[]{:S(2)}) %all-to-all-start.4) | async-done | bytes 524320 | tf_op jit(solution)/shard_map/all_to_all | solution.py:56
  124.5 8.9 %all-to-all-start.5 = ((bf16[8,2,16384]{2,1,0:T(2,128)(2,1)}), bf16[8,2,16384]{2,1,0:T(2,128)(2,1)}, u32[]{:S(2)}, u32[]{:S(2)}) async-start(bf16[8,2,16384]{2,1,0:T(2,128)(2,1)} %reshape.164), calls=%async_computation.5 | async-start | bytes 1048576 | tf_op jit(solution)/shard_map/all_to_all | solution.py:59
  137.7 3.0 reshape.161
  141.4 1.1 pad_maximum_fusion.16
  142.5 12.3 %collective-permute-start.1 = (bf16[4,2,128,256]{3,2,1,0:T(8,128)(2,1)}, bf16[4,2,128,256]{3,2,1,0:T(8,128)(2,1)}, u32[]{:S(2)}, u32[]{:S(2)}) collective-permute-start(bf16[4,2,128,256]{3,2,1,0:T(8,128)(2,1)} %get-tuple-element.162), channel_id=1, source_target_pairs={{8,0},{16,8},{24,16},{32,24},{40,32},{48,40},{56,48},{64,56},{72,6... | collective-permute-start | bytes 1572872 | tf_op jit(solution)/shard_map/ppermute | solution.py:19
  154.8 1.9 collective-permute-start
  157.0 3.2 reshape.163
  160.2 1.9 copy.78
  162.1 3.0 reshape.165
  165.1 1.9 copy.80
  166.9 2.4 collective-permute-done.1
  169.4 8.6 %collective-permute-done = bf16[4,2,128,256]{3,2,1,0:T(8,128)(2,1)} collective-permute-done((bf16[4,2,128,256]{3,2,1,0:T(8,128)(2,1)}, bf16[4,2,128,256]{3,2,1,0:T(8,128)(2,1)}, u32[]{:S(2)}, u32[]{:S(2)}) %collective-permute-start) | collective-permute-done | bytes 524320 | tf_op jit(solution)/shard_map/ppermute | solution.py:17
  178.0 1.3 pad_maximum_fusion.12
  179.3 1.4 slice_bitcast_fusion
  180.7 38.3 %while.13 = (s32[]{:T(128)}, bf16[2,2,256,2,128]{4,3,2,1,0:T(2,128)(2,1)}, bf16[2,2,256,2,128]{4,3,0,2,1:T(2,128)(2,1)}, bf16[2,768,256]{2,1,0:T(8,128)(2,1)S(1)...) while((s32[]{:T(128)}, ...), condition=%wide.region_4.5_spmd.clone, body=%wide.region_0.4_spmd.clone.sunk | while | flops 816971264 | bytes 74348096 | solution.py:106
  182.1 1.1 constant_dynamic-slice_fusion.14
  183.3 2.5 fusion.76
  185.8 2.2 fusion.77
  188.4 0.8 copy-done.15
  189.7 1.3 constant_dynamic-slice_fusion.15
  191.7 2.5 multiply_reduce_fusion.2
  194.2 1.5 fusion.79
  196.0 2.4 fusion.80
  199.0 0.8 copy-done.17
  201.3 1.1 constant_dynamic-slice_fusion.14
  202.4 2.5 fusion.76
  204.9 2.2 fusion.77
  207.5 0.8 copy-done.15
  208.9 1.3 constant_dynamic-slice_fusion.15
  210.8 2.5 multiply_reduce_fusion.2
  213.3 1.5 fusion.79
  215.2 2.4 fusion.80
  218.2 0.8 copy-done.17
  219.0 1.4 reshape.139
  220.9 18.6 %all_to_all.126 = bf16[2,512,256]{2,0,1:T(2,128)(2,1)S(1)} all-to-all(bf16[2,512,256]{2,0,1:T(2,128)(2,1)S(1)} %copy.86), channel_id=1, replica_groups=mesh['seq'=64,'uly'=8] {'uly'}, dimensions={1} | all-to-all | bytes 1048576 | tf_op jit(solution)/shard_map/all_to_all | solution.py:112
  240.0 132.7 %all-gather.3.cloned.1.call-done = bf16[2048,1536]{0,1:T(8,128)(2,1)} async-done(((bf16[2048,24]{0,1:T(8,128)(2,1)}), bf16[2048,1536]{0,1:T(8,128)(2,1)}) %all-gather.3.cloned.1.call-update) | async-done | bytes 6291472 | tf_op jit(solution)/shard_map/all_gather | solution.py:122
  372.8 5.8 multiply_convert_fusion.2
  378.6 42.8 %all-gather.5.cloned.1.call-done = bf16[2,512,1536]{2,1,0:T(8,128)(2,1)} async-done(((bf16[2,64,1536]{2,1,0:T(8,128)(2,1)}), bf16[2,512,1536]{2,1,0:T(8,128)(2,1)}) %all-gather.5.cloned.1.call-update) | async-done | bytes 3145744 | tf_op jit(solution)/shard_map/all_gather | solution.py:140
  421.4 4.4 convolution_bitcast_fusion
  426.1 18.9 %all_to_all.127 = bf16[2,512,256]{2,0,1:T(2,128)(2,1)S(1)} all-to-all(bf16[2,512,256]{2,0,1:T(2,128)(2,1)S(1)} %reshape.153), channel_id=1, replica_groups=mesh['seq'=64,'uly'=8] {'uly'}, dimensions={1} | all-to-all | bytes 1048576 | tf_op jit(solution)/shard_map/all_to_all | solution.py:113
  445.1 5.7 fusion.51
  450.9 298.7 %reduce-scatter.2.cloned.1.call-done = f32[256,24]{0,1:T(8,128)} async-done(((f32[256,1536]{0,1:T(8,128)}), f32[256,24]{0,1:T(8,128)}) %reduce-scatter.2.cloned.1.call-update) | async-done | bytes 24592 | tf_op jit(solution)/shard_map/reduce_scatter | solution.py:143
  (140 shorter events, 15.2 us)
Async XLA Ops:
  7.2 11.1 %copy-start.11 = (bf16[2,64,2048]{2,1,0:T(8,128)(2,1)S(1)}, bf16[2,64,2048]{2,1,0:T(8,128)(2,1)}, u32[]{:S(2)}) copy-start(bf16[2,64,2048]{2,1,0:T(8,128)(2,1)} %param.16) | copy-start | bytes 1572868
  11.1 18.5 %all-to-all-start.3 = ((bf16[8,2,16384]{2,1,0:T(2,128)(2,1)}), bf16[8,2,16384]{2,1,0:T(2,128)(2,1)S(1)}, u32[]{:S(2)}, u32[]{:S(2)}) async-start(bf16[8,2,16384]{2,1,0:T(2,128)(2,1)} %reshape.154), calls=%async_computation.3 | async-start | bytes 1048576 | tf_op jit(solution)/shard_map/all_to_all | solution.py:61
  18.3 21.8 %copy-start.20 = (f32[2048,24]{0,1:T(8,128)S(1)}, f32[2048,24]{0,1:T(8,128)}, u32[]{:S(2)}) copy-start(f32[2048,24]{0,1:T(8,128)} %param.18) | copy-start | bytes 589828
  18.3 22.5 %copy-start.12 = (bf16[2,64,2048]{2,1,0:T(8,128)(2,1)S(1)}, bf16[2,64,2048]{2,1,0:T(8,128)(2,1)}, u32[]{:S(2)}) copy-start(bf16[2,64,2048]{2,1,0:T(8,128)(2,1)} %param.14) | copy-start | bytes 1572868
  29.6 23.5 %all-to-all-start.2 = ((bf16[8,2,16384]{2,1,0:T(2,128)(2,1)}), bf16[8,2,16384]{2,1,0:T(2,128)(2,1)S(1)}, u32[]{:S(2)}, u32[]{:S(2)}) async-start(bf16[8,2,16384]{2,1,0:T(2,128)(2,1)} %reshape.156), calls=%async_computation.2 | async-start | bytes 1048576 | tf_op jit(solution)/shard_map/all_to_all | solution.py:60
  40.1 332.7 %all-gather.3.cloned.1.call-start = ((), (), s32[]{:S(2)}) async-start(), calls=%async_computation.9 | async-start | bytes 6389760 | tf_op jit(solution)/shard_map/all_gather | solution.py:122
  40.8 20.4 %copy-start.13 = (bf16[2,64,2048]{2,1,0:T(8,128)(2,1)S(1)}, bf16[2,64,2048]{2,1,0:T(8,128)(2,1)}, u32[]{:S(2)}) copy-start(bf16[2,64,2048]{2,1,0:T(8,128)(2,1)} %param.13) | copy-start | bytes 1572868
  53.1 22.7 %all-to-all-start.1 = ((bf16[8,2,16384]{2,1,0:T(2,128)(2,1)}), bf16[8,2,16384]{2,1,0:T(2,128)(2,1)S(1)}, u32[]{:S(2)}, u32[]{:S(2)}) async-start(bf16[8,2,16384]{2,1,0:T(2,128)(2,1)} %reshape.158), calls=%async_computation.1 | async-start | bytes 1048576 | tf_op jit(solution)/shard_map/all_to_all | solution.py:58
  75.8 25.2 %all-to-all-start = ((bf16[8,2,16384]{2,1,0:T(2,128)(2,1)}), bf16[8,2,16384]{2,1,0:T(2,128)(2,1)S(1)}, u32[]{:S(2)}, u32[]{:S(2)}) async-start(bf16[8,2,16384]{2,1,0:T(2,128)(2,1)} %reshape.160), calls=%async_computation | async-start | bytes 1048576 | tf_op jit(solution)/shard_map/all_to_all | solution.py:57
  100.9 0.8 copy-start.10
  101.7 22.8 %all-to-all-start.4 = ((bf16[8,2,16384]{2,1,0:T(2,128)(2,1)}), bf16[8,2,16384]{2,1,0:T(2,128)(2,1)S(1)}, u32[]{:S(2)}, u32[]{:S(2)}) async-start(bf16[8,2,16384]{2,1,0:T(2,128)(2,1)} %reshape.162), calls=%async_computation.4 | async-start | bytes 1048576 | tf_op jit(solution)/shard_map/all_to_all | solution.py:56
  124.5 8.9 %copy-start.9 = (bf16[8,2,16384]{2,1,0:T(2,128)(2,1)}, bf16[8,2,16384]{2,1,0:T(2,128)(2,1)S(1)}, u32[]{:S(2)}) copy-start(bf16[8,2,16384]{2,1,0:T(2,128)(2,1)S(1)} %all-to-all-done.4) | copy-start | bytes 1572868
  124.5 37.5 %all-to-all-start.5 = ((bf16[8,2,16384]{2,1,0:T(2,128)(2,1)}), bf16[8,2,16384]{2,1,0:T(2,128)(2,1)}, u32[]{:S(2)}, u32[]{:S(2)}) async-start(bf16[8,2,16384]{2,1,0:T(2,128)(2,1)} %reshape.164), calls=%async_computation.5 | async-start | bytes 1048576 | tf_op jit(solution)/shard_map/all_to_all | solution.py:59
  133.4 287.9 %all-gather.5.cloned.1.call-start = ((), (), s32[]{:S(2)}) async-start(), calls=%async_computation.10 | async-start | bytes 3538944 | tf_op jit(solution)/shard_map/all_gather | solution.py:140
  142.5 26.9 %collective-permute-start.1 = (bf16[4,2,128,256]{3,2,1,0:T(8,128)(2,1)}, bf16[4,2,128,256]{3,2,1,0:T(8,128)(2,1)}, u32[]{:S(2)}, u32[]{:S(2)}) collective-permute-start(bf16[4,2,128,256]{3,2,1,0:T(8,128)(2,1)} %get-tuple-element.162), channel_id=1, source_target_pairs={{8,0},{16,8},{24,16},{32,24},{40,32},{48,40},{56,48},{64,56},{72,6... | collective-permute-start | bytes 1572872 | tf_op jit(solution)/shard_map/ppermute | solution.py:19
  154.8 23.2 %collective-permute-start = (bf16[4,2,128,256]{3,2,1,0:T(8,128)(2,1)}, bf16[4,2,128,256]{3,2,1,0:T(8,128)(2,1)}, u32[]{:S(2)}, u32[]{:S(2)}) collective-permute-start(bf16[4,2,128,256]{3,2,1,0:T(8,128)(2,1)} %get-tuple-element.161), channel_id=1, source_target_pairs={{0,8},{8,16},{16,24},{24,32},{32,40},{40,48},{48,56},{56,64},{64,7... | collective-permute-start | bytes 1572872 | tf_op jit(solution)/shard_map/ppermute | solution.py:17
  180.7 0.9 copy-start
  180.7 1.1 copy-start.2
  180.9 4.9 copy-start.4
  181.0 4.7 copy-start.6
  183.3 4.7 copy-start.8
  185.8 2.4 copy-start.14
  188.4 0.8 copy-start.15
  191.7 2.5 copy-start.5
  191.7 2.5 copy-start.7
  191.7 2.5 copy-start.23
  196.0 2.6 copy-start.16
  196.0 3.8 copy-start.1
  196.0 3.8 copy-start.3
  199.0 0.8 copy-start.17
  199.8 0.9 copy-start
  199.8 1.1 copy-start.2
  200.0 4.8 copy-start.4
  200.2 4.7 copy-start.6
  202.4 4.7 copy-start.8
  204.9 2.4 copy-start.14
  207.5 0.8 copy-start.15
  210.8 2.5 copy-start.5
  210.8 2.5 copy-start.7
  210.8 2.5 copy-start.23
  215.1 2.6 copy-start.16
  215.2 3.8 copy-start.1
  215.2 3.8 copy-start.3
  218.1 0.8 copy-start.17
  220.3 152.4 %copy-start.19 = (bf16[2,64,1536]{2,1,0:T(8,128)(2,1)S(1)}, bf16[2,64,1536]{2,1,0:T(8,128)(2,1)}, u32[]{:S(2)}) copy-start(bf16[2,64,1536]{2,1,0:T(8,128)(2,1)} %param.21) | copy-start | bytes 1179652
  220.3 152.4 %copy-start.21 = (f32[2,1536]{1,0:T(2,128)S(1)}, f32[2,1536]{1,0:T(2,128)}, u32[]{:S(2)}) copy-start(f32[2,1536]{1,0:T(2,128)} %param.19) | copy-start | bytes 36868
  378.5 47.2 %copy-start.18 = (bf16[2,2,256,2,128]{4,3,0,2,1:T(2,128)(2,1)S(1)}, bf16[2,2,256,2,128]{4,3,0,2,1:T(2,128)(2,1)}, u32[]{:S(2)}) copy-start(bf16[2,2,256,2,128]{4,3,0,2,1:T(2,128)(2,1)} %get-tuple-element.57) | copy-start | bytes 1572868
  378.5 371.1 %reduce-scatter.2.cloned.1.call-start = ((), (), s32[]{:S(2)}) async-start(), calls=%async_computation.11 | async-start | bytes 1597440 | tf_op jit(solution)/shard_map/reduce_scatter | solution.py:143
  425.8 19.3 %copy-start.22 = (f32[2,1536]{1,0:T(2,128)S(1)}, f32[2,1536]{1,0:T(2,128)}, u32[]{:S(2)}) copy-start(f32[2,1536]{1,0:T(2,128)} %param.20) | copy-start | bytes 36868
Sparse Core Ops, SparseCore 0:
  43.0 329.7 all-gather.2
  378.7 42.6 all-gather.4
  425.9 323.6 reduce-scatter.1
where the time goes:
time: 757 us; the launch traced here: 756 us
  waiting for transfers between devices  540 us (71%)
  starting transfers between devices  66 us (9%)
  local copies, waits for them, and re-layouts  55.8 us (7%)
  matrix products  38.9 us (5%)
  blocking collectives  37.4 us (5%)
  between operations  14 us (2%)
    reduce_scatter x1, waiting for transfers between devices, on_device(): lax.psum_scatter(partial_grad, 'seq', scatter_dimension=1, tiled=True)  299 us
    all_gather x1, waiting for transfers between devices, on_device(): lax.all_gather(weight_out.astype(jnp.bfloat16), 'seq', axis=1, tiled=True)  133 us
    all_gather x1, waiting for transfers between devices, on_device(): lax.all_gather(weighted, 'uly', axis=1, tiled=True)  42.8 us
    unnamed x38, local copies, waits for them, and re-layouts  30.4 us
    all_to_all x1, blocking collectives, on_device(): lax.all_to_all(att_head_tan, 'uly', split_axis=1, concat_axis=2, tiled=True)  18.9 us
    all_to_all x1, blocking collectives, on_device(): lax.all_to_all(att_head, 'uly', split_axis=1, concat_axis=2, tiled=True)  18.6 us
    dot_general x10, matrix products, contract(): return jnp.einsum(form, left, right, preferred_element_type=jnp.float32)  18.1 us
  transfers between devices with their start and end apart: 11, of which 10 were waited for; matrix products, arithmetic and copies ran while one was open for 11% of the time, Pallas kernels for 0%

commit v1 on v0

v1 whole, which is shorter than its diff:
```python
import functools

import jax
import jax.numpy as jnp
from jax import lax
from jax.experimental import pallas as pl
from jax.experimental.pallas import tpu as pltpu
from jax.sharding import PartitionSpec as P

AXES = ("seq", "uly")
NX, NZ, NYL, NYH, NC = 4, 8, 2, 4, 2
HD = 128
PAIR = 2 * HD
NJ = 4
GROUP = NJ * PAIR
SCALE = HD ** (-0.5)
BF = jnp.bfloat16
F32 = jnp.float32


def device_of(x, yl, yh, z, c):
    return ((yl * NZ + z) * NX + x) * (NYH * NC) + yh * NC + c


def all_places():
    for x in range(NX):
        for yl in range(NYL):
            for yh in range(NYH):
                for z in range(NZ):
                    for c in range(NC):
                        yield x, yl, yh, z, c


def moves(rule):
    return sorted((device_of(*p), device_of(*rule(*p))) for p in all_places())


SWAP_CORE = moves(lambda x, yl, yh, z, c: (x, yl, yh, z, 1 - c))
SWAP_YLO = moves(lambda x, yl, yh, z, c: (x, 1 - yl, yh, z, c))
TURN = moves(lambda x, yl, yh, z, c: (yh, yl, x, z, c))


def swap_z(bit):
    return moves(lambda x, yl, yh, z, c: (x, yl, yh, z ^ bit, c))


def shift_x(by):
    return moves(lambda x, yl, yh, z, c: ((x + by) % NX, yl, yh, z, c))


COUNT = NX * NYL * NYH * NZ * NC
TO_NEXT = [(d, d + NC) for d in range(COUNT - NC)]
TO_PREV = [(d + NC, d) for d in range(COUNT - NC)]
GROUPS_X = [
    [device_of(x, yl, yh, z, c) for x in range(NX)]
    for yl in range(NYL) for yh in range(NYH) for z in range(NZ) for c in range(NC)
]
GROUPS_Z = [
    [device_of(x, yl, yh, z, c) for z in range(NZ)]
    for yl in range(NYL) for yh in range(NYH) for x in range(NX) for c in range(NC)
]
GROUPS_Y = [
    [device_of(x, yl, yh, z, c) for yl in range(NYL) for yh in range(NYH)]
    for z in range(NZ) for x in range(NX) for c in range(NC)
]


def send(array, pairs):
    return lax.ppermute(array, AXES, pairs)


def nt(left, right):
    return lax.dot_general(left, right, (((1,), (1,)), ((), ())), preferred_element_type=F32)


def nn(left, right):
    return lax.dot_general(left, right, (((1,), (0,)), ((), ())), preferred_element_type=F32)


def vmem_spec():
    return pl.BlockSpec(memory_space=pltpu.VMEM)


def smem_spec():
    return pl.BlockSpec(memory_space=pltpu.SMEM)


def params(*semantics):
    return pltpu.CompilerParams(
        vmem_limit_bytes=40 * 2**20, dimension_semantics=semantics or None
    )


def cost(flops, nbytes, trans=0):
    return pl.CostEstimate(flops=flops, bytes_accessed=nbytes, transcendentals=trans)


def group_cols(ref, s, j, side):
    return ref[s, :, pl.ds(pl.multiple_of(j * 2 * PAIR + side * PAIR, PAIR), PAIR)]


def split_body(meta, *refs, count, with_own):
    core = meta[0]
    ins, outs = refs[:count], refs[count:]
    for a in range(count):
        for s in range(2):
            for j in range(NJ):
                cols = slice(j * PAIR, (j + 1) * PAIR)
                if with_own:
                    outs[1][a, s, :, cols] = group_cols(ins[a], s, j, core)
                outs[0][a, s, :, cols] = group_cols(ins[a], s, j, 1 - core)


def split_groups(meta, arrays, with_own):
    count = len(arrays)
    seqs, rows, _ = arrays[0].shape
    shape = jax.ShapeDtypeStruct((count, seqs, rows, GROUP), BF)
    outs = [shape, shape] if with_own else [shape]
    return pl.pallas_call(
        functools.partial(split_body, count=count, with_own=with_own),
        out_shape=outs,
        in_specs=[smem_spec()] + [vmem_spec()] * count,
        out_specs=[vmem_spec()] * len(outs),
        compiler_params=params(),
        cost_estimate=cost(0, count * 2**20),
    )(meta, *arrays)


def join_body(meta, kt, vt, got, first, second):
    core = meta[0]
    rows = kt.shape[1]
    for a, ref in enumerate((kt, vt)):
        for s in range(2):
            for j in range(NJ):
                out = first if j < NJ // 2 else second
                cols = slice((j % 2) * PAIR, (j % 2 + 1) * PAIR)
                out[a, s, :rows, cols] = group_cols(ref, s, j, core)
                out[a, s, rows:, cols] = got[2 + a, s, :, j * PAIR : (j + 1) * PAIR]


def join_rows(meta, kt, vt, got):
    seqs, rows, _ = kt.shape
    shape = jax.ShapeDtypeStruct((2, seqs, 2 * rows, GROUP // 2), BF)
    return pl.pallas_call(
        join_body,
        out_shape=[shape, shape],
        in_specs=[smem_spec()] + [vmem_spec()] * 3,
        out_specs=[vmem_spec()] * 2,
        compiler_params=params(),
        cost_estimate=cost(0, 3 * 2**20),
    )(meta, kt, vt, got)


def allowed_keys(meta):
    core, chunk = meta[0], meta[1]
    span = 2 * 64
    shape = (span, 3 * span)
    rows = lax.broadcasted_iota(jnp.int32, shape, 0)
    cols = lax.broadcasted_iota(jnp.int32, shape, 1)
    q_pos = (rows + 64 * core) & (span - 1)
    k_pos = (cols + 64 * core) & (span - 1)
    block = cols >> 7
    before = (block == 0) & (k_pos >= q_pos) & (chunk > 0)
    after = (block == 2) & (k_pos <= q_pos) & (chunk < COUNT // NC - 1)
    return before | (block == 1) | after


def probs_of(q, k, mask):
    scores = jnp.where(mask, nt(q, k) * SCALE, -1e30)
    top = jnp.max(scores, axis=-1, keepdims=True)
    terms = jnp.exp(scores - top)
    return terms / jnp.sum(terms, axis=-1, keepdims=True)


def rows_of(refs, a, cols):
    return jnp.concatenate([ref[a, 0, :, cols] for ref in refs], axis=0)


def attend_body(meta, q_own, q_sib, lo, ls, mo, ms, ro, rs, quarter, out_own, out_sib):
    mask = allowed_keys(meta)
    keyed = (lo, ls, mo, ms, ro, rs)
    half = q_own.shape[1]
    for n in range(2):
        cols = slice(n * HD, (n + 1) * HD)
        q = jnp.concatenate([q_own[0, :, cols], q_sib[0, 0, :, cols]], axis=0)
        probs = probs_of(q, rows_of(keyed, 0, cols), mask).astype(BF)
        att = nn(probs, rows_of(keyed, 1, cols)).astype(BF)
        quarter[0, 0, 0, :, cols] = att[:half]
        quarter[0, 1, 0, :, cols] = att[half:]
        out_own[0, :, cols] = att[:half]
        out_sib[0, :, cols] = att[half:]


def attend(meta, queries, got, keyed):
    seqs, rows, _ = queries.shape
    pair = pl.BlockSpec((2, 1, rows, PAIR), lambda s, j, m: (0, s, 0, j))
    flat = pl.BlockSpec((1, rows, PAIR), lambda s, j, m: (s, 0, j))
    wide = jax.ShapeDtypeStruct((seqs, rows, GROUP), BF)
    return pl.pallas_call(
        attend_body,
        out_shape=[jax.ShapeDtypeStruct((NJ, 2, seqs, rows, PAIR), BF), wide, wide],
        grid_spec=pltpu.PrefetchScalarGridSpec(
            num_scalar_prefetch=1,
            grid=(seqs, NJ),
            in_specs=[
                pl.BlockSpec((1, rows, PAIR), lambda s, j, m: (s, 0, 2 * j + m[0])),
                pl.BlockSpec((1, 1, rows, PAIR), lambda s, j, m: (0, s, 0, j)),
            ]
            + [pair] * 6,
            out_specs=[
                pl.BlockSpec((1, 2, 1, rows, PAIR), lambda s, j, m: (j, 0, s, 0, 0)),
                flat,
                flat,
            ],
        ),
        compiler_params=params("arbitrary", "arbitrary"),
        cost_estimate=cost(2**29, 5 * 2**20, 2**20),
    )(meta, queries, got, *keyed)


def tangent_body(
    meta, q_own, q_sib, qt_own, qt_sib, lo, ls, mo, ms, ro, rs, lt, mt, rt, out_own, out_sib
):
    mask = allowed_keys(meta)
    keyed, keyed_tan = (lo, ls, mo, ms, ro, rs), (lt, mt, rt)
    half = q_own.shape[1]
    for n in range(2):
        cols = slice(n * HD, (n + 1) * HD)
        q = jnp.concatenate([q_own[0, :, cols], q_sib[0, 0, :, cols]], axis=0)
        qt = jnp.concatenate([qt_own[0, :, cols], qt_sib[0, 0, :, cols]], axis=0)
        k = rows_of(keyed, 0, cols)
        probs = probs_of(q, k, mask)
        tan = (nt(qt, k) + nt(q, rows_of(keyed_tan, 0, cols))) * SCALE
        probs_tan = probs * (tan - jnp.sum(probs * tan, axis=-1, keepdims=True))
        att = nn(probs_tan.astype(BF), rows_of(keyed, 1, cols)) + nn(
            probs.astype(BF), rows_of(keyed_tan, 1, cols)
        )
        att = att.astype(BF)
        out_own[0, :, cols] = att[:half]
        out_sib[0, :, cols] = att[half:]


def attend_tangent(meta, queries, query_tan, got, keyed, keyed_tan, part):
    seqs, rows, _ = queries.shape
    first = part * (NJ // 2)
    own = pl.BlockSpec((1, rows, PAIR), lambda s, j, m: (s, 0, 2 * (first + j) + m[0]))
    pair = pl.BlockSpec((2, 1, rows, PAIR), lambda s, j, m: (0, s, 0, first + j))
    tall = pl.BlockSpec((2, 1, 2 * rows, PAIR), lambda s, j, m: (0, s, 0, j))
    flat = pl.BlockSpec((1, rows, PAIR), lambda s, j, m: (s, 0, j))
    wide = jax.ShapeDtypeStruct((seqs, rows, GROUP // 2), BF)
    return pl.pallas_call(
        tangent_body,
        out_shape=[wide, wide],
        grid_spec=pltpu.PrefetchScalarGridSpec(
            num_scalar_prefetch=1,
            grid=(seqs, NJ // 2),
            in_specs=[
                own,
                pl.BlockSpec((1, 1, rows, PAIR), lambda s, j, m: (0, s, 0, first + j)),
                own,
                pl.BlockSpec((1, 1, rows, PAIR), lambda s, j, m: (1, s, 0, first + j)),
            ]
            + [pair] * 6
            + [tall] * 3,
            out_specs=[flat, flat],
        ),
        compiler_params=params("arbitrary", "arbitrary"),
        cost_estimate=cost(2**29, 5 * 2**20, 2**20),
    )(meta, queries, got, query_tan, got, *keyed, *keyed_tan)


def gate_rows(ref, rows):
    return jnp.concatenate(
        [jnp.broadcast_to(ref[s : s + 1, :], (rows, ref.shape[1])) for s in range(2)], axis=0
    )


def flat2(ref):
    return ref[...].reshape(ref.shape[0] * ref.shape[1], ref.shape[2])


def project_body(att_o, att_s, tan_o, tan_s, w_o, w_s, gate, gate_tan, mixed, part):
    rows = att_o.shape[1]
    half = tan_o.shape[2]
    proj = nt(flat2(att_o), w_o[...]) + nt(flat2(att_s), w_s[...])
    proj_tan = nt(flat2(tan_o), w_o[:, :half]) + nt(flat2(tan_s), w_s[:, :half])
    g, gt = gate_rows(gate, rows), gate_rows(gate_tan, rows)
    mixed[...] = (g * proj).astype(BF).reshape(mixed.shape)
    part[...] = (gt * proj + g * proj_tan).reshape(part.shape)


def project(att_o, att_s, tan_o, tan_s, w_o, w_s, gate, gate_tan):
    seqs, rows, _ = att_o.shape
    width = gate.shape[1]
    step = 512
    weight = pl.BlockSpec((step, GROUP), lambda i: (i, 0))
    gates = pl.BlockSpec((2, step), lambda i: (0, i))
    block = pl.BlockSpec((seqs, rows, step), lambda i: (0, 0, i))
    return pl.pallas_call(
        project_body,
        grid=(width // step,),
        out_shape=[
            jax.ShapeDtypeStruct((seqs, rows, width), BF),
            jax.ShapeDtypeStruct((seqs, rows, width), F32),
        ],
        in_specs=[vmem_spec()] * 4 + [weight, weight, gates, gates],
        out_specs=[block, block],
        compiler_params=params("arbitrary"),
        cost_estimate=cost(2**30, 9 * 2**20),
    )(att_o, att_s, tan_o, tan_s, w_o, w_s, gate, gate_tan)


def finish_body(tan_o, tan_s, w_o, w_s, gate, part, mixed_tan):
    rows = tan_o.shape[1]
    proj_tan = nt(flat2(tan_o), w_o[...]) + nt(flat2(tan_s), w_s[...])
    total = part[...].reshape(proj_tan.shape) + gate_rows(gate, rows) * proj_tan
    mixed_tan[...] = total.astype(BF).reshape(mixed_tan.shape)


def finish(tan_o, tan_s, w_o, w_s, gate, part):
    seqs, rows, width = part.shape
    step = 512
    weight = pl.BlockSpec((step, GROUP // 2), lambda i: (i, 1))
    block = pl.BlockSpec((seqs, rows, step), lambda i: (0, 0, i))
    return pl.pallas_call(
        finish_body,
        grid=(width // step,),
        out_shape=jax.ShapeDtypeStruct((seqs, rows, width), BF),
        in_specs=[vmem_spec()] * 2
        + [weight, weight, pl.BlockSpec((2, step), lambda i: (0, i)), block],
        out_specs=block,
        compiler_params=params("arbitrary"),
        cost_estimate=cost(2**29, 5 * 2**20),
    )(tan_o, tan_s, w_o, w_s, gate, part)


def grad_body(meta, w_own, w_sib, a0, a1, a2, a3, out):
    place = meta[2]
    total = None
    for back, att in enumerate((a0, a1, a2, a3)):
        origin = lax.rem(place + (NX - back), NX)
        for side, weighted in enumerate((w_own, w_sib)):
            block = att[side].reshape(-1, PAIR)
            term = nn(weighted[origin], block)
            total = term if total is None else total + term
    total = total.astype(BF)
    piece = out.shape[2]
    for yl in range(NYL):
        for z in range(NZ):
            start = (yl * NZ + z) * piece
            out[z, yl] = total[start : start + piece]


def grad_terms(meta, w_own, w_sib, parts):
    width = w_own.shape[1]
    return pl.pallas_call(
        grad_body,
        out_shape=jax.ShapeDtypeStruct((NZ, NYL, width // (NZ * NYL), PAIR), BF),
        in_specs=[smem_spec()] + [vmem_spec()] * 6,
        out_specs=vmem_spec(),
        compiler_params=params(),
        cost_estimate=cost(2**30, 4 * 2**20),
    )(meta, w_own, w_sib, *parts)


def in_order(mine, other, bit, axis):
    return jnp.where(
        bit == 0,
        jnp.concatenate([mine, other], axis=axis),
        jnp.concatenate([other, mine], axis=axis),
    )


def on_device(
    queries, keys, values, query_tan, key_tan, value_tan, weight_out, gate, gate_tan, cotangent
):
    seq_at, uly_at = lax.axis_index("seq"), lax.axis_index("uly")
    core = uly_at % NC
    x_at, z_at, yl_at = seq_at % NX, (seq_at // NX) % NZ, seq_at // (NX * NZ)
    chunk = seq_at * NYH + uly_at // NC
    meta = jnp.stack([core, chunk, x_at]).astype(jnp.int32)
    seqs, rows, _ = queries.shape

    kv_sib_out, kv_own = split_groups(meta, (keys, values), True)
    kv_lo, kv_ro = send(kv_own, TO_NEXT), send(kv_own, TO_PREV)
    kv_sib = send(kv_sib_out, SWAP_CORE)
    kv_ls, kv_rs = send(kv_sib, TO_NEXT), send(kv_sib, TO_PREV)

    (rest_out,) = split_groups(meta, (queries, query_tan, key_tan, value_tan), False)
    rest = send(rest_out, SWAP_CORE)
    tan_a, tan_b = join_rows(meta, key_tan, value_tan, rest)
    tan_a_l, tan_a_r = send(tan_a, TO_NEXT), send(tan_a, TO_PREV)
    tan_b_l, tan_b_r = send(tan_b, TO_NEXT), send(tan_b, TO_PREV)

    weighted = (gate[:, None, :] * cotangent.astype(F32)).astype(BF)
    weighted = weighted.reshape(seqs * rows, -1).T
    w_own = lax.all_gather(weighted, AXES, axis_index_groups=GROUPS_X)
    w_sib = send(w_own, SWAP_CORE)

    low = weight_out.astype(BF).reshape(NJ, NC, PAIR, -1)
    low = lax.dynamic_index_in_dim(low, core, 1, keepdims=False).reshape(GROUP, -1).T
    low = low.reshape(1, 1, -1, GROUP)
    low = in_order(low, send(low, SWAP_YLO), yl_at, 0)
    for step in range(3):
        bit = 1 << step
        low = in_order(low, send(low, swap_z(bit)), (z_at // bit) % 2, 1)
    low = low.reshape(NYL * NZ, -1, GROUP)
    proj_own = lax.all_gather(low, AXES, axis_index_groups=GROUPS_X, axis=1, tiled=True)
    proj_own = proj_own.reshape(-1, GROUP)
    proj_sib = send(proj_own, SWAP_CORE)

    keyed = (kv_lo, kv_ls, kv_own, kv_sib, kv_ro, kv_rs)
    quarter, att_own, att_out = attend(meta, queries, rest, keyed)
    parts = [lax.dynamic_index_in_dim(quarter, x_at, 0, keepdims=False)]
    for by in range(1, NX):
        piece = lax.dynamic_index_in_dim(quarter, (x_at + by) % NX, 0, keepdims=False)
        parts.append(send(piece, shift_x(by)))
    att_sib = send(att_out, SWAP_CORE)

    terms = grad_terms(meta, w_own, w_sib, parts)
    terms = lax.all_to_all(terms, AXES, 0, 0, axis_index_groups=GROUPS_Z, tiled=True)
    terms = jnp.sum(terms.astype(F32), axis=0).reshape(NYL * NYH, -1, PAIR)
    terms = lax.all_to_all(terms, AXES, 0, 0, axis_index_groups=GROUPS_Y, tiled=True)
    weight_grad = send(jnp.sum(terms, axis=0), TURN).T

    tan_own_a, tan_out_a = attend_tangent(
        meta, queries, query_tan, rest, keyed, (tan_a_l, tan_a, tan_a_r), 0
    )
    tan_sib_a = send(tan_out_a, SWAP_CORE)
    mixed, part = project(
        att_own, att_sib, tan_own_a, tan_sib_a, proj_own, proj_sib, gate, gate_tan
    )
    tan_own_b, tan_out_b = attend_tangent(
        meta, queries, query_tan, rest, keyed, (tan_b_l, tan_b, tan_b_r), 1
    )
    tan_sib_b = send(tan_out_b, SWAP_CORE)
    mixed_tan = finish(tan_own_b, tan_sib_b, proj_own, proj_sib, gate, part)
    return mixed, mixed_tan, weight_grad


def solution(mesh):
    rows = P(None, ("seq", "uly"), None)
    return jax.shard_map(
        on_device,
        mesh=mesh,
        in_specs=(rows,) * 6 + (P(None, "seq"), P(), P(), rows),
        out_specs=(rows, rows, P("uly", "seq")),
        check_vma=False,
    )
```

time: 757 us -> 292 us (0.39)
  the two profiles are of different devices: /device:TPU:40 before, /device:TPU:30 now
where the time goes in v1:
time: 292 us; the launch traced here: 291 us
  starting transfers between devices  125 us (43%)
  waiting for transfers between devices  94.1 us (32%)
  Pallas kernels  40.8 us (14%)
  between operations  14.8 us (5%)
  local copies, waits for them, and re-layouts  10.6 us (4%)
  other arithmetic  5.1 us (2%)
    ppermute x23, starting transfers between devices, send(): return lax.ppermute(array, AXES, pairs)  89.9 us
    ppermute x23, waiting for transfers between devices, send(): return lax.ppermute(array, AXES, pairs)  70.6 us
    all_to_all x1, starting transfers between devices, on_device(): lax.all_to_all(terms, AXES, 0, 0, axis_index_groups=GROUPS_Y, tiled=True)  26.6 us
    all_gather x1, waiting for transfers between devices, on_device(): lax.all_gather(low, AXES, axis_index_groups=GROUPS_X, axis=1, tiled=True)  23.4 us
    pallas_call x2, Pallas kernels, attend_tangent(): pl.pallas_call(tangent_body, out_shape=[wide, wide], grid_spec=pltpu.Pref...  14.2 us
    pallas_call x1, Pallas kernels, attend(): pl.pallas_call(attend_body, out_shape=[jax.ShapeDtypeStruct((NJ, 2, seqs,...  9.4 us
    unnamed x38, local copies, waits for them, and re-layouts  9.3 us
    all_to_all x1, starting transfers between devices, on_device(): lax.all_to_all(terms, AXES, 0, 0, axis_index_groups=GROUPS_Z, tiled=True)  8.77 us
  transfers between devices with their start and end apart: 27, of which 10 were waited for; matrix products, arithmetic and copies ran while one was open for 2% of the time, Pallas kernels for 13%

profile of v1, /device:TPU:30, one launch (start us, length us, event | category | flops | bytes accessed | tf_op | source)
XLA Modules:
  0.0 290.7 jit_solution(14110978008212424837)
XLA Ops:
  7.2 0.0 all-gather.6.cloned.1.call-start
  7.2 1.1 multiply_convert_fusion
  8.3 0.9 copy.17
  9.3 0.0 all-gather.4.cloned.1.call-start
  9.4 0.3 dynamic-slice_reduce_fusion
  9.8 2.4 collective-permute-start.10
  12.1 3.6 %collective-permute-done.10 = bf16[1,1,24,1024]{3,2,1,0:T(8,128)(2,1)S(1)} collective-permute-done((bf16[1,1,24,1024]{3,2,1,0:T(8,128)(2,1)S(1)}, bf16[1,1,24,1024]{3,2,1,0:T(8,128)(2,1)S(1)}, u32[]{:S(2)}, u32[]{:S(2)}) %collective-permute-start.10) | collective-permute-done | bytes 49184 | tf_op jit(solution)/shard_map/ppermute | solution.py:69
  15.8 4.3 %collective-permute-start.11 = (bf16[2,1,24,1024]{3,2,1,0:T(8,128)(2,1)S(1)}, bf16[2,1,24,1024]{3,2,1,0:T(8,128)(2,1)S(1)}, u32[]{:S(2)}, u32[]{:S(2)}) collective-permute-start(bf16[2,1,24,1024]{3,2,1,0:T(8,128)(2,1)S(1)} %maximum_select_fusion.3), channel_id=1, source_target_pairs={{0,32},{1,33},{2,34},{3,35},{4,36},{5,37},{6,38},{7,39},{8,40},{9,... | collective-permute-start | bytes 294920 | tf_op jit(solution)/shard_map/ppermute | solution.py:69
  20.1 2.5 collective-permute-done.11
  22.7 6.1 %collective-permute-start.12 = (bf16[2,2,24,1024]{3,2,1,0:T(8,128)(2,1)S(1)}, bf16[2,2,24,1024]{3,2,1,0:T(8,128)(2,1)S(1)}, u32[]{:S(2)}, u32[]{:S(2)}) collective-permute-start(bf16[2,2,24,1024]{3,2,1,0:T(8,128)(2,1)S(1)} %maximum_select_fusion.2), channel_id=1, source_target_pairs={{0,64},{1,65},{2,66},{3,67},{4,68},{5,69},{6,70},{7,71},{8,72},{9,... | collective-permute-start | bytes 589832 | tf_op jit(solution)/shard_map/ppermute | solution.py:69
  28.8 7.0 %collective-permute-done.12 = bf16[2,2,24,1024]{3,2,1,0:T(8,128)(2,1)S(1)} collective-permute-done((bf16[2,2,24,1024]{3,2,1,0:T(8,128)(2,1)S(1)}, bf16[2,2,24,1024]{3,2,1,0:T(8,128)(2,1)S(1)}, u32[]{:S(2)}, u32[]{:S(2)}) %collective-permute-start.12) | collective-permute-done | bytes 196640 | tf_op jit(solution)/shard_map/ppermute | solution.py:69
  35.9 8.7 %collective-permute-start.13 = (bf16[2,4,24,1024]{3,2,1,0:T(8,128)(2,1)S(1)}, bf16[2,4,24,1024]{3,2,1,0:T(8,128)(2,1)S(1)}, u32[]{:S(2)}, u32[]{:S(2)}) collective-permute-start(bf16[2,4,24,1024]{3,2,1,0:T(8,128)(2,1)S(1)} %maximum_select_fusion.1), channel_id=1, source_target_pairs={{0,128},{1,129},{2,130},{3,131},{4,132},{5,133},{6,134},{7,135},{8... | collective-permute-start | bytes 1179656 | tf_op jit(solution)/shard_map/ppermute | solution.py:69
  44.7 16.5 %collective-permute-done.13 = bf16[2,4,24,1024]{3,2,1,0:T(8,128)(2,1)S(1)} collective-permute-done((bf16[2,4,24,1024]{3,2,1,0:T(8,128)(2,1)S(1)}, bf16[2,4,24,1024]{3,2,1,0:T(8,128)(2,1)S(1)}, u32[]{:S(2)}, u32[]{:S(2)}) %collective-permute-start.13) | collective-permute-done | bytes 393248 | tf_op jit(solution)/shard_map/ppermute | solution.py:69
  61.2 1.0 maximum_select_fusion
  62.2 0.1 pad_add_fusion.meta
  62.3 1.5 shard_map.122
  63.8 1.9 collective-permute-start.2
  65.7 0.0 all-gather.6.cloned.1.call-done
  65.8 2.4 collective-permute-start.18
  68.2 2.2 collective-permute-start.4
  70.4 5.7 %collective-permute-start.1 = (bf16[2,2,64,1024]{3,2,1,0:T(8,128)(2,1)S(1)}, bf16[2,2,64,1024]{3,2,1,0:T(8,128)(2,1)}, u32[]{:S(2)}, u32[]{:S(2)}) collective-permute-start(bf16[2,2,64,1024]{3,2,1,0:T(8,128)(2,1)S(1)} %get-tuple-element.16.mo), channel_id=1, source_target_pairs={{0,2},{1,3},{2,4},{3,5},{4,6},{5,7},{6,8},{7,9},{8,10},{9,11},{10,... | collective-permute-start | bytes 1572872 | tf_op jit(solution)/shard_map/ppermute | solution.py:69
  76.2 1.1 copy-done.7
  77.2 1.6 shard_map.121
  78.9 1.9 collective-permute-start
  80.8 23.4 %all-gather.4.cloned.1.call-done = bf16[16,96,1024]{2,1,0:T(8,128)(2,1)} async-done(((bf16[16,24,1024]{2,1,0:T(8,128)(2,1)}), bf16[16,96,1024]{2,1,0:T(8,128)(2,1)}) %all-gather.4.cloned.1.call-update) | async-done | bytes 3145744 | tf_op jit(solution)/shard_map/all_gather | solution.py:408
  104.2 1.9 collective-permute-start.14
  106.2 13.5 %collective-permute-start.5 = (bf16[2,2,64,1024]{3,2,1,0:T(8,128)(2,1)S(1)}, bf16[2,2,64,1024]{3,2,1,0:T(8,128)(2,1)}, u32[]{:S(2)}, u32[]{:S(2)}) collective-permute-start(bf16[2,2,64,1024]{3,2,1,0:T(8,128)(2,1)S(1)} %collective-permute-done.2.ms), channel_id=1, source_target_pairs={{2,0},{3,1},{4,2},{5,3},{6,4},{7,5},{8,6},{9,7},{10,8},{11,9},{12,... | collective-permute-start | bytes 1572872 | tf_op jit(solution)/shard_map/ppermute | solution.py:69
  119.7 1.9 collective-permute-start.3
  121.7 20.1 %collective-permute-done.5.rs = bf16[2,2,64,1024]{3,2,1,0:T(8,128)(2,1)} collective-permute-done((bf16[2,2,64,1024]{3,2,1,0:T(8,128)(2,1)S(1)}, bf16[2,2,64,1024]{3,2,1,0:T(8,128)(2,1)}, u32[]{:S(2)}, u32[]{:S(2)}) %collective-permute-start.5) | collective-permute-done | bytes 524320 | tf_op jit(solution)/shard_map/ppermute | solution.py:69
  141.8 6.1 %collective-permute-done.3.ls = bf16[2,2,64,1024]{3,2,1,0:T(8,128)(2,1)} collective-permute-done((bf16[2,2,64,1024]{3,2,1,0:T(8,128)(2,1)S(1)}, bf16[2,2,64,1024]{3,2,1,0:T(8,128)(2,1)}, u32[]{:S(2)}, u32[]{:S(2)}) %collective-permute-start.3) | collective-permute-done | bytes 524320 | tf_op jit(solution)/shard_map/ppermute | solution.py:69
  147.9 9.4 %shard_map.123 = (bf16[4,2,2,64,256]{4,3,2,1,0:T(8,128)(2,1)S(1)}, bf16[2,64,1024]{2,1,0:T(8,128)(2,1)S(1)}, bf16[2,64,1024]{2,1,0:T(8,128)(2,1)S(1)}) custom-call(s32[3]{0:T(128)S(1)} %pad_add_fusion.meta, bf16[2,64,2048]{2,1,0:T(8,128)(2,1)S(1)} %copy-done.1, bf16[4,2,64,1024]{3,2,1,0:T(8,128)(2,1)S(1)} %collective-permute-done.q_sib.got.qt_sib, ...), custom_call_target="tpu_custom_call" | custom-call | flops 536870912 | bytes 5242880 | tf_op jit(solution)/shard_map/pallas_call | solution.py:199
  157.3 0.1 dynamic-slice_bitcast_fusion
  157.4 1.9 collective-permute-start.21
  159.3 3.9 %collective-permute-start.20 = (bf16[2,2,64,256]{3,2,1,0:T(8,128)(2,1)S(1)}, bf16[2,2,64,256]{3,2,1,0:T(8,128)(2,1)S(1)}, u32[]{:S(2)}, u32[]{:S(2)}) collective-permute-start(bf16[2,2,64,256]{3,2,1,0:T(8,128)(2,1)S(1)} %get-tuple-element.30), channel_id=1, source_target_pairs={{0,16},{1,17},{2,18},{3,19},{4,20},{5,21},{6,22},{7,23},{8,24},{9,... | collective-permute-start | bytes 393224 | tf_op jit(solution)/shard_map/ppermute | solution.py:69
  163.2 3.2 %collective-permute-start.19 = (bf16[2,2,64,256]{3,2,1,0:T(8,128)(2,1)S(1)}, bf16[2,2,64,256]{3,2,1,0:T(8,128)(2,1)S(1)}, u32[]{:S(2)}, u32[]{:S(2)}) collective-permute-start(bf16[2,2,64,256]{3,2,1,0:T(8,128)(2,1)S(1)} %get-tuple-element.31), channel_id=1, source_target_pairs={{0,8},{1,9},{2,10},{3,11},{4,12},{5,13},{6,14},{7,15},{8,16},{9,17... | collective-permute-start | bytes 393224 | tf_op jit(solution)/shard_map/ppermute | solution.py:69
  166.4 1.9 collective-permute-done.21.a3
  168.3 2.8 collective-permute-done.19.a1
  171.1 3.2 %shard_map.129 = bf16[8,2,96,256]{3,2,1,0:T(8,128)(2,1)S(1)} custom-call(s32[3]{0:T(128)S(1)} %pad_add_fusion.meta, bf16[4,1536,128]{2,1,0:T(8,128)(2,1)S(1)} %bitcast.32, bf16[4,1536,128]{2,1,0:T(8,128)(2,1)} %collective-permute-done.18.w_sib, bf16[2,2,64,256]{3,2,1,0:T(8,128)(2,1)S(1)} %get-tuple-element.32.a0, ...), custom_call_target="tpu_custom_call" | custom-call | flops 1073741824 | bytes 4194304 | tf_op jit(solution)/shard_map/pallas_call | solution.py:356
  174.3 0.9 copy-done.4
  175.2 8.8 %all-to-all-start = ((bf16[8,2,96,256]{3,2,1,0:T(8,128)(2,1)}), bf16[8,2,96,256]{3,2,1,0:T(8,128)(2,1)}, u32[]{:S(2)}, u32[]{:S(2)}) async-start(bf16[8,2,96,256]{3,2,1,0:T(8,128)(2,1)} %copy-done.4), calls=%async_computation | async-start | bytes 1572864 | tf_op jit(solution)/shard_map/all_to_all | solution.py:421
  184.0 1.0 copy-done.6
  185.0 1.0 copy-done.8
  186.1 1.7 shard_map.124
  187.7 9.8 %collective-permute-start.8 = (bf16[2,2,128,512]{3,2,1,0:T(8,128)(2,1)}, bf16[2,2,128,512]{3,2,1,0:T(8,128)(2,1)}, u32[]{:S(2)}, u32[]{:S(2)}) collective-permute-start(bf16[2,2,128,512]{3,2,1,0:T(8,128)(2,1)} %get-tuple-element.20.mt), channel_id=1, source_target_pairs={{2,0},{3,1},{4,2},{5,3},{6,4},{7,5},{8,6},{9,7},{10,8},{11,9},{12,... | collective-permute-start | bytes 1572872 | tf_op jit(solution)/shard_map/ppermute | solution.py:69
  197.6 1.9 collective-permute-start.7
  199.5 4.8 %collective-permute-start.16 = (bf16[2,2,128,512]{3,2,1,0:T(8,128)(2,1)}, bf16[2,2,128,512]{3,2,1,0:T(8,128)(2,1)}, u32[]{:S(2)}, u32[]{:S(2)}) collective-permute-start(bf16[2,2,128,512]{3,2,1,0:T(8,128)(2,1)} %get-tuple-element.24.mt), channel_id=1, source_target_pairs={{2,0},{3,1},{4,2},{5,3},{6,4},{7,5},{8,6},{9,7},{10,8},{11,9},{12,... | collective-permute-start | bytes 1572872 | tf_op jit(solution)/shard_map/ppermute | solution.py:69
  204.3 3.1 %collective-permute-start.15 = (bf16[2,2,128,512]{3,2,1,0:T(8,128)(2,1)}, bf16[2,2,128,512]{3,2,1,0:T(8,128)(2,1)}, u32[]{:S(2)}, u32[]{:S(2)}) collective-permute-start(bf16[2,2,128,512]{3,2,1,0:T(8,128)(2,1)} %get-tuple-element.24.mt), channel_id=1, source_target_pairs={{0,2},{1,3},{2,4},{3,5},{4,6},{5,7},{6,8},{7,9},{8,10},{9,11},{10,... | collective-permute-start | bytes 1572872 | tf_op jit(solution)/shard_map/ppermute | solution.py:69
  207.5 1.9 convert_reduce_fusion
  209.4 26.6 %all-to-all-start.1 = ((f32[8,24,256]{2,1,0:T(8,128)}), f32[8,24,256]{2,1,0:T(8,128)}, u32[]{:S(2)}, u32[]{:S(2)}) async-start(f32[8,24,256]{2,1,0:T(8,128)} %bitcast.36), calls=%async_computation.1 | async-start | bytes 393216 | tf_op jit(solution)/shard_map/all_to_all | solution.py:423
  236.0 1.9 collective-permute-start.6
  237.9 1.0 copy-done.3
  239.0 7.1 %shard_map.125 = (bf16[2,64,512]{2,1,0:T(8,128)(2,1)S(1)}, bf16[2,64,512]{2,1,0:T(8,128)(2,1)}) custom-call(s32[3]{0:T(128)S(1)} %pad_add_fusion.meta, bf16[2,64,2048]{2,1,0:T(8,128)(2,1)S(1)} %copy-done.1, bf16[4,2,64,1024]{3,2,1,0:T(8,128)(2,1)S(1)} %collective-permute-done.q_sib.got.qt_sib, bf16[2,64,2048]{2,1,0:T(8,128)(2,1)S(1)} %copy-done.3, ...), custom_call_target="tpu_custom_call" | custom-call | flops 536870912 | bytes 5242880 | tf_op jit(solution)/shard_map/pallas_call | solution.py:251
  246.1 2.4 collective-permute-start.9
  248.5 7.1 %shard_map.127 = (bf16[2,64,512]{2,1,0:T(8,128)(2,1)S(1)}, bf16[2,64,512]{2,1,0:T(8,128)(2,1)}) custom-call(s32[3]{0:T(128)S(1)} %pad_add_fusion.meta, bf16[2,64,2048]{2,1,0:T(8,128)(2,1)S(1)} %copy-done.1, bf16[4,2,64,1024]{3,2,1,0:T(8,128)(2,1)S(1)} %collective-permute-done.q_sib.got.qt_sib, bf16[2,64,2048]{2,1,0:T(8,128)(2,1)S(1)} %copy-done.3, ...), custom_call_target="tpu_custom_call" | custom-call | flops 536870912 | bytes 5242880 | tf_op jit(solution)/shard_map/pallas_call | solution.py:251
  255.7 1.9 collective-permute-start.17
  257.6 0.9 reduce_sum.19
  258.5 2.0 collective-permute-start.22
  260.5 10.0 %collective-permute-done.22 = f32[24,256]{1,0:T(8,128)S(1)} collective-permute-done((f32[24,256]{1,0:T(8,128)S(1)}, f32[24,256]{1,0:T(8,128)S(1)}, u32[]{:S(2)}, u32[]{:S(2)}) %collective-permute-start.22) | collective-permute-done | bytes 24608 | tf_op jit(solution)/shard_map/ppermute | solution.py:69
  270.6 1.9 copy-done
  272.5 0.9 copy-done.13
  273.4 0.7 copy-done.15
  274.1 5.4 %shard_map.126 = (bf16[2,64,1536]{2,1,0:T(8,128)(2,1)}, f32[2,64,1536]{2,1,0:T(8,128)S(1)}) custom-call(bf16[2,64,1024]{2,1,0:T(8,128)(2,1)S(1)} %get-tuple-element.18.att_o, bf16[2,64,1024]{2,1,0:T(8,128)(2,1)} %collective-permute-done.6.att_s, bf16[2,64,512]{2,1,0:T(8,128)(2,1)S(1)} %copy-done.13, bf16[2,64,512]{2,1,0:T(8,128)(2,1)} %collective-permute-done.9.tan_s, ...), custom_call_target="tpu_custom_call" | custom-call | flops 1073741824 | bytes 9437184 | tf_op jit(solution)/shard_map/pallas_call | solution.py:299
  279.5 3.8 %shard_map.128 = bf16[2,64,1536]{2,1,0:T(8,128)(2,1)} custom-call(bf16[2,64,512]{2,1,0:T(8,128)(2,1)S(1)} %get-tuple-element.25.tan_o, bf16[2,64,512]{2,1,0:T(8,128)(2,1)S(1)} %collective-permute-done.17.tan_s, bf16[1536,1024]{1,0:T(8,128)(2,1)S(1)} %bitcast.30, bf16[1536,1024]{1,0:T(8,128)(2,1)} %collective-permute-done.14.w_s, f32[2,1536]{1,0:T(2,128)S(1)} %copy-done.14, ...), custom_call_target="tpu_custom_call" | custom-call | flops 536870912 | bytes 5242880 | tf_op jit(solution)/shard_map/pallas_call | solution.py:325
  283.3 0.6 copy.21
  (52 shorter events, 0.3 us)
Async XLA Ops:
  7.2 2.2 copy-start.17
  7.2 58.6 %all-gather.6.cloned.1.call-start = ((), (), s32[]{:S(2)}) async-start(), calls=%async_computation.3 | async-start | bytes 1966080 | tf_op jit(solution)/shard_map/all_gather | solution.py:397
  9.3 95.0 %all-gather.4.cloned.1.call-start = ((), (), s32[]{:S(2)}) async-start(), calls=%async_computation.2 | async-start | bytes 3932160 | tf_op jit(solution)/shard_map/all_gather | solution.py:408
  9.8 6.0 %collective-permute-start.10 = (bf16[1,1,24,1024]{3,2,1,0:T(8,128)(2,1)S(1)}, bf16[1,1,24,1024]{3,2,1,0:T(8,128)(2,1)S(1)}, u32[]{:S(2)}, u32[]{:S(2)}) collective-permute-start(bf16[1,1,24,1024]{3,2,1,0:T(8,128)(2,1)S(1)} %bitcast.37), channel_id=1, source_target_pairs={{0,256},{1,257},{2,258},{3,259},{4,260},{5,261},{6,262},{7,263},{8... | collective-permute-start | bytes 147464 | tf_op jit(solution)/shard_map/ppermute | solution.py:69
  15.8 6.9 %collective-permute-start.11 = (bf16[2,1,24,1024]{3,2,1,0:T(8,128)(2,1)S(1)}, bf16[2,1,24,1024]{3,2,1,0:T(8,128)(2,1)S(1)}, u32[]{:S(2)}, u32[]{:S(2)}) collective-permute-start(bf16[2,1,24,1024]{3,2,1,0:T(8,128)(2,1)S(1)} %maximum_select_fusion.3), channel_id=1, source_target_pairs={{0,32},{1,33},{2,34},{3,35},{4,36},{5,37},{6,38},{7,39},{8,40},{9,... | collective-permute-start | bytes 294920 | tf_op jit(solution)/shard_map/ppermute | solution.py:69
  22.7 13.2 %collective-permute-start.12 = (bf16[2,2,24,1024]{3,2,1,0:T(8,128)(2,1)S(1)}, bf16[2,2,24,1024]{3,2,1,0:T(8,128)(2,1)S(1)}, u32[]{:S(2)}, u32[]{:S(2)}) collective-permute-start(bf16[2,2,24,1024]{3,2,1,0:T(8,128)(2,1)S(1)} %maximum_select_fusion.2), channel_id=1, source_target_pairs={{0,64},{1,65},{2,66},{3,67},{4,68},{5,69},{6,70},{7,71},{8,72},{9,... | collective-permute-start | bytes 589832 | tf_op jit(solution)/shard_map/ppermute | solution.py:69
  28.8 33.5 %copy-start.10 = (bf16[2,64,2048]{2,1,0:T(8,128)(2,1)S(1)}, bf16[2,64,2048]{2,1,0:T(8,128)(2,1)}, u32[]{:S(2)}) copy-start(bf16[2,64,2048]{2,1,0:T(8,128)(2,1)} %refs_0_.3) | copy-start | bytes 1572868
  28.8 33.5 %copy-start.11 = (bf16[2,64,2048]{2,1,0:T(8,128)(2,1)S(1)}, bf16[2,64,2048]{2,1,0:T(8,128)(2,1)}, u32[]{:S(2)}) copy-start(bf16[2,64,2048]{2,1,0:T(8,128)(2,1)} %refs_1_.3) | copy-start | bytes 1572868
  35.9 25.3 %collective-permute-start.13 = (bf16[2,4,24,1024]{3,2,1,0:T(8,128)(2,1)S(1)}, bf16[2,4,24,1024]{3,2,1,0:T(8,128)(2,1)S(1)}, u32[]{:S(2)}, u32[]{:S(2)}) collective-permute-start(bf16[2,4,24,1024]{3,2,1,0:T(8,128)(2,1)S(1)} %maximum_select_fusion.1), channel_id=1, source_target_pairs={{0,128},{1,129},{2,130},{3,131},{4,132},{5,133},{6,134},{7,135},{8... | collective-permute-start | bytes 1179656 | tf_op jit(solution)/shard_map/ppermute | solution.py:69
  44.6 31.5 %copy-start.1 = (bf16[2,64,2048]{2,1,0:T(8,128)(2,1)S(1)}, bf16[2,64,2048]{2,1,0:T(8,128)(2,1)}, u32[]{:S(2)}) copy-start(bf16[2,64,2048]{2,1,0:T(8,128)(2,1)} %q_own.5) | copy-start | bytes 1572868
  44.7 31.5 %copy-start.2 = (bf16[2,64,2048]{2,1,0:T(8,128)(2,1)S(1)}, bf16[2,64,2048]{2,1,0:T(8,128)(2,1)}, u32[]{:S(2)}) copy-start(bf16[2,64,2048]{2,1,0:T(8,128)(2,1)} %qt_own.3) | copy-start | bytes 1572868
  44.7 31.5 %copy-start.5 = (bf16[2,64,2048]{2,1,0:T(8,128)(2,1)S(1)}, bf16[2,64,2048]{2,1,0:T(8,128)(2,1)}, u32[]{:S(2)}) copy-start(bf16[2,64,2048]{2,1,0:T(8,128)(2,1)} %kt.1) | copy-start | bytes 1572868
  63.8 17.0 %collective-permute-start.2 = (bf16[2,2,64,1024]{3,2,1,0:T(8,128)(2,1)}, bf16[2,2,64,1024]{3,2,1,0:T(8,128)(2,1)S(1)}, u32[]{:S(2)}, u32[]{:S(2)}) collective-permute-start(bf16[2,2,64,1024]{3,2,1,0:T(8,128)(2,1)} %get-tuple-element.17), channel_id=1, source_target_pairs={{0,1},{1,0},{2,3},{3,2},{4,5},{5,4},{6,7},{7,6},{8,9},{9,8},{10,11... | collective-permute-start | bytes 1572872 | tf_op jit(solution)/shard_map/ppermute | solution.py:69
  65.8 105.3 %collective-permute-start.18 = (bf16[4,1536,128]{2,1,0:T(8,128)(2,1)}, bf16[4,1536,128]{2,1,0:T(8,128)(2,1)}, u32[]{:S(2)}, u32[]{:S(2)}) collective-permute-start(bf16[4,1536,128]{2,1,0:T(8,128)(2,1)} %bitcast.31), channel_id=1, source_target_pairs={{0,1},{1,0},{2,3},{3,2},{4,5},{5,4},{6,7},{7,6},{8,9},{9,8},{10,11... | collective-permute-start | bytes 4718600 | tf_op jit(solution)/shard_map/ppermute | solution.py:69
  68.2 38.0 %collective-permute-start.4 = (bf16[2,2,64,1024]{3,2,1,0:T(8,128)(2,1)S(1)}, bf16[2,2,64,1024]{3,2,1,0:T(8,128)(2,1)S(1)}, u32[]{:S(2)}, u32[]{:S(2)}) collective-permute-start(bf16[2,2,64,1024]{3,2,1,0:T(8,128)(2,1)S(1)} %get-tuple-element.16.mo), channel_id=1, source_target_pairs={{2,0},{3,1},{4,2},{5,3},{6,4},{7,5},{8,6},{9,7},{10,8},{11,9},{12,... | collective-permute-start | bytes 1572872 | tf_op jit(solution)/shard_map/ppermute | solution.py:69
  70.4 49.3 %collective-permute-start.1 = (bf16[2,2,64,1024]{3,2,1,0:T(8,128)(2,1)S(1)}, bf16[2,2,64,1024]{3,2,1,0:T(8,128)(2,1)}, u32[]{:S(2)}, u32[]{:S(2)}) collective-permute-start(bf16[2,2,64,1024]{3,2,1,0:T(8,128)(2,1)S(1)} %get-tuple-element.16.mo), channel_id=1, source_target_pairs={{0,2},{1,3},{2,4},{3,5},{4,6},{5,7},{6,8},{7,9},{8,10},{9,11},{10,... | collective-permute-start | bytes 1572872 | tf_op jit(solution)/shard_map/ppermute | solution.py:69
  76.2 1.1 copy-start.7
  78.9 69.0 %collective-permute-start = (bf16[4,2,64,1024]{3,2,1,0:T(8,128)(2,1)}, bf16[4,2,64,1024]{3,2,1,0:T(8,128)(2,1)S(1)}, u32[]{:S(2)}, u32[]{:S(2)}) collective-permute-start(bf16[4,2,64,1024]{3,2,1,0:T(8,128)(2,1)} %shard_map.121), channel_id=1, source_target_pairs={{0,1},{1,0},{2,3},{3,2},{4,5},{5,4},{6,7},{7,6},{8,9},{9,8},{10,11... | collective-permute-start | bytes 3145736 | tf_op jit(solution)/shard_map/ppermute | solution.py:69
  104.2 166.3 %collective-permute-start.14 = (bf16[1536,1024]{1,0:T(8,128)(2,1)}, bf16[1536,1024]{1,0:T(8,128)(2,1)}, u32[]{:S(2)}, u32[]{:S(2)}) collective-permute-start(bf16[1536,1024]{1,0:T(8,128)(2,1)} %bitcast.28), channel_id=1, source_target_pairs={{0,1},{1,0},{2,3},{3,2},{4,5},{5,4},{6,7},{7,6},{8,9},{9,8},{10,11... | collective-permute-start | bytes 9437192 | tf_op jit(solution)/shard_map/ppermute | solution.py:69
  106.2 35.7 %collective-permute-start.5 = (bf16[2,2,64,1024]{3,2,1,0:T(8,128)(2,1)S(1)}, bf16[2,2,64,1024]{3,2,1,0:T(8,128)(2,1)}, u32[]{:S(2)}, u32[]{:S(2)}) collective-permute-start(bf16[2,2,64,1024]{3,2,1,0:T(8,128)(2,1)S(1)} %collective-permute-done.2.ms), channel_id=1, source_target_pairs={{2,0},{3,1},{4,2},{5,3},{6,4},{7,5},{8,6},{9,7},{10,8},{11,9},{12,... | collective-permute-start | bytes 1572872 | tf_op jit(solution)/shard_map/ppermute | solution.py:69
  119.7 28.2 %collective-permute-start.3 = (bf16[2,2,64,1024]{3,2,1,0:T(8,128)(2,1)S(1)}, bf16[2,2,64,1024]{3,2,1,0:T(8,128)(2,1)}, u32[]{:S(2)}, u32[]{:S(2)}) collective-permute-start(bf16[2,2,64,1024]{3,2,1,0:T(8,128)(2,1)S(1)} %collective-permute-done.2.ms), channel_id=1, source_target_pairs={{0,2},{1,3},{2,4},{3,5},{4,6},{5,7},{6,8},{7,9},{8,10},{9,11},{10,... | collective-permute-start | bytes 1572872 | tf_op jit(solution)/shard_map/ppermute | solution.py:69
  121.7 49.4 %copy-start.9 = (bf16[6144,128]{1,0:T(8,128)(2,1)S(1)}, bf16[6144,128]{1,0:T(8,128)(2,1)}, u32[]{:S(2)}) copy-start(bf16[6144,128]{1,0:T(8,128)(2,1)} %all-gather.6.cloned.1.call-done) | copy-start | bytes 4718596
  157.3 13.7 %copy-start.16 = (bf16[2,64,1024]{2,1,0:T(8,128)(2,1)}, bf16[2,64,1024]{2,1,0:T(8,128)(2,1)S(1)}, u32[]{:S(2)}) copy-start(bf16[2,64,1024]{2,1,0:T(8,128)(2,1)S(1)} %get-tuple-element.19) | copy-start | bytes 786436
  157.4 10.9 %collective-permute-start.21 = (bf16[2,2,64,256]{3,2,1,0:T(8,128)(2,1)S(1)}, bf16[2,2,64,256]{3,2,1,0:T(8,128)(2,1)S(1)}, u32[]{:S(2)}, u32[]{:S(2)}) collective-permute-start(bf16[2,2,64,256]{3,2,1,0:T(8,128)(2,1)S(1)} %get-tuple-element.29), channel_id=1, source_target_pairs={{0,24},{1,25},{2,26},{3,27},{4,28},{5,29},{6,30},{7,31},{8,0},{9,1... | collective-permute-start | bytes 393224 | tf_op jit(solution)/shard_map/ppermute | solution.py:69
  159.3 9.0 %collective-permute-start.20 = (bf16[2,2,64,256]{3,2,1,0:T(8,128)(2,1)S(1)}, bf16[2,2,64,256]{3,2,1,0:T(8,128)(2,1)S(1)}, u32[]{:S(2)}, u32[]{:S(2)}) collective-permute-start(bf16[2,2,64,256]{3,2,1,0:T(8,128)(2,1)S(1)} %get-tuple-element.30), channel_id=1, source_target_pairs={{0,16},{1,17},{2,18},{3,19},{4,20},{5,21},{6,22},{7,23},{8,24},{9,... | collective-permute-start | bytes 393224 | tf_op jit(solution)/shard_map/ppermute | solution.py:69
  163.2 7.8 %collective-permute-start.19 = (bf16[2,2,64,256]{3,2,1,0:T(8,128)(2,1)S(1)}, bf16[2,2,64,256]{3,2,1,0:T(8,128)(2,1)S(1)}, u32[]{:S(2)}, u32[]{:S(2)}) collective-permute-start(bf16[2,2,64,256]{3,2,1,0:T(8,128)(2,1)S(1)} %get-tuple-element.31), channel_id=1, source_target_pairs={{0,8},{1,9},{2,10},{3,11},{4,12},{5,13},{6,14},{7,15},{8,16},{9,17... | collective-permute-start | bytes 393224 | tf_op jit(solution)/shard_map/ppermute | solution.py:69
  174.3 1.0 copy-start.4
  175.2 32.2 %all-to-all-start = ((bf16[8,2,96,256]{3,2,1,0:T(8,128)(2,1)}), bf16[8,2,96,256]{3,2,1,0:T(8,128)(2,1)}, u32[]{:S(2)}, u32[]{:S(2)}) async-start(bf16[8,2,96,256]{3,2,1,0:T(8,128)(2,1)} %copy-done.4), calls=%async_computation | async-start | bytes 1572864 | tf_op jit(solution)/shard_map/all_to_all | solution.py:421
  184.0 1.0 copy-start.6
  185.0 1.0 copy-start.8
  187.7 48.3 %collective-permute-start.8 = (bf16[2,2,128,512]{3,2,1,0:T(8,128)(2,1)}, bf16[2,2,128,512]{3,2,1,0:T(8,128)(2,1)}, u32[]{:S(2)}, u32[]{:S(2)}) collective-permute-start(bf16[2,2,128,512]{3,2,1,0:T(8,128)(2,1)} %get-tuple-element.20.mt), channel_id=1, source_target_pairs={{2,0},{3,1},{4,2},{5,3},{6,4},{7,5},{8,6},{9,7},{10,8},{11,9},{12,... | collective-permute-start | bytes 1572872 | tf_op jit(solution)/shard_map/ppermute | solution.py:69
  197.6 40.3 %collective-permute-start.7 = (bf16[2,2,128,512]{3,2,1,0:T(8,128)(2,1)}, bf16[2,2,128,512]{3,2,1,0:T(8,128)(2,1)}, u32[]{:S(2)}, u32[]{:S(2)}) collective-permute-start(bf16[2,2,128,512]{3,2,1,0:T(8,128)(2,1)} %get-tuple-element.20.mt), channel_id=1, source_target_pairs={{0,2},{1,3},{2,4},{3,5},{4,6},{5,7},{6,8},{7,9},{8,10},{9,11},{10,... | collective-permute-start | bytes 1572872 | tf_op jit(solution)/shard_map/ppermute | solution.py:69
  199.5 49.0 %collective-permute-start.16 = (bf16[2,2,128,512]{3,2,1,0:T(8,128)(2,1)}, bf16[2,2,128,512]{3,2,1,0:T(8,128)(2,1)}, u32[]{:S(2)}, u32[]{:S(2)}) collective-permute-start(bf16[2,2,128,512]{3,2,1,0:T(8,128)(2,1)} %get-tuple-element.24.mt), channel_id=1, source_target_pairs={{2,0},{3,1},{4,2},{5,3},{6,4},{7,5},{8,6},{9,7},{10,8},{11,9},{12,... | collective-permute-start | bytes 1572872 | tf_op jit(solution)/shard_map/ppermute | solution.py:69
  204.3 44.2 %collective-permute-start.15 = (bf16[2,2,128,512]{3,2,1,0:T(8,128)(2,1)}, bf16[2,2,128,512]{3,2,1,0:T(8,128)(2,1)}, u32[]{:S(2)}, u32[]{:S(2)}) collective-permute-start(bf16[2,2,128,512]{3,2,1,0:T(8,128)(2,1)} %get-tuple-element.24.mt), channel_id=1, source_target_pairs={{0,2},{1,3},{2,4},{3,5},{4,6},{5,7},{6,8},{7,9},{8,10},{9,11},{10,... | collective-permute-start | bytes 1572872 | tf_op jit(solution)/shard_map/ppermute | solution.py:69
  209.4 48.2 %all-to-all-start.1 = ((f32[8,24,256]{2,1,0:T(8,128)}), f32[8,24,256]{2,1,0:T(8,128)}, u32[]{:S(2)}, u32[]{:S(2)}) async-start(f32[8,24,256]{2,1,0:T(8,128)} %bitcast.36), calls=%async_computation.1 | async-start | bytes 393216 | tf_op jit(solution)/shard_map/all_to_all | solution.py:423
  236.0 34.6 %collective-permute-start.6 = (bf16[2,64,1024]{2,1,0:T(8,128)(2,1)}, bf16[2,64,1024]{2,1,0:T(8,128)(2,1)}, u32[]{:S(2)}, u32[]{:S(2)}) collective-permute-start(bf16[2,64,1024]{2,1,0:T(8,128)(2,1)} %copy-done.16), channel_id=1, source_target_pairs={{0,1},{1,0},{2,3},{3,2},{4,5},{5,4},{6,7},{7,6},{8,9},{9,8},{10,11... | collective-permute-start | bytes 786440 | tf_op jit(solution)/shard_map/ppermute | solution.py:69
  237.9 1.0 copy-start.3
  246.1 9.6 %copy-start.12 = (bf16[2,64,512]{2,1,0:T(8,128)(2,1)}, bf16[2,64,512]{2,1,0:T(8,128)(2,1)S(1)}, u32[]{:S(2)}) copy-start(bf16[2,64,512]{2,1,0:T(8,128)(2,1)S(1)} %get-tuple-element.21.tan_o) | copy-start | bytes 393220
  246.1 24.5 %copy-start.14 = (f32[2,1536]{1,0:T(2,128)S(1)}, f32[2,1536]{1,0:T(2,128)}, u32[]{:S(2)}) copy-start(f32[2,1536]{1,0:T(2,128)} %gate.3) | copy-start | bytes 36868
  246.1 24.5 %collective-permute-start.9 = (bf16[2,64,512]{2,1,0:T(8,128)(2,1)}, bf16[2,64,512]{2,1,0:T(8,128)(2,1)}, u32[]{:S(2)}, u32[]{:S(2)}) collective-permute-start(bf16[2,64,512]{2,1,0:T(8,128)(2,1)} %get-tuple-element.22), channel_id=1, source_target_pairs={{0,1},{1,0},{2,3},{3,2},{4,5},{5,4},{6,7},{7,6},{8,9},{9,8},{10,11... | collective-permute-start | bytes 393224 | tf_op jit(solution)/shard_map/ppermute | solution.py:69
  255.7 23.8 %collective-permute-start.17 = (bf16[2,64,512]{2,1,0:T(8,128)(2,1)}, bf16[2,64,512]{2,1,0:T(8,128)(2,1)S(1)}, u32[]{:S(2)}, u32[]{:S(2)}) collective-permute-start(bf16[2,64,512]{2,1,0:T(8,128)(2,1)} %get-tuple-element.26), channel_id=1, source_target_pairs={{0,1},{1,0},{2,3},{3,2},{4,5},{5,4},{6,7},{7,6},{8,9},{9,8},{10,11... | collective-permute-start | bytes 393224 | tf_op jit(solution)/shard_map/ppermute | solution.py:69
  258.5 12.0 %collective-permute-start.22 = (f32[24,256]{1,0:T(8,128)S(1)}, f32[24,256]{1,0:T(8,128)S(1)}, u32[]{:S(2)}, u32[]{:S(2)}) collective-permute-start(f32[24,256]{1,0:T(8,128)S(1)} %reduce_sum.19), channel_id=1, source_target_pairs={{0,0},{1,1},{2,8},{3,9},{4,16},{5,17},{6,24},{7,25},{8,2},{9,3},{1... | collective-permute-start | bytes 73736 | tf_op jit(solution)/shard_map/ppermute | solution.py:69
  270.6 1.9 copy-start
  272.5 0.9 copy-start.13
  273.4 0.7 copy-start.15
Sparse Core Ops, SparseCore 0:
  10.7 35.0 all-gather.5
  62.3 41.8 all-gather.3

commit v2 on v1

v2 whole, which is shorter than its diff:
```python
import functools

import jax
import jax.numpy as jnp
from jax import lax
from jax.experimental import pallas as pl
from jax.experimental.pallas import tpu as pltpu
from jax.sharding import PartitionSpec as P

AXES = ("seq", "uly")
NX, NZ, NYL, NYH, NC = 4, 8, 2, 4, 2
HD = 128
PAIR = 2 * HD
NJ = 4
GROUP = NJ * PAIR
PIECES = ((0, 2), (2, 4))
SCALE = HD ** (-0.5)
BF = jnp.bfloat16
F32 = jnp.float32


def device_of(x, yl, yh, z, c):
    return ((yl * NZ + z) * NX + x) * (NYH * NC) + yh * NC + c


def all_places():
    for x in range(NX):
        for yl in range(NYL):
            for yh in range(NYH):
                for z in range(NZ):
                    for c in range(NC):
                        yield x, yl, yh, z, c


def moves(rule):
    return sorted((device_of(*p), device_of(*rule(*p))) for p in all_places())


SWAP_CORE = moves(lambda x, yl, yh, z, c: (x, yl, yh, z, 1 - c))
SWAP_YLO = moves(lambda x, yl, yh, z, c: (x, 1 - yl, yh, z, c))
TURN = moves(lambda x, yl, yh, z, c: (yh, yl, x, z, c))


def swap_z(bit):
    return moves(lambda x, yl, yh, z, c: (x, yl, yh, z ^ bit, c))


def shift_x(by):
    return moves(lambda x, yl, yh, z, c: ((x + by) % NX, yl, yh, z, c))


COUNT = NX * NYL * NYH * NZ * NC
TO_NEXT = [(d, d + NC) for d in range(COUNT - NC)]
TO_PREV = [(d + NC, d) for d in range(COUNT - NC)]
GROUPS_X = [
    [device_of(x, yl, yh, z, c) for x in range(NX)]
    for yl in range(NYL) for yh in range(NYH) for z in range(NZ) for c in range(NC)
]
GROUPS_Z = [
    [device_of(x, yl, yh, z, c) for z in range(NZ)]
    for yl in range(NYL) for yh in range(NYH) for x in range(NX) for c in range(NC)
]
GROUPS_ZYL = [
    [device_of(x, yl, yh, z, c) for yl in range(NYL) for z in range(NZ)]
    for yh in range(NYH) for x in range(NX) for c in range(NC)
]
GROUPS_Y = [
    [device_of(x, yl, yh, z, c) for yl in range(NYL) for yh in range(NYH)]
    for z in range(NZ) for x in range(NX) for c in range(NC)
]


def send(array, pairs, tag):
    with jax.named_scope(tag):
        return lax.ppermute(array, AXES, pairs)


def after(values):
    return lax.optimization_barrier(values)


def nt(left, right):
    return lax.dot_general(left, right, (((1,), (1,)), ((), ())), preferred_element_type=F32)


def nn(left, right):
    return lax.dot_general(left, right, (((1,), (0,)), ((), ())), preferred_element_type=F32)


def vmem_spec():
    return pl.BlockSpec(memory_space=pltpu.VMEM)


def smem_spec():
    return pl.BlockSpec(memory_space=pltpu.SMEM)


def params(*semantics):
    return pltpu.CompilerParams(
        vmem_limit_bytes=50 * 2**20, dimension_semantics=semantics or None
    )


def cost(flops, nbytes, trans=0):
    return pl.CostEstimate(flops=flops, bytes_accessed=nbytes, transcendentals=trans)


COSTS = dict(
    split=cost(1, 1),
    join=cost(1, 1),
    attend=cost(2**35, 1),
    tangent=cost(2**33, 1),
    project=cost(1, 1),
    finish=cost(1, 1),
    grad=cost(1, 1),
)


def group_cols(ref, s, j, side):
    return ref[s, :, pl.ds(pl.multiple_of(j * 2 * PAIR + side * PAIR, PAIR), PAIR)]


def split_body(meta, *refs):
    core = meta[0]
    ins, out = refs[:-1], refs[-1]
    for a, ref in enumerate(ins):
        for s in range(2):
            for j in range(NJ):
                out[a, s, :, j * PAIR : (j + 1) * PAIR] = group_cols(ref, s, j, 1 - core)


def split_groups(meta, arrays):
    count = len(arrays)
    seqs, rows, _ = arrays[0].shape
    return pl.pallas_call(
        split_body,
        out_shape=jax.ShapeDtypeStruct((count, seqs, rows, GROUP), BF),
        in_specs=[smem_spec()] + [vmem_spec()] * count,
        out_specs=vmem_spec(),
        compiler_params=params(),
        cost_estimate=COSTS["split"],
    )(meta, *arrays)


def join_body(meta, *refs, pieces, first):
    core = meta[0]
    count = len(refs) - 1 - len(pieces)
    ins, got, outs = refs[:count], refs[count], refs[count + 1 :]
    rows = ins[0].shape[1]
    for out, (sources, (start, stop)) in zip(outs, pieces):
        for n, a in enumerate(sources):
            for s in range(2):
                for j in range(start, stop):
                    cols = slice((j - start) * PAIR, (j - start + 1) * PAIR)
                    out[n, s, :rows, cols] = group_cols(ins[a], s, j, core)
                    out[n, s, rows:, cols] = got[first + a, s, :, j * PAIR : (j + 1) * PAIR]


def join_rows(meta, arrays, got, pieces, first):
    seqs, rows, _ = arrays[0].shape
    count = len(arrays)
    part = pl.BlockSpec((6, seqs, rows, GROUP), lambda: (0, 0, 0, 0))
    return pl.pallas_call(
        functools.partial(join_body, pieces=pieces, first=first),
        out_shape=[
            jax.ShapeDtypeStruct((len(src), seqs, 2 * rows, (stop - start) * PAIR), BF)
            for src, (start, stop) in pieces
        ],
        in_specs=[smem_spec()] + [vmem_spec()] * count + [part],
        out_specs=[vmem_spec()] * len(pieces),
        compiler_params=params(),
        cost_estimate=COSTS["join"],
    )(meta, *arrays, got)


def allowed_keys(meta):
    core, chunk = meta[0], meta[1]
    span = 2 * 64
    shape = (span, 3 * span)
    rows = lax.broadcasted_iota(jnp.int32, shape, 0)
    cols = lax.broadcasted_iota(jnp.int32, shape, 1)
    q_pos = (rows + 64 * core) & (span - 1)
    k_pos = (cols + 64 * core) & (span - 1)
    block = cols >> 7
    before = (block == 0) & (k_pos >= q_pos) & (chunk > 0)
    after = (block == 2) & (k_pos <= q_pos) & (chunk < COUNT // NC - 1)
    return before | (block == 1) | after


def probs_of(q, k, mask):
    scores = jnp.where(mask, nt(q, k) * SCALE, -1e30)
    top = jnp.max(scores, axis=-1, keepdims=True)
    terms = jnp.exp(scores - top)
    return terms / jnp.sum(terms, axis=-1, keepdims=True)


def rows_of(refs, a, cols):
    return jnp.concatenate([ref[a, 0, :, cols] for ref in refs], axis=0)


def attend_body(meta, q_ref, left, mid, right, quarter, wide):
    mask = allowed_keys(meta)
    keyed = (left, mid, right)
    for n in range(GROUP // HD):
        cols = slice(n * HD, (n + 1) * HD)
        probs = probs_of(q_ref[0, 0, :, cols], rows_of(keyed, 0, cols), mask).astype(BF)
        att = nn(probs, rows_of(keyed, 1, cols)).astype(BF)
        quarter[n // 2, 0, :, (n % 2) * HD : (n % 2 + 1) * HD] = att
        wide[0, :, cols] = att


def attend(meta, q_rows, keyed):
    _, seqs, rows, _ = q_rows.shape
    pair = pl.BlockSpec((2, 1, rows, GROUP), lambda s, m: (0, s, 0, 0))
    return pl.pallas_call(
        attend_body,
        out_shape=[
            jax.ShapeDtypeStruct((NJ, seqs, rows, PAIR), BF),
            jax.ShapeDtypeStruct((seqs, rows, GROUP), BF),
        ],
        grid_spec=pltpu.PrefetchScalarGridSpec(
            num_scalar_prefetch=1,
            grid=(seqs,),
            in_specs=[pl.BlockSpec((1, 1, rows, GROUP), lambda s, m: (0, s, 0, 0))] + [pair] * 3,
            out_specs=[
                pl.BlockSpec((NJ, 1, rows, PAIR), lambda s, m: (0, s, 0, 0)),
                pl.BlockSpec((1, rows, GROUP), lambda s, m: (s, 0, 0)),
            ],
        ),
        compiler_params=params("arbitrary"),
        cost_estimate=COSTS["attend"],
    )(meta, q_rows, *keyed)


def tangent_body(meta, q_ref, left, mid, right, left_tan, mid_tan, right_tan, wide):
    mask = allowed_keys(meta)
    keyed, keyed_tan = (left, mid, right), (left_tan, mid_tan, right_tan)
    for n in range(wide.shape[2] // HD):
        cols = slice(n * HD, (n + 1) * HD)
        q, qt = q_ref[0, 0, :, cols], q_ref[1, 0, :, cols]
        k = rows_of(keyed, 0, cols)
        probs = probs_of(q, k, mask)
        tan = (nt(qt, k) + nt(q, rows_of(keyed_tan, 0, cols))) * SCALE
        probs_tan = probs * (tan - jnp.sum(probs * tan, axis=-1, keepdims=True))
        att = nn(probs_tan.astype(BF), rows_of(keyed, 1, cols)) + nn(
            probs.astype(BF), rows_of(keyed_tan, 1, cols)
        )
        wide[0, :, cols] = att.astype(BF)


def attend_tangent(meta, q_rows, keyed, keyed_tan, piece):
    _, seqs, rows, _ = q_rows.shape
    first, stop = PIECES[piece]
    width = (stop - first) * PAIR
    part = pl.BlockSpec((2, 1, rows, width), lambda s, m: (0, s, 0, first * PAIR // width))
    tall = pl.BlockSpec((2, 1, rows, width), lambda s, m: (0, s, 0, 0))
    return pl.pallas_call(
        tangent_body,
        out_shape=jax.ShapeDtypeStruct((seqs, rows, width), BF),
        grid_spec=pltpu.PrefetchScalarGridSpec(
            num_scalar_prefetch=1,
            grid=(seqs,),
            in_specs=[part] * 4 + [tall] * 3,
            out_specs=pl.BlockSpec((1, rows, width), lambda s, m: (s, 0, 0)),
        ),
        compiler_params=params("arbitrary"),
        cost_estimate=COSTS["tangent"],
    )(meta, q_rows, *keyed, *keyed_tan)


def gate_rows(ref, rows):
    return jnp.concatenate(
        [jnp.broadcast_to(ref[s : s + 1, :], (rows, ref.shape[1])) for s in range(2)], axis=0
    )


def flat2(ref):
    return ref[...].reshape(ref.shape[0] * ref.shape[1], ref.shape[2])


def put_halves(value, here, other, at):
    rows = here.shape[-2]
    for s in range(2):
        here[at, s] = value[2 * s * rows : (2 * s + 1) * rows]
        other[at, s] = value[(2 * s + 1) * rows : (2 * s + 2) * rows]


def project_body(att, tan, weight, gate, gate_tan, here, other):
    rows = att.shape[1]
    proj = nt(flat2(att), weight[...])
    proj_tan = nt(flat2(tan), weight[:, : tan.shape[2]])
    g, gt = gate_rows(gate, rows), gate_rows(gate_tan, rows)
    put_halves(g * proj, here, other, 0)
    put_halves(gt * proj + g * proj_tan, here, other, 1)


def project(att, tan, weight, gate, gate_tan):
    seqs, rows, _ = att.shape
    width = gate.shape[1]
    step = 512
    gates = pl.BlockSpec((2, step), lambda i: (0, i))
    block = pl.BlockSpec((2, seqs, rows // 2, step), lambda i: (0, 0, 0, i))
    return pl.pallas_call(
        project_body,
        grid=(width // step,),
        out_shape=[jax.ShapeDtypeStruct((2, seqs, rows // 2, width), F32)] * 2,
        in_specs=[vmem_spec()] * 2
        + [pl.BlockSpec((step, GROUP), lambda i: (i, 0)), gates, gates],
        out_specs=[block, block],
        compiler_params=params("arbitrary"),
        cost_estimate=COSTS["project"],
    )(att, tan, weight, gate, gate_tan)


def finish_body(tan, weight, gate, here, other):
    proj_tan = nt(flat2(tan), weight[...])
    put_halves(gate_rows(gate, tan.shape[1]) * proj_tan, here, other, 0)


def finish(tan, weight, gate):
    seqs, rows, half = tan.shape
    width = gate.shape[1]
    step = 512
    block = pl.BlockSpec((1, seqs, rows // 2, step), lambda i: (0, 0, 0, i))
    return pl.pallas_call(
        finish_body,
        grid=(width // step,),
        out_shape=[jax.ShapeDtypeStruct((1, seqs, rows // 2, width), F32)] * 2,
        in_specs=[
            vmem_spec(),
            pl.BlockSpec((step, half), lambda i: (i, 1)),
            pl.BlockSpec((2, step), lambda i: (0, i)),
        ],
        out_specs=[block, block],
        compiler_params=params("arbitrary"),
        cost_estimate=COSTS["finish"],
    )(tan, weight, gate)


def grad_body(w_own, w_sib, att, out):
    half = att.shape[2] // 2
    total = None
    for x in range(NX):
        for side, weighted in enumerate((w_own, w_sib)):
            rows = slice(side * half, (side + 1) * half)
            block = jnp.concatenate([att[x, s, rows] for s in range(2)], axis=0)
            term = nn(weighted[x], block)
            total = term if total is None else total + term
    total = total.astype(BF)
    piece = out.shape[2]
    for yl in range(NYL):
        for z in range(NZ):
            start = (yl * NZ + z) * piece
            out[z, yl] = total[start : start + piece]


def grad_terms(w_own, w_sib, att):
    width = w_own.shape[1]
    return pl.pallas_call(
        grad_body,
        out_shape=jax.ShapeDtypeStruct((NZ, NYL, width // (NZ * NYL), PAIR), BF),
        in_specs=[vmem_spec()] * 3,
        out_specs=vmem_spec(),
        compiler_params=params(),
        cost_estimate=COSTS["grad"],
    )(w_own, w_sib, att)


def on_device(
    queries, keys, values, query_tan, key_tan, value_tan, weight_out, gate, gate_tan, cotangent
):
    seq_at, uly_at = lax.axis_index("seq"), lax.axis_index("uly")
    core = uly_at % NC
    chunk = seq_at * NYH + uly_at // NC
    meta = jnp.stack([core, chunk]).astype(jnp.int32)
    seqs, rows, _ = queries.shape

    arrays = (keys, values, queries, query_tan, key_tan, value_tan)
    got = send(split_groups(meta, arrays), SWAP_CORE, "Sx")
    (kv,) = join_rows(meta, arrays[:2], got, (((0, 1), (0, NJ)),), 0)
    keyed = (send(kv, TO_NEXT, "Ha"), kv, send(kv, TO_PREV, "Hb"))
    q_rows, *tans = join_rows(
        meta, arrays[2:], got, (((0, 1), (0, NJ)),) + tuple(((2, 3), p) for p in PIECES), 2
    )
    tans = [[send(t, TO_NEXT, "T%da" % n), t, send(t, TO_PREV, "T%db" % n)] for n, t in enumerate(tans)]

    weighted = (gate[:, None, :] * cotangent.astype(F32)).astype(BF)
    weighted = weighted.reshape(seqs * rows, -1).T
    w_own = lax.all_gather(weighted, AXES, axis_index_groups=GROUPS_X)
    w_own, _ = after((w_own, kv))
    w_sib = send(w_own, SWAP_CORE, "Cswap")

    low = weight_out.astype(BF).reshape(NJ, NC, PAIR, -1)
    low = lax.dynamic_index_in_dim(low, core, 1, keepdims=False).reshape(GROUP, -1).T
    low = jnp.broadcast_to(low[None], (NYL * NZ,) + low.shape)
    low = lax.all_to_all(low, AXES, 0, 0, axis_index_groups=GROUPS_ZYL, tiled=True)
    weight = lax.all_gather(low, AXES, axis_index_groups=GROUPS_X, axis=1, tiled=True)
    weight = weight.reshape(-1, GROUP)

    quarter, att = attend(meta, q_rows, keyed)
    quarter, _ = after((quarter, low))
    quarter = lax.all_to_all(quarter, AXES, 0, 0, axis_index_groups=GROUPS_X, tiled=True)
    (quarter, tans[0][0], tans[0][2]) = after((quarter, tans[0][0], tans[0][2]))
    terms = grad_terms(w_own, w_sib, quarter)
    terms = lax.all_to_all(terms, AXES, 0, 0, axis_index_groups=GROUPS_Z, tiled=True)
    terms = jnp.sum(terms.astype(F32), axis=0).reshape(NYL * NYH, -1, PAIR)
    terms = lax.all_to_all(terms, AXES, 0, 0, axis_index_groups=GROUPS_Y, tiled=True)
    weight_grad = send(jnp.sum(terms, axis=0), TURN, "Turn").T

    tan_first = attend_tangent(meta, q_rows, keyed, tans[0], 0)
    here, other = project(att, tan_first, weight, gate, gate_tan)
    other = send(other, SWAP_CORE, "Pswap")
    tan_last = attend_tangent(meta, q_rows, keyed, tans[1], 1)
    rest, rest_other = finish(tan_last, weight, gate)
    rest_other = send(rest_other, SWAP_CORE, "Uswap")
    mixed = (here[0] + other[0]).astype(BF)
    mixed_tan = ((here[1] + other[1]) + (rest[0] + rest_other[0])).astype(BF)
    return mixed, mixed_tan, weight_grad


def solution(mesh):
    rows = P(None, ("seq", "uly"), None)
    return jax.shard_map(
        on_device,
        mesh=mesh,
        in_specs=(rows,) * 6 + (P(None, "seq"), P(), P(), rows),
        out_specs=(rows, rows, P("uly", "seq")),
        check_vma=False,
    )
```

time: 292 us -> 214 us (0.73)
  waiting for transfers between devices: 94.1 us -> 36.7 us
  starting transfers between devices: 125 us -> 71.6 us
  blocking collectives: 0 us -> 30.6 us
  local copies, waits for them, and re-layouts: 10.6 us -> 15.9 us
  Pallas kernels: 40.8 us -> 37.8 us
    ppermute x23 -> x11, waiting for transfers between devices: 70.6 us -> 8.37 us  [send(): return lax.ppermute(array, AXES, pairs)]
    ppermute x23 -> x11, starting transfers between devices: 89.9 us -> 50.6 us  [send(): return lax.ppermute(array, AXES, pairs)]
    all_to_all x0 -> x1, blocking collectives: none -> 30.6 us  [on_device(): lax.all_to_all(terms, AXES, 0, 0, axis_index_groups=GROUPS_Y, tiled=True)]
    all_to_all x1 -> x2, waiting for transfers between devices: 0.01 us -> 28.3 us  [the longest x1 28.3 us: on_device(): lax.all_to_all(low, AXES, 0, 0, axis_index_groups=GROUPS_ZYL, tiled=True)]
    all_gather x1, waiting for transfers between devices: 23.4 us -> 0.02 us  [on_device(): lax.all_gather(low, AXES, axis_index_groups=GROUPS_X, axis=1, tiled=True)]
    all_to_all x1 -> x2, starting transfers between devices: 26.6 us -> 16.6 us  [the longest x1 11.8 us: on_device(): lax.all_to_all(low, AXES, 0, 0, axis_index_groups=GROUPS_ZYL, tiled=True)]
    all_to_all x1, starting transfers between devices: 8.77 us -> 4.34 us  [on_device(): lax.all_to_all(terms, AXES, 0, 0, axis_index_groups=GROUPS_Z, tiled=True)]
    unnamed x38 -> x50, local copies, waits for them, and re-layouts: 9.3 us -> 13.7 us
  transfers between devices with their start and end apart: 27 -> 16, of which waited for: 10 -> 3; matrix products, arithmetic and copies ran while one was open for 2% -> 1% of each run, Pallas kernels for 13% -> 18%
where the time goes in v2:
time: 214 us; the launch traced here: 212 us
  starting transfers between devices  71.6 us (33%)
  Pallas kernels  37.8 us (18%)
  waiting for transfers between devices  36.7 us (17%)
  blocking collectives  30.6 us (14%)
  local copies, waits for them, and re-layouts  15.9 us (7%)
  between operations  14.5 us (7%)
  other arithmetic  5.33 us (2%)
    ppermute x11, starting transfers between devices, send(): return lax.ppermute(array, AXES, pairs)  50.6 us
    all_to_all x1, blocking collectives, on_device(): lax.all_to_all(terms, AXES, 0, 0, axis_index_groups=GROUPS_Y, tiled=True)  30.6 us
    all_to_all x1, waiting for transfers between devices, on_device(): lax.all_to_all(low, AXES, 0, 0, axis_index_groups=GROUPS_ZYL, tiled=True)  28.3 us
    unnamed x50, local copies, waits for them, and re-layouts  13.7 us
    all_to_all x1, starting transfers between devices, on_device(): lax.all_to_all(low, AXES, 0, 0, axis_index_groups=GROUPS_ZYL, tiled=True)  11.8 us
    pallas_call x2, Pallas kernels, attend_tangent(): pl.pallas_call(tangent_body, out_shape=jax.ShapeDtypeStruct((seqs, rows,...  11 us
    ppermute x11, waiting for transfers between devices, send(): return lax.ppermute(array, AXES, pairs)  8.37 us
    pallas_call x1, Pallas kernels, attend(): pl.pallas_call(attend_body, out_shape=[jax.ShapeDtypeStruct((NJ, seqs, ro...  8.37 us
  transfers between devices with their start and end apart: 16, of which 3 were waited for; matrix products, arithmetic and copies ran while one was open for 1% of the time, Pallas kernels for 18%

profile of v2, /device:TPU:30, one launch (start us, length us, event | category | flops | bytes accessed | tf_op | source)
XLA Modules:
  0.0 212.4 jit_solution(9745517716982152755)
XLA Ops:
  7.2 0.0 all-gather.6.cloned.1.call-start
  7.2 1.2 multiply_convert_fusion
  8.4 0.9 copy.17
  9.3 0.0 all-gather.6.cloned.1.call-update
  9.4 0.1 pad_add_fusion.meta
  9.5 1.0 copy-done.4
  10.5 1.0 copy-done.6
  11.6 1.0 copy-done.8
  12.6 1.9 shard_map.121
  14.5 1.9 collective-permute-start
  16.5 0.3 dynamic-slice_reduce_fusion
  16.9 1.0 broadcast_in_dim.2
  17.8 11.8 %all-to-all-start = ((bf16[16,24,1024]{2,1,0:T(8,128)(2,1)}), bf16[16,24,1024]{2,1,0:T(8,128)(2,1)}, u32[]{:S(2)}, u32[]{:S(2)}) async-start(bf16[16,24,1024]{2,1,0:T(8,128)(2,1)} %broadcast_in_dim.2), calls=%async_computation | async-start | bytes 1572864 | tf_op jit(solution)/shard_map/all_to_all | solution.py:396
  29.6 0.0 all-gather.4.cloned.1.call-start
  29.7 0.0 collective-permute-done.refs_4_.refs_2_
  29.7 1.6 shard_map.123.mid
  31.3 4.8 %collective-permute-start.1 = (bf16[2,2,128,1024]{3,2,1,0:T(8,128)(2,1)}, bf16[2,2,128,1024]{3,2,1,0:T(8,128)(2,1)S(1)}, u32[]{:S(2)}, u32[]{:S(2)}) collective-permute-start(bf16[2,2,128,1024]{3,2,1,0:T(8,128)(2,1)} %shard_map.123.mid), channel_id=1, source_target_pairs={{0,2},{1,3},{2,4},{3,5},{4,6},{5,7},{6,8},{7,9},{8,10},{9,11},{10,... | collective-permute-start | bytes 3145736 | tf_op jit(solution)/shard_map/Ha/ppermute | solution.py:75
  36.1 1.9 collective-permute-start.2
  38.1 28.3 %all-to-all-done = bf16[16,24,1024]{2,1,0:T(8,128)(2,1)} async-done(((bf16[16,24,1024]{2,1,0:T(8,128)(2,1)}), bf16[16,24,1024]{2,1,0:T(8,128)(2,1)}, u32[]{:S(2)}, u32[]{:S(2)}) %all-to-all-start) | async-done | bytes 786464 | tf_op jit(solution)/shard_map/all_to_all | solution.py:396
  66.4 0.0 all-gather.4.cloned.1.call-update
  66.4 0.0 copy-start.5
  66.4 1.0 copy-done.5
  67.4 1.0 copy-done.7
  68.5 1.0 copy-done.9
  69.5 2.9 %shard_map.122 = (bf16[2,2,128,1024]{3,2,1,0:T(8,128)(2,1)}, bf16[2,2,128,512]{3,2,1,0:T(8,128)(2,1)}, bf16[2,2,128,512]{3,2,1,0:T(8,128)(2,1)}) custom-call(s32[2]{0:T(128)S(1)} %pad_add_fusion.meta, bf16[2,64,2048]{2,1,0:T(8,128)(2,1)S(1)} %copy-done.3, bf16[2,64,2048]{2,1,0:T(8,128)(2,1)S(1)} %copy-done.5, bf16[2,64,2048]{2,1,0:T(8,128)(2,1)S(1)} %copy-done.7, ...), custom_call_target="tpu_custom_call" | custom-call | flops 1 | bytes 1 | tf_op jit(solution)/shard_map/pallas_call | solution.py:163
  72.4 5.4 %collective-permute-start.3 = (bf16[2,2,128,512]{3,2,1,0:T(8,128)(2,1)}, bf16[2,2,128,512]{3,2,1,0:T(8,128)(2,1)S(1)}, u32[]{:S(2)}, u32[]{:S(2)}) collective-permute-start(bf16[2,2,128,512]{3,2,1,0:T(8,128)(2,1)} %get-tuple-element.21.mid_tan), channel_id=1, source_target_pairs={{0,2},{1,3},{2,4},{3,5},{4,6},{5,7},{6,8},{7,9},{8,10},{9,11},{10,... | collective-permute-start | bytes 1572872 | tf_op jit(solution)/shard_map/T0a/ppermute | solution.py:75
  77.8 6.3 %collective-permute-start.4 = (bf16[2,2,128,512]{3,2,1,0:T(8,128)(2,1)}, bf16[2,2,128,512]{3,2,1,0:T(8,128)(2,1)}, u32[]{:S(2)}, u32[]{:S(2)}) collective-permute-start(bf16[2,2,128,512]{3,2,1,0:T(8,128)(2,1)} %get-tuple-element.21.mid_tan), channel_id=1, source_target_pairs={{2,0},{3,1},{4,2},{5,3},{6,4},{7,5},{8,6},{9,7},{10,8},{11,9},{12,... | collective-permute-start | bytes 1572872 | tf_op jit(solution)/shard_map/T0b/ppermute | solution.py:75
  84.1 0.0 all-gather.6.cloned.1.call-done
  84.1 1.9 collective-permute-start.9
  86.1 0.0 collective-permute-done.1.left
  86.1 1.0 copy-done.13
  87.0 1.4 collective-permute-done.2.right
  88.5 1.1 copy-done.23
  89.5 1.2 copy-done.14
  90.8 1.2 copy-done.17
  92.0 8.4 %shard_map.124 = (bf16[4,2,128,256]{3,2,1,0:T(8,128)(2,1)}, bf16[2,128,1024]{2,1,0:T(8,128)(2,1)S(1)}) custom-call(s32[2]{0:T(128)S(1)} %pad_add_fusion.meta, bf16[2,2,128,1024]{3,2,1,0:T(8,128)(2,1)S(1)} %copy-done.17, bf16[2,2,128,1024]{3,2,1,0:T(8,128)(2,1)S(1)} %copy-done.14, bf16[2,2,128,1024]{3,2,1,0:T(8,128)(2,1)} %shard_map.123.mid, ...), custom_call_target="tpu_custom_call" | custom-call | flops 34359738368 | bytes 1 | tf_op jit(solution)/shard_map/pallas_call | solution.py:215
  100.4 4.8 %all-to-all-start.1 = ((bf16[4,2,128,256]{3,2,1,0:T(8,128)(2,1)}), bf16[4,2,128,256]{3,2,1,0:T(8,128)(2,1)S(1)}, u32[]{:S(2)}, u32[]{:S(2)}) async-start(bf16[4,2,128,256]{3,2,1,0:T(8,128)(2,1)} %get-tuple-element.20), calls=%async_computation.1 | async-start | bytes 1048576 | tf_op jit(solution)/shard_map/all_to_all | solution.py:402
  105.2 2.6 %collective-permute-start.6 = (bf16[2,2,128,512]{3,2,1,0:T(8,128)(2,1)}, bf16[2,2,128,512]{3,2,1,0:T(8,128)(2,1)}, u32[]{:S(2)}, u32[]{:S(2)}) collective-permute-start(bf16[2,2,128,512]{3,2,1,0:T(8,128)(2,1)} %get-tuple-element.26.mid_tan), channel_id=1, source_target_pairs={{0,2},{1,3},{2,4},{3,5},{4,6},{5,7},{6,8},{7,9},{8,10},{9,11},{10,... | collective-permute-start | bytes 1572872 | tf_op jit(solution)/shard_map/T1a/ppermute | solution.py:75
  107.8 16.3 %collective-permute-start.7 = (bf16[2,2,128,512]{3,2,1,0:T(8,128)(2,1)}, bf16[2,2,128,512]{3,2,1,0:T(8,128)(2,1)}, u32[]{:S(2)}, u32[]{:S(2)}) collective-permute-start(bf16[2,2,128,512]{3,2,1,0:T(8,128)(2,1)} %get-tuple-element.26.mid_tan), channel_id=1, source_target_pairs={{2,0},{3,1},{4,2},{5,3},{6,4},{7,5},{8,6},{9,7},{10,8},{11,9},{12,... | collective-permute-start | bytes 1572872 | tf_op jit(solution)/shard_map/T1b/ppermute | solution.py:75
  124.1 0.0 collective-permute-done.3.left_tan
  124.1 0.0 collective-permute-done.4.right_tan
  124.1 0.0 all-to-all-done.1.att
  124.2 0.0 collective-permute-done.9.w_sib
  124.2 4.2 %shard_map.129 = bf16[8,2,96,256]{3,2,1,0:T(8,128)(2,1)} custom-call(bf16[4,1536,128]{2,1,0:T(8,128)(2,1)S(1)} %bitcast.21, bf16[4,1536,128]{2,1,0:T(8,128)(2,1)} %collective-permute-done.9.w_sib, bf16[4,2,128,256]{3,2,1,0:T(8,128)(2,1)S(1)} %all-to-all-done.1.att), custom_call_target="tpu_custom_call" | custom-call | flops 1 | bytes 1 | tf_op jit(solution)/shard_map/pallas_call | solution.py:359
  128.4 4.3 %all-to-all-start.2 = ((bf16[8,2,96,256]{3,2,1,0:T(8,128)(2,1)}), bf16[8,2,96,256]{3,2,1,0:T(8,128)(2,1)}, u32[]{:S(2)}, u32[]{:S(2)}) async-start(bf16[8,2,96,256]{3,2,1,0:T(8,128)(2,1)} %shard_map.129), calls=%async_computation.2 | async-start | bytes 1572864 | tf_op jit(solution)/shard_map/all_to_all | solution.py:405
  132.8 1.2 copy-done.18
  134.0 1.0 copy-done.21
  135.0 5.4 %shard_map.125.tan = bf16[2,128,512]{2,1,0:T(8,128)(2,1)S(1)} custom-call(s32[2]{0:T(128)S(1)} %pad_add_fusion.meta, bf16[2,2,128,1024]{3,2,1,0:T(8,128)(2,1)S(1)} %copy-done.18, bf16[2,2,128,1024]{3,2,1,0:T(8,128)(2,1)S(1)} %copy-done.15, bf16[2,2,128,1024]{3,2,1,0:T(8,128)(2,1)} %shard_map.123.mid, bf16[2,2,128,1024]{3,2,1,0:T(8,128)(2,1)} %copy-done.23, ...), custom_call_target="tpu_custom_call" | custom-call | flops 8589934592 | bytes 1 | tf_op jit(solution)/shard_map/pallas_call | solution.py:257
  140.5 0.0 all-gather.4.cloned.1.call-done
  140.5 4.9 %shard_map.126 = (f32[2,2,64,1536]{3,2,1,0:T(8,128)S(1)}, f32[2,2,64,1536]{3,2,1,0:T(8,128)}) custom-call(bf16[2,128,1024]{2,1,0:T(8,128)(2,1)S(1)} %get-tuple-element.18.att, bf16[2,128,512]{2,1,0:T(8,128)(2,1)S(1)} %shard_map.125.tan, bf16[1536,1024]{1,0:T(8,128)(2,1)} %bitcast.22, f32[2,1536]{1,0:T(2,128)S(1)} %copy-done.11, f32[2,1536]{1,0:T(2,128)S(1)} %copy-done.12), custom_call_target="tpu_custom_call" | custom-call | flops 1 | bytes 1 | tf_op jit(solution)/shard_map/pallas_call | solution.py:303
  145.5 1.9 collective-permute-start.5
  147.4 0.0 collective-permute-done.6.left_tan
  147.4 0.0 collective-permute-done.7.right_tan
  147.4 5.5 %shard_map.127.tan = bf16[2,128,512]{2,1,0:T(8,128)(2,1)S(1)} custom-call(s32[2]{0:T(128)S(1)} %pad_add_fusion.meta, bf16[2,2,128,1024]{3,2,1,0:T(8,128)(2,1)S(1)} %copy-done.19, bf16[2,2,128,1024]{3,2,1,0:T(8,128)(2,1)S(1)} %copy-done.16, bf16[2,2,128,1024]{3,2,1,0:T(8,128)(2,1)} %shard_map.123.mid, bf16[2,2,128,1024]{3,2,1,0:T(8,128)(2,1)} %copy-done.23, ...), custom_call_target="tpu_custom_call" | custom-call | flops 8589934592 | bytes 1 | tf_op jit(solution)/shard_map/pallas_call | solution.py:257
  153.0 2.8 %shard_map.128 = (f32[1,2,64,1536]{3,2,1,0:T(8,128)S(1)}, f32[1,2,64,1536]{3,2,1,0:T(8,128)S(1)}) custom-call(bf16[2,128,512]{2,1,0:T(8,128)(2,1)S(1)} %shard_map.127.tan, bf16[1536,1024]{1,0:T(8,128)(2,1)} %bitcast.23, f32[2,1536]{1,0:T(2,128)S(1)} %copy-done.11), custom_call_target="tpu_custom_call" | custom-call | flops 1 | bytes 1 | tf_op jit(solution)/shard_map/pallas_call | solution.py:325
  155.8 2.4 %collective-permute-start.8 = (f32[1,2,64,1536]{3,2,1,0:T(8,128)S(1)}, f32[1,2,64,1536]{3,2,1,0:T(8,128)}, u32[]{:S(2)}, u32[]{:S(2)}) collective-permute-start(f32[1,2,64,1536]{3,2,1,0:T(8,128)S(1)} %get-tuple-element.28), channel_id=1, source_target_pairs={{0,1},{1,0},{2,3},{3,2},{4,5},{5,4},{6,7},{7,6},{8,9},{9,8},{10,11... | collective-permute-start | bytes 2359304 | tf_op jit(solution)/shard_map/Uswap/ppermute | solution.py:75
  158.2 0.0 all-to-all-done.2
  158.3 1.3 convert_reduce_fusion
  159.5 30.6 %all_to_all.20 = f32[8,24,256]{2,1,0:T(8,128)S(1)} all-to-all(f32[8,24,256]{2,1,0:T(8,128)S(1)} %bitcast.26), channel_id=1, replica_groups={{0,2,4,6,256,258,260,262},{1,3,5,7,257,259,261,263},{8,10,12,14,264,266..., dimensions={0} | all-to-all | bytes 393216 | tf_op jit(solution)/shard_map/all_to_all | solution.py:407
  190.2 5.1 %collective-permute-start.10 = (f32[24,256]{1,0:T(8,128)S(1)}, f32[24,256]{1,0:T(8,128)S(1)}, u32[]{:S(2)}, u32[]{:S(2)}) collective-permute-start(f32[24,256]{1,0:T(8,128)S(1)} %reduce_sum.19), channel_id=1, source_target_pairs={{0,0},{1,1},{2,8},{3,9},{4,16},{5,17},{6,24},{7,25},{8,2},{9,3},{1... | collective-permute-start | bytes 73736 | tf_op jit(solution)/shard_map/Turn/ppermute | solution.py:75
  195.2 6.9 %collective-permute-done.10 = f32[24,256]{1,0:T(8,128)S(1)} collective-permute-done((f32[24,256]{1,0:T(8,128)S(1)}, f32[24,256]{1,0:T(8,128)S(1)}, u32[]{:S(2)}, u32[]{:S(2)}) %collective-permute-start.10) | collective-permute-done | bytes 24608 | tf_op jit(solution)/shard_map/Turn/ppermute | solution.py:75
  202.2 0.0 collective-permute-done.5
  202.2 2.8 %fusion.4 = (bf16[2,64,1536]{2,1,0:T(8,128)(2,1)}, bf16[2,64,1536]{2,1,0:T(8,128)(2,1)}) fusion(f32[1,2,64,1536]{3,2,1,0:T(8,128)S(1)} %get-tuple-element.27, f32[1,2,64,1536]{3,2,1,0:T(8,128)} %collective-permute-done.8, f32[2,2,64,1536]{3,2,1,0:T(8,128)} %collective-permute-done.5, f32[2,2,64,1536]{3,2,1,0:T(8,128)S(1)} %get-tuple-element.24), kind=kLoop, calls=%fused_computation.8 | loop fusion | flops 1179648 | bytes 5505024 | tf_op jit(solution)/shard_map/convert_element_type | solution.py:417
  205.0 0.6 copy.21
  (40 shorter events, 0.2 us)
Async XLA Ops:
  7.2 2.3 %copy-start.3 = (bf16[2,64,2048]{2,1,0:T(8,128)(2,1)S(1)}, bf16[2,64,2048]{2,1,0:T(8,128)(2,1)}, u32[]{:S(2)}) copy-start(bf16[2,64,2048]{2,1,0:T(8,128)(2,1)} %refs_0_.4) | copy-start | bytes 1572868
  7.2 2.3 %copy-start.1 = (bf16[2,64,2048]{2,1,0:T(8,128)(2,1)S(1)}, bf16[2,64,2048]{2,1,0:T(8,128)(2,1)}, u32[]{:S(2)}) copy-start(bf16[2,64,2048]{2,1,0:T(8,128)(2,1)} %refs_0_.5) | copy-start | bytes 1572868
  7.2 2.3 %copy-start.2 = (bf16[2,64,2048]{2,1,0:T(8,128)(2,1)S(1)}, bf16[2,64,2048]{2,1,0:T(8,128)(2,1)}, u32[]{:S(2)}) copy-start(bf16[2,64,2048]{2,1,0:T(8,128)(2,1)} %refs_1_.5) | copy-start | bytes 1572868
  7.2 76.9 %all-gather.6.cloned.1.call-start = ((), (), s32[]{:S(2)}) async-start(), calls=%async_computation.5 | async-start | bytes 1966080 | tf_op jit(solution)/shard_map/all_gather | solution.py:389
  9.5 1.0 copy-start.4
  10.5 1.0 copy-start.6
  11.5 1.0 copy-start.8
  12.6 3.8 %copy-start.22 = (f32[2048,24]{0,1:T(8,128)S(1)}, f32[2048,24]{0,1:T(8,128)}, u32[]{:S(2)}) copy-start(f32[2048,24]{0,1:T(8,128)} %param.16) | copy-start | bytes 589828
  14.5 15.2 %collective-permute-start = (bf16[6,2,64,1024]{3,2,1,0:T(8,128)(2,1)}, bf16[6,2,64,1024]{3,2,1,0:T(8,128)(2,1)S(1)}, u32[]{:S(2)}, u32[]{:S(2)}) collective-permute-start(bf16[6,2,64,1024]{3,2,1,0:T(8,128)(2,1)} %shard_map.121), channel_id=1, source_target_pairs={{0,1},{1,0},{2,3},{3,2},{4,5},{5,4},{6,7},{7,6},{8,9},{9,8},{10,11... | collective-permute-start | bytes 4718600 | tf_op jit(solution)/shard_map/Sx/ppermute | solution.py:75
  17.8 48.5 %all-to-all-start = ((bf16[16,24,1024]{2,1,0:T(8,128)(2,1)}), bf16[16,24,1024]{2,1,0:T(8,128)(2,1)}, u32[]{:S(2)}, u32[]{:S(2)}) async-start(bf16[16,24,1024]{2,1,0:T(8,128)(2,1)} %broadcast_in_dim.2), calls=%async_computation | async-start | bytes 1572864 | tf_op jit(solution)/shard_map/all_to_all | solution.py:396
  29.6 110.9 %all-gather.4.cloned.1.call-start = ((), (), s32[]{:S(2)}) async-start(), calls=%async_computation.4 | async-start | bytes 3932160 | tf_op jit(solution)/shard_map/all_gather | solution.py:397
  29.7 1.6 copy-start
  31.3 54.7 %collective-permute-start.1 = (bf16[2,2,128,1024]{3,2,1,0:T(8,128)(2,1)}, bf16[2,2,128,1024]{3,2,1,0:T(8,128)(2,1)S(1)}, u32[]{:S(2)}, u32[]{:S(2)}) collective-permute-start(bf16[2,2,128,1024]{3,2,1,0:T(8,128)(2,1)} %shard_map.123.mid), channel_id=1, source_target_pairs={{0,2},{1,3},{2,4},{3,5},{4,6},{5,7},{6,8},{7,9},{8,10},{9,11},{10,... | collective-permute-start | bytes 3145736 | tf_op jit(solution)/shard_map/Ha/ppermute | solution.py:75
  36.1 52.3 %collective-permute-start.2 = (bf16[2,2,128,1024]{3,2,1,0:T(8,128)(2,1)}, bf16[2,2,128,1024]{3,2,1,0:T(8,128)(2,1)S(1)}, u32[]{:S(2)}, u32[]{:S(2)}) collective-permute-start(bf16[2,2,128,1024]{3,2,1,0:T(8,128)(2,1)} %shard_map.123.mid), channel_id=1, source_target_pairs={{2,0},{3,1},{4,2},{5,3},{6,4},{7,5},{8,6},{9,7},{10,8},{11,9},{12,... | collective-permute-start | bytes 3145736 | tf_op jit(solution)/shard_map/Hb/ppermute | solution.py:75
  66.4 1.0 copy-start.5
  67.4 1.0 copy-start.7
  68.5 1.0 copy-start.9
  72.4 51.7 %collective-permute-start.3 = (bf16[2,2,128,512]{3,2,1,0:T(8,128)(2,1)}, bf16[2,2,128,512]{3,2,1,0:T(8,128)(2,1)S(1)}, u32[]{:S(2)}, u32[]{:S(2)}) collective-permute-start(bf16[2,2,128,512]{3,2,1,0:T(8,128)(2,1)} %get-tuple-element.21.mid_tan), channel_id=1, source_target_pairs={{0,2},{1,3},{2,4},{3,5},{4,6},{5,7},{6,8},{7,9},{8,10},{9,11},{10,... | collective-permute-start | bytes 1572872 | tf_op jit(solution)/shard_map/T0a/ppermute | solution.py:75
  77.8 46.3 %collective-permute-start.4 = (bf16[2,2,128,512]{3,2,1,0:T(8,128)(2,1)}, bf16[2,2,128,512]{3,2,1,0:T(8,128)(2,1)}, u32[]{:S(2)}, u32[]{:S(2)}) collective-permute-start(bf16[2,2,128,512]{3,2,1,0:T(8,128)(2,1)} %get-tuple-element.21.mid_tan), channel_id=1, source_target_pairs={{2,0},{3,1},{4,2},{5,3},{6,4},{7,5},{8,6},{9,7},{10,8},{11,9},{12,... | collective-permute-start | bytes 1572872 | tf_op jit(solution)/shard_map/T0b/ppermute | solution.py:75
  84.1 40.0 %collective-permute-start.9 = (bf16[4,1536,128]{2,1,0:T(8,128)(2,1)}, bf16[4,1536,128]{2,1,0:T(8,128)(2,1)}, u32[]{:S(2)}, u32[]{:S(2)}) collective-permute-start(bf16[4,1536,128]{2,1,0:T(8,128)(2,1)} %bitcast.20), channel_id=1, source_target_pairs={{0,1},{1,0},{2,3},{3,2},{4,5},{5,4},{6,7},{7,6},{8,9},{9,8},{10,11... | collective-permute-start | bytes 4718600 | tf_op jit(solution)/shard_map/Cswap/ppermute | solution.py:75
  86.1 1.0 copy-start.13
  88.5 1.1 copy-start.23
  89.5 1.2 copy-start.14
  90.8 1.2 copy-start.17
  92.0 32.2 %copy-start.10 = (bf16[6144,128]{1,0:T(8,128)(2,1)S(1)}, bf16[6144,128]{1,0:T(8,128)(2,1)}, u32[]{:S(2)}) copy-start(bf16[6144,128]{1,0:T(8,128)(2,1)} %all-gather.6.cloned.1.call-done) | copy-start | bytes 4718596
  100.4 23.8 %all-to-all-start.1 = ((bf16[4,2,128,256]{3,2,1,0:T(8,128)(2,1)}), bf16[4,2,128,256]{3,2,1,0:T(8,128)(2,1)S(1)}, u32[]{:S(2)}, u32[]{:S(2)}) async-start(bf16[4,2,128,256]{3,2,1,0:T(8,128)(2,1)} %get-tuple-element.20), calls=%async_computation.1 | async-start | bytes 1048576 | tf_op jit(solution)/shard_map/all_to_all | solution.py:402
  105.2 42.2 %collective-permute-start.6 = (bf16[2,2,128,512]{3,2,1,0:T(8,128)(2,1)}, bf16[2,2,128,512]{3,2,1,0:T(8,128)(2,1)}, u32[]{:S(2)}, u32[]{:S(2)}) collective-permute-start(bf16[2,2,128,512]{3,2,1,0:T(8,128)(2,1)} %get-tuple-element.26.mid_tan), channel_id=1, source_target_pairs={{0,2},{1,3},{2,4},{3,5},{4,6},{5,7},{6,8},{7,9},{8,10},{9,11},{10,... | collective-permute-start | bytes 1572872 | tf_op jit(solution)/shard_map/T1a/ppermute | solution.py:75
  107.8 39.6 %collective-permute-start.7 = (bf16[2,2,128,512]{3,2,1,0:T(8,128)(2,1)}, bf16[2,2,128,512]{3,2,1,0:T(8,128)(2,1)}, u32[]{:S(2)}, u32[]{:S(2)}) collective-permute-start(bf16[2,2,128,512]{3,2,1,0:T(8,128)(2,1)} %get-tuple-element.26.mid_tan), channel_id=1, source_target_pairs={{2,0},{3,1},{4,2},{5,3},{6,4},{7,5},{8,6},{9,7},{10,8},{11,9},{12,... | collective-permute-start | bytes 1572872 | tf_op jit(solution)/shard_map/T1b/ppermute | solution.py:75
  124.1 4.3 %copy-start.20 = (bf16[2,2,128,512]{3,2,1,0:T(8,128)(2,1)}, bf16[2,2,128,512]{3,2,1,0:T(8,128)(2,1)S(1)}, u32[]{:S(2)}) copy-start(bf16[2,2,128,512]{3,2,1,0:T(8,128)(2,1)S(1)} %collective-permute-done.3.left_tan) | copy-start | bytes 1572868
  128.4 4.4 %copy-start.15 = (bf16[2,2,128,1024]{3,2,1,0:T(8,128)(2,1)S(1)}, bf16[2,2,128,1024]{3,2,1,0:T(8,128)(2,1)}, u32[]{:S(2)}) copy-start(bf16[2,2,128,1024]{3,2,1,0:T(8,128)(2,1)} %copy-done.13) | copy-start | bytes 3145732
  128.4 29.8 %all-to-all-start.2 = ((bf16[8,2,96,256]{3,2,1,0:T(8,128)(2,1)}), bf16[8,2,96,256]{3,2,1,0:T(8,128)(2,1)}, u32[]{:S(2)}, u32[]{:S(2)}) async-start(bf16[8,2,96,256]{3,2,1,0:T(8,128)(2,1)} %shard_map.129), calls=%async_computation.2 | async-start | bytes 1572864 | tf_op jit(solution)/shard_map/all_to_all | solution.py:405
  132.8 1.2 copy-start.18
  134.0 1.0 copy-start.21
  135.0 5.5 %copy-start.11 = (f32[2,1536]{1,0:T(2,128)S(1)}, f32[2,1536]{1,0:T(2,128)}, u32[]{:S(2)}) copy-start(f32[2,1536]{1,0:T(2,128)} %gate.3) | copy-start | bytes 36868
  135.0 5.5 %copy-start.12 = (f32[2,1536]{1,0:T(2,128)S(1)}, f32[2,1536]{1,0:T(2,128)}, u32[]{:S(2)}) copy-start(f32[2,1536]{1,0:T(2,128)} %gate_tan.1) | copy-start | bytes 36868
  140.5 6.9 %copy-start.16 = (bf16[2,2,128,1024]{3,2,1,0:T(8,128)(2,1)S(1)}, bf16[2,2,128,1024]{3,2,1,0:T(8,128)(2,1)}, u32[]{:S(2)}) copy-start(bf16[2,2,128,1024]{3,2,1,0:T(8,128)(2,1)} %copy-done.13) | copy-start | bytes 3145732
  140.5 6.9 %copy-start.19 = (bf16[2,2,128,1024]{3,2,1,0:T(8,128)(2,1)S(1)}, bf16[2,2,128,1024]{3,2,1,0:T(8,128)(2,1)}, u32[]{:S(2)}) copy-start(bf16[2,2,128,1024]{3,2,1,0:T(8,128)(2,1)} %get-tuple-element.17.q_ref) | copy-start | bytes 3145732
  145.5 56.7 %collective-permute-start.5 = (f32[2,2,64,1536]{3,2,1,0:T(8,128)}, f32[2,2,64,1536]{3,2,1,0:T(8,128)}, u32[]{:S(2)}, u32[]{:S(2)}) collective-permute-start(f32[2,2,64,1536]{3,2,1,0:T(8,128)} %get-tuple-element.25), channel_id=1, source_target_pairs={{0,1},{1,0},{2,3},{3,2},{4,5},{5,4},{6,7},{7,6},{8,9},{9,8},{10,11... | collective-permute-start | bytes 4718600 | tf_op jit(solution)/shard_map/Pswap/ppermute | solution.py:75
  155.8 46.4 %collective-permute-start.8 = (f32[1,2,64,1536]{3,2,1,0:T(8,128)S(1)}, f32[1,2,64,1536]{3,2,1,0:T(8,128)}, u32[]{:S(2)}, u32[]{:S(2)}) collective-permute-start(f32[1,2,64,1536]{3,2,1,0:T(8,128)S(1)} %get-tuple-element.28), channel_id=1, source_target_pairs={{0,1},{1,0},{2,3},{3,2},{4,5},{5,4},{6,7},{7,6},{8,9},{9,8},{10,11... | collective-permute-start | bytes 2359304 | tf_op jit(solution)/shard_map/Uswap/ppermute | solution.py:75
  190.2 12.0 %collective-permute-start.10 = (f32[24,256]{1,0:T(8,128)S(1)}, f32[24,256]{1,0:T(8,128)S(1)}, u32[]{:S(2)}, u32[]{:S(2)}) collective-permute-start(f32[24,256]{1,0:T(8,128)S(1)} %reduce_sum.19), channel_id=1, source_target_pairs={{0,0},{1,1},{2,8},{3,9},{4,16},{5,17},{6,24},{7,25},{8,2},{9,3},{1... | collective-permute-start | bytes 73736 | tf_op jit(solution)/shard_map/Turn/ppermute | solution.py:75
Sparse Core Ops, SparseCore 0:
  10.7 35.0 all-gather.5
  66.5 51.8 all-gather.3

commit v3 on v2

--- a/solution.py
+++ b/solution.py
@@ -15,6 +15,7 @@
 GROUP = NJ * PAIR
 PIECES = ((0, 2), (2, 4))
 SCALE = HD ** (-0.5)
+LOG2E = 1.4426950408889634
 BF = jnp.bfloat16
 F32 = jnp.float32
 
@@ -60,9 +61,9 @@
     [device_of(x, yl, yh, z, c) for z in range(NZ)]
     for yl in range(NYL) for yh in range(NYH) for x in range(NX) for c in range(NC)
 ]
-GROUPS_ZYL = [
-    [device_of(x, yl, yh, z, c) for yl in range(NYL) for z in range(NZ)]
-    for yh in range(NYH) for x in range(NX) for c in range(NC)
+GROUPS_XYL = [
+    [device_of(x, yl, yh, z, c) for yl in range(NYL) for x in range(NX)]
+    for yh in range(NYH) for z in range(NZ) for c in range(NC)
 ]
 GROUPS_Y = [
     [device_of(x, yl, yh, z, c) for yl in range(NYL) for yh in range(NYH)]
@@ -97,7 +98,7 @@
 
 def params(*semantics):
     return pltpu.CompilerParams(
-        vmem_limit_bytes=50 * 2**20, dimension_semantics=semantics or None
+        vmem_limit_bytes=60 * 2**20, dimension_semantics=semantics or None
     )
 
 
@@ -108,10 +109,10 @@
 COSTS = dict(
     split=cost(1, 1),
     join=cost(1, 1),
-    attend=cost(2**35, 1),
+    attend=cost(2**37, 1),
     tangent=cost(2**33, 1),
-    project=cost(1, 1),
-    finish=cost(1, 1),
+    project=cost(2**33, 1),
+    finish=cost(2**33, 1),
     grad=cost(1, 1),
 )
 
@@ -173,38 +174,43 @@
     )(meta, *arrays, got)
 
 
-def allowed_keys(meta):
+def key_bias(meta):
     core, chunk = meta[0], meta[1]
     span = 2 * 64
-    shape = (span, 3 * span)
-    rows = lax.broadcasted_iota(jnp.int32, shape, 0)
-    cols = lax.broadcasted_iota(jnp.int32, shape, 1)
+    rows = lax.broadcasted_iota(jnp.int32, (span, span), 0)
+    cols = lax.broadcasted_iota(jnp.int32, (span, span), 1)
     q_pos = (rows + 64 * core) & (span - 1)
     k_pos = (cols + 64 * core) & (span - 1)
-    block = cols >> 7
-    before = (block == 0) & (k_pos >= q_pos) & (chunk > 0)
-    after = (block == 2) & (k_pos <= q_pos) & (chunk < COUNT // NC - 1)
-    return before | (block == 1) | after
-
-
-def probs_of(q, k, mask):
-    scores = jnp.where(mask, nt(q, k) * SCALE, -1e30)
-    top = jnp.max(scores, axis=-1, keepdims=True)
-    terms = jnp.exp(scores - top)
-    return terms / jnp.sum(terms, axis=-1, keepdims=True)
-
-
-def rows_of(refs, a, cols):
-    return jnp.concatenate([ref[a, 0, :, cols] for ref in refs], axis=0)
+    before = (k_pos >= q_pos) & (chunk > 0)
+    after_ = (k_pos <= q_pos) & (chunk < COUNT // NC - 1)
+    return jnp.where(before, 0.0, -1e30), jnp.where(after_, 0.0, -1e30)
+
+
+def exp_terms(q, keys, bias):
+    scores = [nt(q, k) for k in keys]
+    scores = [scores[0] + bias[0], scores[1], scores[2] + bias[1]]
+    top = jnp.maximum(jnp.maximum(scores[0], scores[1]), scores[2])
+    top = jnp.max(top, axis=-1, keepdims=True)
+    terms = [jnp.exp2((score - top) * (SCALE * LOG2E)) for score in scores]
+    return terms, 1.0 / jnp.sum(terms[0] + terms[1] + terms[2], axis=-1, keepdims=True)
+
+
+def added(terms):
+    return terms[0] + terms[1] + terms[2]
+
+
+def blocks_of(refs, a, cols):
+    return [ref[a, 0, :, cols] for ref in refs]
 
 
 def attend_body(meta, q_ref, left, mid, right, quarter, wide):
-    mask = allowed_keys(meta)
+    bias = key_bias(meta)
     keyed = (left, mid, right)
     for n in range(GROUP // HD):
         cols = slice(n * HD, (n + 1) * HD)
-        probs = probs_of(q_ref[0, 0, :, cols], rows_of(keyed, 0, cols), mask).astype(BF)
-        att = nn(probs, rows_of(keyed, 1, cols)).astype(BF)
+        terms, inverse = exp_terms(q_ref[0, 0, :, cols], blocks_of(keyed, 0, cols), bias)
+        values = blocks_of(keyed, 1, cols)
+        att = added([nn((t * inverse).astype(BF), v) for t, v in zip(terms, values)]).astype(BF)
         quarter[n // 2, 0, :, (n % 2) * HD : (n % 2 + 1) * HD] = att
         wide[0, :, cols] = att
 
@@ -233,18 +239,22 @@
 
 
 def tangent_body(meta, q_ref, left, mid, right, left_tan, mid_tan, right_tan, wide):
-    mask = allowed_keys(meta)
+    bias = key_bias(meta)
     keyed, keyed_tan = (left, mid, right), (left_tan, mid_tan, right_tan)
     for n in range(wide.shape[2] // HD):
         cols = slice(n * HD, (n + 1) * HD)
         q, qt = q_ref[0, 0, :, cols], q_ref[1, 0, :, cols]
-        k = rows_of(keyed, 0, cols)
-        probs = probs_of(q, k, mask)
-        tan = (nt(qt, k) + nt(q, rows_of(keyed_tan, 0, cols))) * SCALE
-        probs_tan = probs * (tan - jnp.sum(probs * tan, axis=-1, keepdims=True))
-        att = nn(probs_tan.astype(BF), rows_of(keyed, 1, cols)) + nn(
-            probs.astype(BF), rows_of(keyed_tan, 1, cols)
-        )
+        keys = blocks_of(keyed, 0, cols)
+        terms, inverse = exp_terms(q, keys, bias)
+        probs = [t * inverse for t in terms]
+        tans = [
+            (nt(qt, k) + nt(q, kt)) * SCALE
+            for k, kt in zip(keys, blocks_of(keyed_tan, 0, cols))
+        ]
+        mean = jnp.sum(added([p * t for p, t in zip(probs, tans)]), axis=-1, keepdims=True)
+        att = added([nn(p.astype(BF), v) for p, v in zip(probs, blocks_of(keyed_tan, 1, cols))])
+        probs = [p * (t - mean) for p, t in zip(probs, tans)]
+        att += added([nn(p.astype(BF), v) for p, v in zip(probs, blocks_of(keyed, 1, cols))])
         wide[0, :, cols] = att.astype(BF)
 
 
@@ -384,6 +394,7 @@
     )
     tans = [[send(t, TO_NEXT, "T%da" % n), t, send(t, TO_PREV, "T%db" % n)] for n, t in enumerate(tans)]
 
+    cotangent, _ = after((cotangent, got))
     weighted = (gate[:, None, :] * cotangent.astype(F32)).astype(BF)
     weighted = weighted.reshape(seqs * rows, -1).T
     w_own = lax.all_gather(weighted, AXES, axis_index_groups=GROUPS_X)
@@ -392,25 +403,30 @@
 
     low = weight_out.astype(BF).reshape(NJ, NC, PAIR, -1)
     low = lax.dynamic_index_in_dim(low, core, 1, keepdims=False).reshape(GROUP, -1).T
-    low = jnp.broadcast_to(low[None], (NYL * NZ,) + low.shape)
-    low = lax.all_to_all(low, AXES, 0, 0, axis_index_groups=GROUPS_ZYL, tiled=True)
-    weight = lax.all_gather(low, AXES, axis_index_groups=GROUPS_X, axis=1, tiled=True)
+    low = jnp.broadcast_to(low[None], (NYL * NX,) + low.shape)
+    low = lax.all_to_all(low, AXES, 0, 0, axis_index_groups=GROUPS_XYL, tiled=True)
+    low = low.reshape(NYL, -1, GROUP)
+    weight = lax.all_gather(low, AXES, axis_index_groups=GROUPS_Z, axis=1, tiled=True)
     weight = weight.reshape(-1, GROUP)
 
     quarter, att = attend(meta, q_rows, keyed)
     quarter, _ = after((quarter, low))
     quarter = lax.all_to_all(quarter, AXES, 0, 0, axis_index_groups=GROUPS_X, tiled=True)
-    (quarter, tans[0][0], tans[0][2]) = after((quarter, tans[0][0], tans[0][2]))
+    (quarter, tans[1][0], tans[1][2]) = after((quarter, tans[1][0], tans[1][2]))
     terms = grad_terms(w_own, w_sib, quarter)
     terms = lax.all_to_all(terms, AXES, 0, 0, axis_index_groups=GROUPS_Z, tiled=True)
     terms = jnp.sum(terms.astype(F32), axis=0).reshape(NYL * NYH, -1, PAIR)
+    summed = terms
     terms = lax.all_to_all(terms, AXES, 0, 0, axis_index_groups=GROUPS_Y, tiled=True)
-    weight_grad = send(jnp.sum(terms, axis=0), TURN, "Turn").T
+    terms = jnp.sum(terms, axis=0)
+    weight_grad = send(terms, TURN, "Turn").T
 
     tan_first = attend_tangent(meta, q_rows, keyed, tans[0], 0)
+    att, _ = after((att, summed))
     here, other = project(att, tan_first, weight, gate, gate_tan)
     other = send(other, SWAP_CORE, "Pswap")
     tan_last = attend_tangent(meta, q_rows, keyed, tans[1], 1)
+    tan_last, _ = after((tan_last, terms))
     rest, rest_other = finish(tan_last, weight, gate)
     rest_other = send(rest_other, SWAP_CORE, "Uswap")
     mixed = (here[0] + other[0]).astype(BF)

time: 214 us -> 230 us (1.075)
  blocking collectives: 30.6 us -> 49.8 us
  local copies, waits for them, and re-layouts: 15.9 us -> 4.21 us
  Pallas kernels: 37.8 us -> 47 us
  starting transfers between devices: 71.6 us -> 79.5 us
  waiting for transfers between devices: 36.7 us -> 30.8 us
    all_to_all x1, waiting for transfers between devices: 28.3 us -> 0.01 us  [on_device(): lax.all_to_all(terms, AXES, 0, 0, axis_index_groups=GROUPS_Y, tiled=True)]
    all_to_all x1, blocking collectives: 30.6 us -> 49.8 us  [on_device(): lax.all_to_all(low, AXES, 0, 0, axis_index_groups=GROUPS_XYL, tiled=True)]
    ppermute x11, starting transfers between devices: 50.6 us -> 32.1 us  [send(): return lax.ppermute(array, AXES, pairs)]
    all_to_all x1, starting transfers between devices: 11.8 us -> 26.4 us  [on_device(): lax.all_to_all(terms, AXES, 0, 0, axis_index_groups=GROUPS_Y, tiled=True)]
    all_to_all x1, starting transfers between devices: 4.83 us -> 17.4 us  [on_device(): lax.all_to_all(quarter, AXES, 0, 0, axis_index_groups=GROUPS_X, tiled=True)]
    unnamed x50 -> x18, local copies, waits for them, and re-layouts: 13.7 us -> 2.69 us
    all_to_all x1, waiting for transfers between devices: 0.01 us -> 9.21 us  [on_device(): lax.all_to_all(terms, AXES, 0, 0, axis_index_groups=GROUPS_Z, tiled=True)]
    all_to_all x1, waiting for transfers between devices: 0.01 us -> 8.33 us  [on_device(): lax.all_to_all(quarter, AXES, 0, 0, axis_index_groups=GROUPS_X, tiled=True)]
  transfers between devices with their start and end apart: 16 -> 16, of which waited for: 3 -> 4; matrix products, arithmetic and copies ran while one was open for 1% -> 1% of each run, Pallas kernels for 18% -> 19%
where the time goes in v3:
time: 230 us; the launch traced here: 229 us
  starting transfers between devices  79.5 us (35%)
  blocking collectives  49.8 us (22%)
  Pallas kernels  47 us (20%)
  waiting for transfers between devices  30.8 us (13%)
  between operations  14.3 us (6%)
  local copies, waits for them, and re-layouts  4.21 us (2%)
  other arithmetic  3.8 us (2%)
    all_to_all x1, blocking collectives, on_device(): lax.all_to_all(low, AXES, 0, 0, axis_index_groups=GROUPS_XYL, tiled=True)  49.8 us
    ppermute x11, starting transfers between devices, send(): return lax.ppermute(array, AXES, pairs)  32.1 us
    all_to_all x1, starting transfers between devices, on_device(): lax.all_to_all(terms, AXES, 0, 0, axis_index_groups=GROUPS_Y, tiled=True)  26.4 us
    all_to_all x1, starting transfers between devices, on_device(): lax.all_to_all(quarter, AXES, 0, 0, axis_index_groups=GROUPS_X, tiled=True)  17.4 us
    pallas_call x2, Pallas kernels, attend_tangent(): pl.pallas_call(tangent_body, out_shape=jax.ShapeDtypeStruct((seqs, rows,...  13.9 us
    ppermute x11, waiting for transfers between devices, send(): return lax.ppermute(array, AXES, pairs)  13.2 us
    all_to_all x1, waiting for transfers between devices, on_device(): lax.all_to_all(terms, AXES, 0, 0, axis_index_groups=GROUPS_Z, tiled=True)  9.21 us
    pallas_call x1, Pallas kernels, attend(): pl.pallas_call(attend_body, out_shape=[jax.ShapeDtypeStruct((NJ, seqs, ro...  9.17 us
  transfers between devices with their start and end apart: 16, of which 4 were waited for; matrix products, arithmetic and copies ran while one was open for 1% of the time, Pallas kernels for 19%

profile of v3, /device:TPU:30, one launch (start us, length us, event | category | flops | bytes accessed | tf_op | source)
XLA Modules:
  0.0 229.4 jit_solution(5418390503268994236)
XLA Ops:
  7.2 0.0 all-gather.6.cloned.1.call-start
  7.2 0.6 pad_add_fusion.meta
  7.8 0.0 copy-start.4
  7.8 0.0 copy-start.6
  7.8 3.3 %shard_map.121 = bf16[6,2,64,1024]{3,2,1,0:T(8,128)(2,1)} custom-call(s32[2]{0:T(128)} %pad_add_fusion.meta, bf16[2,64,2048]{2,1,0:T(8,128)(2,1)} %refs_0_.5, bf16[2,64,2048]{2,1,0:T(8,128)(2,1)} %refs_1_.5, bf16[2,64,2048]{2,1,0:T(8,128)(2,1)} %refs_0_.4, bf16[2,64,2048]{2,1,0:T(8,128)(2,1)} %refs_1_.4, bf16[2,64,2048]{2,1,0:T(8,128)(2,1)} %refs_2_.3, ...), custom_call_target="tpu_custom_call" | custom-call | flops 1 | bytes 1 | tf_op jit(solution)/shard_map/pallas_call | solution.py:136
  11.1 1.9 collective-permute-start
  13.0 3.6 %collective-permute-done.refs_4_.refs_2_ = bf16[6,2,64,1024]{3,2,1,0:T(8,128)(2,1)S(1)} collective-permute-done((bf16[6,2,64,1024]{3,2,1,0:T(8,128)(2,1)}, bf16[6,2,64,1024]{3,2,1,0:T(8,128)(2,1)S(1)}, u32[]{:S(2)}, u32[]{:S(2)}) %collective-permute-start) | collective-permute-done | bytes 1572896 | tf_op jit(solution)/shard_map/Sx/ppermute | solution.py:76
  16.6 0.0 copy-done.4
  16.6 0.0 copy-done.6
  16.6 0.0 copy-start
  16.6 0.1 multiply_convert_fusion
  16.7 1.1 copy.16
  17.8 0.0 all-gather.6.cloned.1.call-update
  17.9 0.0 copy-start.5
  17.9 0.0 all-gather.4.cloned.1.call-start
  17.9 0.0 copy-done
  18.0 2.8 %shard_map.123.mid = bf16[2,2,128,1024]{3,2,1,0:T(8,128)(2,1)} custom-call(s32[2]{0:T(128)} %pad_add_fusion.meta, bf16[2,64,2048]{2,1,0:T(8,128)(2,1)} %refs_0_.5, bf16[2,64,2048]{2,1,0:T(8,128)(2,1)} %refs_1_.5, bf16[6,2,64,1024]{3,2,1,0:T(8,128)(2,1)} %copy-done), custom_call_target="tpu_custom_call" | custom-call | flops 1 | bytes 1 | tf_op jit(solution)/shard_map/pallas_call | solution.py:164
  20.8 4.8 %collective-permute-start.1 = (bf16[2,2,128,1024]{3,2,1,0:T(8,128)(2,1)}, bf16[2,2,128,1024]{3,2,1,0:T(8,128)(2,1)S(1)}, u32[]{:S(2)}, u32[]{:S(2)}) collective-permute-start(bf16[2,2,128,1024]{3,2,1,0:T(8,128)(2,1)} %shard_map.123.mid), channel_id=1, source_target_pairs={{0,2},{1,3},{2,4},{3,5},{4,6},{5,7},{6,8},{7,9},{8,10},{9,11},{10,... | collective-permute-start | bytes 3145736 | tf_op jit(solution)/shard_map/Ha/ppermute | solution.py:76
  25.6 1.9 collective-permute-start.2
  27.5 0.0 copy-done.5
  27.6 0.3 dynamic-slice_reduce_fusion
  28.0 49.8 %all_to_all.20 = bf16[8,24,1024]{2,1,0:T(8,128)(2,1)} all-to-all(bf16[8,24,1024]{2,1,0:T(8,128)(2,1)S(1)} %broadcast_in_dim.2), channel_id=1, replica_groups={{0,8,16,24,256,264,272,280},{1,9,17,25,257,265,273,281},{32,40,48,56,28..., dimensions={0} | all-to-all | bytes 786432 | tf_op jit(solution)/shard_map/all_to_all | solution.py:407
  77.7 0.0 all-gather.4.cloned.1.call-update
  77.8 3.5 %shard_map.122 = (bf16[2,2,128,1024]{3,2,1,0:T(8,128)(2,1)}, bf16[2,2,128,512]{3,2,1,0:T(8,128)(2,1)}, bf16[2,2,128,512]{3,2,1,0:T(8,128)(2,1)}) custom-call(s32[2]{0:T(128)} %pad_add_fusion.meta, bf16[2,64,2048]{2,1,0:T(8,128)(2,1)} %refs_0_.4, bf16[2,64,2048]{2,1,0:T(8,128)(2,1)} %refs_1_.4, bf16[2,64,2048]{2,1,0:T(8,128)(2,1)} %refs_2_.3, ...), custom_call_target="tpu_custom_call" | custom-call | flops 1 | bytes 1 | tf_op jit(solution)/shard_map/pallas_call | solution.py:164
  81.2 4.9 %collective-permute-start.4 = (bf16[2,2,128,512]{3,2,1,0:T(8,128)(2,1)}, bf16[2,2,128,512]{3,2,1,0:T(8,128)(2,1)}, u32[]{:S(2)}, u32[]{:S(2)}) collective-permute-start(bf16[2,2,128,512]{3,2,1,0:T(8,128)(2,1)} %get-tuple-element.26.mid_tan), channel_id=1, source_target_pairs={{0,2},{1,3},{2,4},{3,5},{4,6},{5,7},{6,8},{7,9},{8,10},{9,11},{10,... | collective-permute-start | bytes 1572872 | tf_op jit(solution)/shard_map/T1a/ppermute | solution.py:76
  86.1 1.9 collective-permute-start.5
  88.1 6.0 %collective-permute-start.6 = (bf16[2,2,128,512]{3,2,1,0:T(8,128)(2,1)}, bf16[2,2,128,512]{3,2,1,0:T(8,128)(2,1)}, u32[]{:S(2)}, u32[]{:S(2)}) collective-permute-start(bf16[2,2,128,512]{3,2,1,0:T(8,128)(2,1)} %get-tuple-element.29.mid_tan), channel_id=1, source_target_pairs={{0,2},{1,3},{2,4},{3,5},{4,6},{5,7},{6,8},{7,9},{8,10},{9,11},{10,... | collective-permute-start | bytes 1572872 | tf_op jit(solution)/shard_map/T0a/ppermute | solution.py:76
  94.1 0.0 all-gather.6.cloned.1.call-done
  94.1 0.0 collective-permute-done.1.left
  94.2 0.0 copy-start.7
  94.2 1.9 collective-permute-start.7
  96.1 0.0 collective-permute-done.2.right
  96.1 1.9 collective-permute-start.3
  98.0 0.0 copy-done.7
  98.0 9.2 %shard_map.124 = (bf16[4,2,128,256]{3,2,1,0:T(8,128)(2,1)}, bf16[2,128,1024]{2,1,0:T(8,128)(2,1)}) custom-call(s32[2]{0:T(128)} %pad_add_fusion.meta, bf16[2,2,128,1024]{3,2,1,0:T(8,128)(2,1)} %get-tuple-element.20.q_ref, bf16[2,2,128,1024]{3,2,1,0:T(8,128)(2,1)} %copy-done.7, bf16[2,2,128,1024]{3,2,1,0:T(8,128)(2,1)} %shard_map.123.mid, ...), custom_call_target="tpu_custom_call" | custom-call | flops 137438953472 | bytes 1 | tf_op jit(solution)/shard_map/pallas_call | solution.py:221
  107.2 17.4 %all-to-all-start.1 = ((bf16[4,2,128,256]{3,2,1,0:T(8,128)(2,1)}), bf16[4,2,128,256]{3,2,1,0:T(8,128)(2,1)S(1)}, u32[]{:S(2)}, u32[]{:S(2)}) async-start(bf16[4,2,128,256]{3,2,1,0:T(8,128)(2,1)} %get-tuple-element.25), calls=%async_computation.1 | async-start | bytes 1048576 | tf_op jit(solution)/shard_map/all_to_all | solution.py:414
  124.6 0.0 collective-permute-done.4.left_tan
  124.6 0.0 collective-permute-done.5.right_tan
  124.6 8.3 %all-to-all-done.1.att = bf16[4,2,128,256]{3,2,1,0:T(8,128)(2,1)S(1)} async-done(((bf16[4,2,128,256]{3,2,1,0:T(8,128)(2,1)}), bf16[4,2,128,256]{3,2,1,0:T(8,128)(2,1)S(1)}, u32[]{:S(2)}, u32[]{:S(2)}) %all-to-all-start.1) | async-done | bytes 524320 | tf_op jit(solution)/shard_map/all_to_all | solution.py:414
  133.0 0.0 collective-permute-done.3.w_sib
  133.0 0.8 copy-done.1
  133.8 1.2 copy-done.2
  135.0 4.7 %shard_map.125 = bf16[8,2,96,256]{3,2,1,0:T(8,128)(2,1)} custom-call(bf16[4,1536,128]{2,1,0:T(8,128)(2,1)} %bitcast.22, bf16[4,1536,128]{2,1,0:T(8,128)(2,1)} %copy-done.2, bf16[4,2,128,256]{3,2,1,0:T(8,128)(2,1)} %copy-done.1), custom_call_target="tpu_custom_call" | custom-call | flops 1 | bytes 1 | tf_op jit(solution)/shard_map/pallas_call | solution.py:369
  139.6 3.5 %all-to-all-start.2 = ((bf16[8,2,96,256]{3,2,1,0:T(8,128)(2,1)}), bf16[8,2,96,256]{3,2,1,0:T(8,128)(2,1)S(1)}, u32[]{:S(2)}, u32[]{:S(2)}) async-start(bf16[8,2,96,256]{3,2,1,0:T(8,128)(2,1)} %shard_map.125), calls=%async_computation.2 | async-start | bytes 1572864 | tf_op jit(solution)/shard_map/all_to_all | solution.py:417
  143.2 0.0 collective-permute-done.6.left_tan
  143.2 0.0 collective-permute-done.7.right_tan
  143.2 7.0 %shard_map.126.tan = bf16[2,128,512]{2,1,0:T(8,128)(2,1)} custom-call(s32[2]{0:T(128)} %pad_add_fusion.meta, bf16[2,2,128,1024]{3,2,1,0:T(8,128)(2,1)} %get-tuple-element.20.q_ref, bf16[2,2,128,1024]{3,2,1,0:T(8,128)(2,1)} %copy-done.7, bf16[2,2,128,1024]{3,2,1,0:T(8,128)(2,1)} %shard_map.123.mid, bf16[2,2,128,1024]{3,2,1,0:T(8,128)(2,1)} %collective-permute-done.2.right, ...), custom_call_target="tpu_custom_call" | custom-call | flops 8589934592 | bytes 1 | tf_op jit(solution)/shard_map/pallas_call | solution.py:267
  150.2 7.0 %shard_map.128.tan = bf16[2,128,512]{2,1,0:T(8,128)(2,1)} custom-call(s32[2]{0:T(128)} %pad_add_fusion.meta, bf16[2,2,128,1024]{3,2,1,0:T(8,128)(2,1)} %get-tuple-element.20.q_ref, bf16[2,2,128,1024]{3,2,1,0:T(8,128)(2,1)} %copy-done.7, bf16[2,2,128,1024]{3,2,1,0:T(8,128)(2,1)} %shard_map.123.mid, bf16[2,2,128,1024]{3,2,1,0:T(8,128)(2,1)} %collective-permute-done.2.right, ...), custom_call_target="tpu_custom_call" | custom-call | flops 8589934592 | bytes 1 | tf_op jit(solution)/shard_map/pallas_call | solution.py:267
  157.1 9.2 %all-to-all-done.2 = bf16[8,2,96,256]{3,2,1,0:T(8,128)(2,1)S(1)} async-done(((bf16[8,2,96,256]{3,2,1,0:T(8,128)(2,1)}), bf16[8,2,96,256]{3,2,1,0:T(8,128)(2,1)S(1)}, u32[]{:S(2)}, u32[]{:S(2)}) %all-to-all-start.2) | async-done | bytes 786464 | tf_op jit(solution)/shard_map/all_to_all | solution.py:417
  166.4 0.8 convert_reduce_fusion
  167.1 26.4 %all-to-all-start.3 = ((f32[8,24,256]{2,1,0:T(8,128)}), f32[8,24,256]{2,1,0:T(8,128)S(1)}, u32[]{:S(2)}, u32[]{:S(2)}) async-start(f32[8,24,256]{2,1,0:T(8,128)} %bitcast.7), calls=%async_computation.3 | async-start | bytes 393216 | tf_op jit(solution)/shard_map/all_to_all | solution.py:420
  193.5 5.5 %shard_map.127 = (f32[2,2,64,1536]{3,2,1,0:T(8,128)}, f32[2,2,64,1536]{3,2,1,0:T(8,128)}) custom-call(bf16[2,128,1024]{2,1,0:T(8,128)(2,1)} %get-tuple-element.28.att, bf16[2,128,512]{2,1,0:T(8,128)(2,1)} %shard_map.126.tan, bf16[1536,1024]{1,0:T(8,128)(2,1)} %bitcast.29, f32[2,1536]{1,0:T(2,128)} %gate.3, f32[2,1536]{1,0:T(2,128)} %gate_tan.1), custom_call_target="tpu_custom_call" | custom-call | flops 8589934592 | bytes 1 | tf_op jit(solution)/shard_map/pallas_call | solution.py:313
  199.0 1.9 collective-permute-start.8
  200.9 0.0 all-to-all-done.3
  201.0 0.0 copy-start.3
  201.0 4.2 %shard_map.129 = (f32[1,2,64,1536]{3,2,1,0:T(8,128)}, f32[1,2,64,1536]{3,2,1,0:T(8,128)}) custom-call(bf16[2,128,512]{2,1,0:T(8,128)(2,1)} %shard_map.128.tan, bf16[1536,1024]{1,0:T(8,128)(2,1)} %bitcast.30, f32[2,1536]{1,0:T(2,128)} %gate.3), custom_call_target="tpu_custom_call" | custom-call | flops 8589934592 | bytes 1 | tf_op jit(solution)/shard_map/pallas_call | solution.py:335
  205.1 2.4 %collective-permute-start.9 = (f32[1,2,64,1536]{3,2,1,0:T(8,128)}, f32[1,2,64,1536]{3,2,1,0:T(8,128)S(1)}, u32[]{:S(2)}, u32[]{:S(2)}) collective-permute-start(f32[1,2,64,1536]{3,2,1,0:T(8,128)} %get-tuple-element.36), channel_id=1, source_target_pairs={{0,1},{1,0},{2,3},{3,2},{4,5},{5,4},{6,7},{7,6},{8,9},{9,8},{10,11... | collective-permute-start | bytes 2359304 | tf_op jit(solution)/shard_map/Uswap/ppermute | solution.py:76
  207.5 2.4 %collective-permute-start.10 = (f32[24,256]{1,0:T(8,128)S(1)}, f32[24,256]{1,0:T(8,128)S(1)}, u32[]{:S(2)}, u32[]{:S(2)}) collective-permute-start(f32[24,256]{1,0:T(8,128)S(1)} %reduce_sum.19), channel_id=1, source_target_pairs={{0,0},{1,1},{2,8},{3,9},{4,16},{5,17},{6,24},{7,25},{8,2},{9,3},{1... | collective-permute-start | bytes 73736 | tf_op jit(solution)/shard_map/Turn/ppermute | solution.py:76
  210.0 9.6 %collective-permute-done.10 = f32[24,256]{1,0:T(8,128)S(1)} collective-permute-done((f32[24,256]{1,0:T(8,128)S(1)}, f32[24,256]{1,0:T(8,128)S(1)}, u32[]{:S(2)}, u32[]{:S(2)}) %collective-permute-start.10) | collective-permute-done | bytes 24608 | tf_op jit(solution)/shard_map/Turn/ppermute | solution.py:76
  219.6 0.0 collective-permute-done.9
  219.6 0.0 collective-permute-done.8
  219.6 0.0 copy-done.3
  219.6 2.3 %fusion.4 = (bf16[2,64,1536]{2,1,0:T(8,128)(2,1)}, bf16[2,64,1536]{2,1,0:T(8,128)(2,1)}) fusion(f32[1,2,64,1536]{3,2,1,0:T(8,128)} %get-tuple-element.35, f32[1,2,64,1536]{3,2,1,0:T(8,128)S(1)} %collective-permute-done.9, f32[2,2,64,1536]{3,2,1,0:T(8,128)S(1)} %collective-permute-done.8, f32[2,2,64,1536]{3,2,1,0:T(8,128)S(1)} %copy-done.3), kind=kLoop, calls=%fused_computation.8 | loop fusion | flops 1179648 | bytes 5505024 | tf_op jit(solution)/shard_map/convert_element_type | solution.py:433
  221.9 0.6 copy.21
  (8 shorter events, 0.1 us)
Async XLA Ops:
  7.2 87.0 %all-gather.6.cloned.1.call-start = ((), (), s32[]{:S(2)}) async-start(), calls=%async_computation.5 | async-start | bytes 1966080 | tf_op jit(solution)/shard_map/all_gather | solution.py:400
  7.8 8.8 %copy-start.4 = (bf16[2,64,1536]{2,1,0:T(8,128)(2,1)S(1)}, bf16[2,64,1536]{2,1,0:T(8,128)(2,1)}, u32[]{:S(2)}) copy-start(bf16[2,64,1536]{2,1,0:T(8,128)(2,1)} %param.19) | copy-start | bytes 1179652
  7.8 8.8 %copy-start.6 = (f32[2,1536]{1,0:T(2,128)S(1)}, f32[2,1536]{1,0:T(2,128)}, u32[]{:S(2)}) copy-start(f32[2,1536]{1,0:T(2,128)} %gate.3) | copy-start | bytes 36868
  11.1 5.5 %collective-permute-start = (bf16[6,2,64,1024]{3,2,1,0:T(8,128)(2,1)}, bf16[6,2,64,1024]{3,2,1,0:T(8,128)(2,1)S(1)}, u32[]{:S(2)}, u32[]{:S(2)}) collective-permute-start(bf16[6,2,64,1024]{3,2,1,0:T(8,128)(2,1)} %shard_map.121), channel_id=1, source_target_pairs={{0,1},{1,0},{2,3},{3,2},{4,5},{5,4},{6,7},{7,6},{8,9},{9,8},{10,11... | collective-permute-start | bytes 4718600 | tf_op jit(solution)/shard_map/Sx/ppermute | solution.py:76
  16.6 1.3 copy-start
  17.9 9.7 %copy-start.5 = (f32[2048,24]{0,1:T(8,128)S(1)}, f32[2048,24]{0,1:T(8,128)}, u32[]{:S(2)}) copy-start(f32[2048,24]{0,1:T(8,128)} %param.16) | copy-start | bytes 589828
  17.9 175.7 %all-gather.4.cloned.1.call-start = ((), (), s32[]{:S(2)}) async-start(), calls=%async_computation.4 | async-start | bytes 3538944 | tf_op jit(solution)/shard_map/all_gather | solution.py:409
  20.8 73.4 %collective-permute-start.1 = (bf16[2,2,128,1024]{3,2,1,0:T(8,128)(2,1)}, bf16[2,2,128,1024]{3,2,1,0:T(8,128)(2,1)S(1)}, u32[]{:S(2)}, u32[]{:S(2)}) collective-permute-start(bf16[2,2,128,1024]{3,2,1,0:T(8,128)(2,1)} %shard_map.123.mid), channel_id=1, source_target_pairs={{0,2},{1,3},{2,4},{3,5},{4,6},{5,7},{6,8},{7,9},{8,10},{9,11},{10,... | collective-permute-start | bytes 3145736 | tf_op jit(solution)/shard_map/Ha/ppermute | solution.py:76
  25.6 70.5 %collective-permute-start.2 = (bf16[2,2,128,1024]{3,2,1,0:T(8,128)(2,1)}, bf16[2,2,128,1024]{3,2,1,0:T(8,128)(2,1)}, u32[]{:S(2)}, u32[]{:S(2)}) collective-permute-start(bf16[2,2,128,1024]{3,2,1,0:T(8,128)(2,1)} %shard_map.123.mid), channel_id=1, source_target_pairs={{2,0},{3,1},{4,2},{5,3},{6,4},{7,5},{8,6},{9,7},{10,8},{11,9},{12,... | collective-permute-start | bytes 3145736 | tf_op jit(solution)/shard_map/Hb/ppermute | solution.py:76
  81.2 43.4 %collective-permute-start.4 = (bf16[2,2,128,512]{3,2,1,0:T(8,128)(2,1)}, bf16[2,2,128,512]{3,2,1,0:T(8,128)(2,1)}, u32[]{:S(2)}, u32[]{:S(2)}) collective-permute-start(bf16[2,2,128,512]{3,2,1,0:T(8,128)(2,1)} %get-tuple-element.26.mid_tan), channel_id=1, source_target_pairs={{0,2},{1,3},{2,4},{3,5},{4,6},{5,7},{6,8},{7,9},{8,10},{9,11},{10,... | collective-permute-start | bytes 1572872 | tf_op jit(solution)/shard_map/T1a/ppermute | solution.py:76
  86.1 38.5 %collective-permute-start.5 = (bf16[2,2,128,512]{3,2,1,0:T(8,128)(2,1)}, bf16[2,2,128,512]{3,2,1,0:T(8,128)(2,1)}, u32[]{:S(2)}, u32[]{:S(2)}) collective-permute-start(bf16[2,2,128,512]{3,2,1,0:T(8,128)(2,1)} %get-tuple-element.26.mid_tan), channel_id=1, source_target_pairs={{2,0},{3,1},{4,2},{5,3},{6,4},{7,5},{8,6},{9,7},{10,8},{11,9},{12,... | collective-permute-start | bytes 1572872 | tf_op jit(solution)/shard_map/T1b/ppermute | solution.py:76
  88.1 55.1 %collective-permute-start.6 = (bf16[2,2,128,512]{3,2,1,0:T(8,128)(2,1)}, bf16[2,2,128,512]{3,2,1,0:T(8,128)(2,1)}, u32[]{:S(2)}, u32[]{:S(2)}) collective-permute-start(bf16[2,2,128,512]{3,2,1,0:T(8,128)(2,1)} %get-tuple-element.29.mid_tan), channel_id=1, source_target_pairs={{0,2},{1,3},{2,4},{3,5},{4,6},{5,7},{6,8},{7,9},{8,10},{9,11},{10,... | collective-permute-start | bytes 1572872 | tf_op jit(solution)/shard_map/T0a/ppermute | solution.py:76
  94.2 3.9 %copy-start.7 = (bf16[2,2,128,1024]{3,2,1,0:T(8,128)(2,1)}, bf16[2,2,128,1024]{3,2,1,0:T(8,128)(2,1)S(1)}, u32[]{:S(2)}) copy-start(bf16[2,2,128,1024]{3,2,1,0:T(8,128)(2,1)S(1)} %collective-permute-done.1.left) | copy-start | bytes 3145732
  94.2 49.0 %collective-permute-start.7 = (bf16[2,2,128,512]{3,2,1,0:T(8,128)(2,1)}, bf16[2,2,128,512]{3,2,1,0:T(8,128)(2,1)}, u32[]{:S(2)}, u32[]{:S(2)}) collective-permute-start(bf16[2,2,128,512]{3,2,1,0:T(8,128)(2,1)} %get-tuple-element.29.mid_tan), channel_id=1, source_target_pairs={{2,0},{3,1},{4,2},{5,3},{6,4},{7,5},{8,6},{9,7},{10,8},{11,9},{12,... | collective-permute-start | bytes 1572872 | tf_op jit(solution)/shard_map/T0b/ppermute | solution.py:76
  96.1 36.9 %collective-permute-start.3 = (bf16[4,1536,128]{2,1,0:T(8,128)(2,1)}, bf16[4,1536,128]{2,1,0:T(8,128)(2,1)S(1)}, u32[]{:S(2)}, u32[]{:S(2)}) collective-permute-start(bf16[4,1536,128]{2,1,0:T(8,128)(2,1)} %bitcast.21), channel_id=1, source_target_pairs={{0,1},{1,0},{2,3},{3,2},{4,5},{5,4},{6,7},{7,6},{8,9},{9,8},{10,11... | collective-permute-start | bytes 4718600 | tf_op jit(solution)/shard_map/Cswap/ppermute | solution.py:76
  107.2 25.8 %all-to-all-start.1 = ((bf16[4,2,128,256]{3,2,1,0:T(8,128)(2,1)}), bf16[4,2,128,256]{3,2,1,0:T(8,128)(2,1)S(1)}, u32[]{:S(2)}, u32[]{:S(2)}) async-start(bf16[4,2,128,256]{3,2,1,0:T(8,128)(2,1)} %get-tuple-element.25), calls=%async_computation.1 | async-start | bytes 1048576 | tf_op jit(solution)/shard_map/all_to_all | solution.py:414
  133.0 0.8 copy-start.1
  133.8 1.2 copy-start.2
  139.6 26.7 %all-to-all-start.2 = ((bf16[8,2,96,256]{3,2,1,0:T(8,128)(2,1)}), bf16[8,2,96,256]{3,2,1,0:T(8,128)(2,1)S(1)}, u32[]{:S(2)}, u32[]{:S(2)}) async-start(bf16[8,2,96,256]{3,2,1,0:T(8,128)(2,1)} %shard_map.125), calls=%async_computation.2 | async-start | bytes 1572864 | tf_op jit(solution)/shard_map/all_to_all | solution.py:417
  167.1 33.8 %all-to-all-start.3 = ((f32[8,24,256]{2,1,0:T(8,128)}), f32[8,24,256]{2,1,0:T(8,128)S(1)}, u32[]{:S(2)}, u32[]{:S(2)}) async-start(f32[8,24,256]{2,1,0:T(8,128)} %bitcast.7), calls=%async_computation.3 | async-start | bytes 393216 | tf_op jit(solution)/shard_map/all_to_all | solution.py:420
  199.0 20.6 %collective-permute-start.8 = (f32[2,2,64,1536]{3,2,1,0:T(8,128)}, f32[2,2,64,1536]{3,2,1,0:T(8,128)S(1)}, u32[]{:S(2)}, u32[]{:S(2)}) collective-permute-start(f32[2,2,64,1536]{3,2,1,0:T(8,128)} %get-tuple-element.31), channel_id=1, source_target_pairs={{0,1},{1,0},{2,3},{3,2},{4,5},{5,4},{6,7},{7,6},{8,9},{9,8},{10,11... | collective-permute-start | bytes 4718600 | tf_op jit(solution)/shard_map/Pswap/ppermute | solution.py:76
  201.0 18.6 %copy-start.3 = (f32[2,2,64,1536]{3,2,1,0:T(8,128)S(1)}, f32[2,2,64,1536]{3,2,1,0:T(8,128)}, u32[]{:S(2)}) copy-start(f32[2,2,64,1536]{3,2,1,0:T(8,128)} %get-tuple-element.30) | copy-start | bytes 4718596
  205.1 14.4 %collective-permute-start.9 = (f32[1,2,64,1536]{3,2,1,0:T(8,128)}, f32[1,2,64,1536]{3,2,1,0:T(8,128)S(1)}, u32[]{:S(2)}, u32[]{:S(2)}) collective-permute-start(f32[1,2,64,1536]{3,2,1,0:T(8,128)} %get-tuple-element.36), channel_id=1, source_target_pairs={{0,1},{1,0},{2,3},{3,2},{4,5},{5,4},{6,7},{7,6},{8,9},{9,8},{10,11... | collective-permute-start | bytes 2359304 | tf_op jit(solution)/shard_map/Uswap/ppermute | solution.py:76
  207.5 12.0 %collective-permute-start.10 = (f32[24,256]{1,0:T(8,128)S(1)}, f32[24,256]{1,0:T(8,128)S(1)}, u32[]{:S(2)}, u32[]{:S(2)}) collective-permute-start(f32[24,256]{1,0:T(8,128)S(1)} %reduce_sum.19), channel_id=1, source_target_pairs={{0,0},{1,1},{2,8},{3,9},{4,16},{5,17},{6,24},{7,25},{8,2},{9,3},{1... | collective-permute-start | bytes 73736 | tf_op jit(solution)/shard_map/Turn/ppermute | solution.py:76
Sparse Core Ops, SparseCore 0:
  18.0 35.0 all-gather.5
  77.9 54.2 all-gather.3

commit v4 on v2

--- a/solution.py
+++ b/solution.py
@@ -15,6 +15,7 @@
 GROUP = NJ * PAIR
 PIECES = ((0, 2), (2, 4))
 SCALE = HD ** (-0.5)
+LOG2E = 1.4426950408889634
 BF = jnp.bfloat16
 F32 = jnp.float32
 
@@ -60,10 +61,6 @@
     [device_of(x, yl, yh, z, c) for z in range(NZ)]
     for yl in range(NYL) for yh in range(NYH) for x in range(NX) for c in range(NC)
 ]
-GROUPS_ZYL = [
-    [device_of(x, yl, yh, z, c) for yl in range(NYL) for z in range(NZ)]
-    for yh in range(NYH) for x in range(NX) for c in range(NC)
-]
 GROUPS_Y = [
     [device_of(x, yl, yh, z, c) for yl in range(NYL) for yh in range(NYH)]
     for z in range(NZ) for x in range(NX) for c in range(NC)
@@ -97,7 +94,7 @@
 
 def params(*semantics):
     return pltpu.CompilerParams(
-        vmem_limit_bytes=50 * 2**20, dimension_semantics=semantics or None
+        vmem_limit_bytes=60 * 2**20, dimension_semantics=semantics or None
     )
 
 
@@ -108,10 +105,10 @@
 COSTS = dict(
     split=cost(1, 1),
     join=cost(1, 1),
-    attend=cost(2**35, 1),
+    attend=cost(2**37, 1),
     tangent=cost(2**33, 1),
-    project=cost(1, 1),
-    finish=cost(1, 1),
+    project=cost(2**33, 1),
+    finish=cost(2**33, 1),
     grad=cost(1, 1),
 )
 
@@ -173,7 +170,7 @@
     )(meta, *arrays, got)
 
 
-def allowed_keys(meta):
+def key_bias(meta):
     core, chunk = meta[0], meta[1]
     span = 2 * 64
     shape = (span, 3 * span)
@@ -183,15 +180,15 @@
     k_pos = (cols + 64 * core) & (span - 1)
     block = cols >> 7
     before = (block == 0) & (k_pos >= q_pos) & (chunk > 0)
-    after = (block == 2) & (k_pos <= q_pos) & (chunk < COUNT // NC - 1)
-    return before | (block == 1) | after
-
-
-def probs_of(q, k, mask):
-    scores = jnp.where(mask, nt(q, k) * SCALE, -1e30)
+    behind = (block == 2) & (k_pos <= q_pos) & (chunk < COUNT // NC - 1)
+    return jnp.where(before | (block == 1) | behind, 0.0, -1e30)
+
+
+def probs_of(scores, bias):
+    scores = scores + bias
     top = jnp.max(scores, axis=-1, keepdims=True)
-    terms = jnp.exp(scores - top)
-    return terms / jnp.sum(terms, axis=-1, keepdims=True)
+    terms = jnp.exp2((scores - top) * (SCALE * LOG2E))
+    return terms * (1.0 / jnp.sum(terms, axis=-1, keepdims=True))
 
 
 def rows_of(refs, a, cols):
@@ -199,12 +196,12 @@
 
 
 def attend_body(meta, q_ref, left, mid, right, quarter, wide):
-    mask = allowed_keys(meta)
+    bias = key_bias(meta)
     keyed = (left, mid, right)
     for n in range(GROUP // HD):
         cols = slice(n * HD, (n + 1) * HD)
-        probs = probs_of(q_ref[0, 0, :, cols], rows_of(keyed, 0, cols), mask).astype(BF)
-        att = nn(probs, rows_of(keyed, 1, cols)).astype(BF)
+        probs = probs_of(nt(q_ref[0, 0, :, cols], rows_of(keyed, 0, cols)), bias)
+        att = nn(probs.astype(BF), rows_of(keyed, 1, cols)).astype(BF)
         quarter[n // 2, 0, :, (n % 2) * HD : (n % 2 + 1) * HD] = att
         wide[0, :, cols] = att
 
@@ -233,19 +230,22 @@
 
 
 def tangent_body(meta, q_ref, left, mid, right, left_tan, mid_tan, right_tan, wide):
-    mask = allowed_keys(meta)
+    bias = key_bias(meta)
     keyed, keyed_tan = (left, mid, right), (left_tan, mid_tan, right_tan)
+    rows = q_ref.shape[2]
     for n in range(wide.shape[2] // HD):
         cols = slice(n * HD, (n + 1) * HD)
         q, qt = q_ref[0, 0, :, cols], q_ref[1, 0, :, cols]
-        k = rows_of(keyed, 0, cols)
-        probs = probs_of(q, k, mask)
-        tan = (nt(qt, k) + nt(q, rows_of(keyed_tan, 0, cols))) * SCALE
+        both = nt(jnp.concatenate([q, qt], axis=0), rows_of(keyed, 0, cols))
+        probs = probs_of(both[:rows], bias)
+        tan = (both[rows:] + nt(q, rows_of(keyed_tan, 0, cols))) * SCALE
         probs_tan = probs * (tan - jnp.sum(probs * tan, axis=-1, keepdims=True))
-        att = nn(probs_tan.astype(BF), rows_of(keyed, 1, cols)) + nn(
-            probs.astype(BF), rows_of(keyed_tan, 1, cols)
+        left_side = jnp.concatenate([probs.astype(BF), probs_tan.astype(BF)], axis=0)
+        right_side = jnp.concatenate(
+            [rows_of(keyed_tan, 1, cols), rows_of(keyed, 1, cols)], axis=1
         )
-        wide[0, :, cols] = att.astype(BF)
+        both = nn(left_side, right_side)
+        wide[0, :, cols] = (both[:rows, :HD] + both[rows:, HD:]).astype(BF)
 
 
 def attend_tangent(meta, q_rows, keyed, keyed_tan, piece):
@@ -366,17 +366,28 @@
     )(w_own, w_sib, att)
 
 
+def in_order(mine, other, bit):
+    return jnp.where(
+        bit == 0, jnp.concatenate([mine, other]), jnp.concatenate([other, mine])
+    )
+
+
 def on_device(
     queries, keys, values, query_tan, key_tan, value_tan, weight_out, gate, gate_tan, cotangent
 ):
     seq_at, uly_at = lax.axis_index("seq"), lax.axis_index("uly")
     core = uly_at % NC
+    yl_at = seq_at // (NX * NZ)
     chunk = seq_at * NYH + uly_at // NC
     meta = jnp.stack([core, chunk]).astype(jnp.int32)
     seqs, rows, _ = queries.shape
 
     arrays = (keys, values, queries, query_tan, key_tan, value_tan)
     got = send(split_groups(meta, arrays), SWAP_CORE, "Sx")
+    low = weight_out.astype(BF).reshape(NJ, NC, PAIR, -1)
+    low = lax.dynamic_index_in_dim(low, core, 1, keepdims=False).reshape(GROUP, -1).T
+    low = in_order(low[None], send(low[None], SWAP_YLO, "Wy"), yl_at)
+    got, low = after((got, low))
     (kv,) = join_rows(meta, arrays[:2], got, (((0, 1), (0, NJ)),), 0)
     keyed = (send(kv, TO_NEXT, "Ha"), kv, send(kv, TO_PREV, "Hb"))
     q_rows, *tans = join_rows(
@@ -384,33 +395,34 @@
     )
     tans = [[send(t, TO_NEXT, "T%da" % n), t, send(t, TO_PREV, "T%db" % n)] for n, t in enumerate(tans)]
 
+    cotangent, _ = after((cotangent, got))
     weighted = (gate[:, None, :] * cotangent.astype(F32)).astype(BF)
     weighted = weighted.reshape(seqs * rows, -1).T
     w_own = lax.all_gather(weighted, AXES, axis_index_groups=GROUPS_X)
     w_own, _ = after((w_own, kv))
     w_sib = send(w_own, SWAP_CORE, "Cswap")
 
-    low = weight_out.astype(BF).reshape(NJ, NC, PAIR, -1)
-    low = lax.dynamic_index_in_dim(low, core, 1, keepdims=False).reshape(GROUP, -1).T
-    low = jnp.broadcast_to(low[None], (NYL * NZ,) + low.shape)
-    low = lax.all_to_all(low, AXES, 0, 0, axis_index_groups=GROUPS_ZYL, tiled=True)
-    weight = lax.all_gather(low, AXES, axis_index_groups=GROUPS_X, axis=1, tiled=True)
+    low = lax.all_gather(low, AXES, axis_index_groups=GROUPS_X, axis=1, tiled=True)
+    weight = lax.all_gather(low, AXES, axis_index_groups=GROUPS_Z, axis=1, tiled=True)
     weight = weight.reshape(-1, GROUP)
 
     quarter, att = attend(meta, q_rows, keyed)
-    quarter, _ = after((quarter, low))
     quarter = lax.all_to_all(quarter, AXES, 0, 0, axis_index_groups=GROUPS_X, tiled=True)
-    (quarter, tans[0][0], tans[0][2]) = after((quarter, tans[0][0], tans[0][2]))
+    (quarter, tans[1][0], tans[1][2]) = after((quarter, tans[1][0], tans[1][2]))
     terms = grad_terms(w_own, w_sib, quarter)
     terms = lax.all_to_all(terms, AXES, 0, 0, axis_index_groups=GROUPS_Z, tiled=True)
     terms = jnp.sum(terms.astype(F32), axis=0).reshape(NYL * NYH, -1, PAIR)
+    summed = terms
     terms = lax.all_to_all(terms, AXES, 0, 0, axis_index_groups=GROUPS_Y, tiled=True)
-    weight_grad = send(jnp.sum(terms, axis=0), TURN, "Turn").T
+    terms = jnp.sum(terms, axis=0)
+    weight_grad = send(terms, TURN, "Turn").T
 
     tan_first = attend_tangent(meta, q_rows, keyed, tans[0], 0)
+    att, _ = after((att, summed))
     here, other = project(att, tan_first, weight, gate, gate_tan)
     other = send(other, SWAP_CORE, "Pswap")
     tan_last = attend_tangent(meta, q_rows, keyed, tans[1], 1)
+    tan_last, _ = after((tan_last, terms))
     rest, rest_other = finish(tan_last, weight, gate)
     rest_other = send(rest_other, SWAP_CORE, "Uswap")
     mixed = (here[0] + other[0]).astype(BF)

time: 214 us -> 217 us (1.014)
  the two profiles are of different devices: /device:TPU:30 before, /device:TPU:96 now
where the time goes in v4:
time: 217 us
  waiting for transfers between devices  67.9 us (31%)
  starting transfers between devices  65.7 us (30%)
  Pallas kernels  45.3 us (21%)
  blocking collectives  15.3 us (7%)
  between operations  14.3 us (7%)
  local copies, waits for them, and re-layouts  4.18 us (2%)
  other arithmetic  3.88 us (2%)
    ppermute x12, waiting for transfers between devices, send(): return lax.ppermute(array, AXES, pairs)  39.4 us
    ppermute x12, starting transfers between devices, send(): return lax.ppermute(array, AXES, pairs)  32.3 us
    all_to_all x1, starting transfers between devices, on_device(): lax.all_to_all(terms, AXES, 0, 0, axis_index_groups=GROUPS_Y, tiled=True)  19.2 us
    all_to_all x1, waiting for transfers between devices, on_device(): lax.all_to_all(terms, AXES, 0, 0, axis_index_groups=GROUPS_Z, tiled=True)  18.3 us
    all_gather x1, blocking collectives, on_device(): lax.all_gather(low, AXES, axis_index_groups=GROUPS_X, axis=1, tiled=True)  15.3 us
    pallas_call x2, Pallas kernels, attend_tangent(): pl.pallas_call(tangent_body, out_shape=jax.ShapeDtypeStruct((seqs, rows,...  12.5 us
    all_to_all x1, waiting for transfers between devices, on_device(): lax.all_to_all(quarter, AXES, 0, 0, axis_index_groups=GROUPS_X, tiled=True)  10.1 us
    all_to_all x1, starting transfers between devices, on_device(): lax.all_to_all(terms, AXES, 0, 0, axis_index_groups=GROUPS_Z, tiled=True)  9.95 us
  transfers between devices with their start and end apart: 17, of which 6 were waited for; matrix products, arithmetic and copies ran while one was open for 1% of the time, Pallas kernels for 19%

profile of v4, /device:TPU:96, one launch (start us, length us, event | category | flops | bytes accessed | tf_op | source)
XLA Modules:
  0.0 216.5 jit_solution(13546740914099913903)
XLA Ops:
  7.2 0.0 all-gather.6.cloned.1.call-start
  7.2 0.7 pad_add_fusion.meta
  7.9 0.0 copy-start.5
  7.9 0.0 copy-start.4
  7.9 3.3 %shard_map.121 = bf16[6,2,64,1024]{3,2,1,0:T(8,128)(2,1)} custom-call(s32[2]{0:T(128)} %pad_add_fusion.meta, bf16[2,64,2048]{2,1,0:T(8,128)(2,1)} %refs_0_.5, bf16[2,64,2048]{2,1,0:T(8,128)(2,1)} %refs_1_.5, bf16[2,64,2048]{2,1,0:T(8,128)(2,1)} %refs_0_.4, bf16[2,64,2048]{2,1,0:T(8,128)(2,1)} %refs_1_.4, bf16[2,64,2048]{2,1,0:T(8,128)(2,1)} %refs_2_.3, ...), custom_call_target="tpu_custom_call" | custom-call | flops 1 | bytes 1 | tf_op jit(solution)/shard_map/pallas_call | solution.py:132
  11.2 1.9 collective-permute-start
  13.1 0.0 copy-done.5
  13.2 0.3 dynamic-slice_reduce_fusion
  13.5 2.6 %collective-permute-start.1 = (bf16[1,24,1024]{2,1,0:T(8,128)(2,1)S(1)}, bf16[1,24,1024]{2,1,0:T(8,128)(2,1)S(1)}, u32[]{:S(2)}, u32[]{:S(2)}) collective-permute-start(bf16[1,24,1024]{2,1,0:T(8,128)(2,1)S(1)} %bitcast.26), channel_id=1, source_target_pairs={{0,256},{1,257},{2,258},{3,259},{4,260},{5,261},{6,262},{7,263},{8... | collective-permute-start | bytes 147464 | tf_op jit(solution)/shard_map/Wy/ppermute | solution.py:72
  16.1 3.4 %collective-permute-done.1 = bf16[1,24,1024]{2,1,0:T(8,128)(2,1)S(1)} collective-permute-done((bf16[1,24,1024]{2,1,0:T(8,128)(2,1)S(1)}, bf16[1,24,1024]{2,1,0:T(8,128)(2,1)S(1)}, u32[]{:S(2)}, u32[]{:S(2)}) %collective-permute-start.1) | collective-permute-done | bytes 49184 | tf_op jit(solution)/shard_map/Wy/ppermute | solution.py:72
  19.6 0.0 collective-permute-done.refs_4_.refs_2_
  19.6 0.0 copy-done.4
  19.6 0.0 copy-done.6
  19.6 0.0 copy-start
  19.6 0.1 multiply_convert_fusion
  19.7 1.2 copy.17
  20.9 0.0 all-gather.6.cloned.1.call-update
  20.9 0.0 all-gather.4.cloned.1.call-start
  20.9 0.0 copy-done
  21.0 2.8 %shard_map.123.mid = bf16[2,2,128,1024]{3,2,1,0:T(8,128)(2,1)} custom-call(s32[2]{0:T(128)} %pad_add_fusion.meta, bf16[2,64,2048]{2,1,0:T(8,128)(2,1)} %refs_0_.5, bf16[2,64,2048]{2,1,0:T(8,128)(2,1)} %refs_1_.5, bf16[6,2,64,1024]{3,2,1,0:T(8,128)(2,1)} %copy-done), custom_call_target="tpu_custom_call" | custom-call | flops 1 | bytes 1 | tf_op jit(solution)/shard_map/pallas_call | solution.py:160
  23.8 2.7 %collective-permute-start.2 = (bf16[2,2,128,1024]{3,2,1,0:T(8,128)(2,1)}, bf16[2,2,128,1024]{3,2,1,0:T(8,128)(2,1)S(1)}, u32[]{:S(2)}, u32[]{:S(2)}) collective-permute-start(bf16[2,2,128,1024]{3,2,1,0:T(8,128)(2,1)} %shard_map.123.mid), channel_id=1, source_target_pairs={{0,2},{1,3},{2,4},{3,5},{4,6},{5,7},{6,8},{7,9},{8,10},{9,11},{10,... | collective-permute-start | bytes 3145736 | tf_op jit(solution)/shard_map/Ha/ppermute | solution.py:72
  26.5 5.3 %collective-permute-start.3 = (bf16[2,2,128,1024]{3,2,1,0:T(8,128)(2,1)}, bf16[2,2,128,1024]{3,2,1,0:T(8,128)(2,1)}, u32[]{:S(2)}, u32[]{:S(2)}) collective-permute-start(bf16[2,2,128,1024]{3,2,1,0:T(8,128)(2,1)} %shard_map.123.mid), channel_id=1, source_target_pairs={{2,0},{3,1},{4,2},{5,3},{6,4},{7,5},{8,6},{9,7},{10,8},{11,9},{12,... | collective-permute-start | bytes 3145736 | tf_op jit(solution)/shard_map/Hb/ppermute | solution.py:72
  31.7 3.5 %shard_map.122 = (bf16[2,2,128,1024]{3,2,1,0:T(8,128)(2,1)}, bf16[2,2,128,512]{3,2,1,0:T(8,128)(2,1)}, bf16[2,2,128,512]{3,2,1,0:T(8,128)(2,1)}) custom-call(s32[2]{0:T(128)} %pad_add_fusion.meta, bf16[2,64,2048]{2,1,0:T(8,128)(2,1)} %refs_0_.4, bf16[2,64,2048]{2,1,0:T(8,128)(2,1)} %refs_1_.4, bf16[2,64,2048]{2,1,0:T(8,128)(2,1)} %refs_2_.3, ...), custom_call_target="tpu_custom_call" | custom-call | flops 1 | bytes 1 | tf_op jit(solution)/shard_map/pallas_call | solution.py:160
  35.2 1.9 collective-permute-start.5
  37.1 6.0 %collective-permute-start.6 = (bf16[2,2,128,512]{3,2,1,0:T(8,128)(2,1)}, bf16[2,2,128,512]{3,2,1,0:T(8,128)(2,1)}, u32[]{:S(2)}, u32[]{:S(2)}) collective-permute-start(bf16[2,2,128,512]{3,2,1,0:T(8,128)(2,1)} %get-tuple-element.27.mid_tan), channel_id=1, source_target_pairs={{2,0},{3,1},{4,2},{5,3},{6,4},{7,5},{8,6},{9,7},{10,8},{11,9},{12,... | collective-permute-start | bytes 1572872 | tf_op jit(solution)/shard_map/T1b/ppermute | solution.py:72
  43.2 1.9 collective-permute-start.7
  45.1 15.3 %all_gather.14 = bf16[2,96,1024]{2,1,0:T(8,128)(2,1)} all-gather(bf16[2,24,1024]{2,1,0:T(8,128)(2,1)S(1)} %maximum_select_fusion), channel_id=1, replica_groups={{0,8,16,24},{1,9,17,25},{32,40,48,56},{33,41,49,57},{64,72,80,88},{65,7..., dimensions={1}, use_global_device_ids=true | all-gather | bytes 491520 | tf_op jit(solution)/shard_map/all_gather | solution.py:405
  60.4 0.0 all-gather.4.cloned.1.call-update
  60.4 0.0 all-gather.6.cloned.1.call-done
  60.5 11.9 %collective-permute-done.2.left = bf16[2,2,128,1024]{3,2,1,0:T(8,128)(2,1)S(1)} collective-permute-done((bf16[2,2,128,1024]{3,2,1,0:T(8,128)(2,1)}, bf16[2,2,128,1024]{3,2,1,0:T(8,128)(2,1)S(1)}, u32[]{:S(2)}, u32[]{:S(2)}) %collective-permute-start.2) | collective-permute-done | bytes 1048608 | tf_op jit(solution)/shard_map/Ha/ppermute | solution.py:72
  72.3 1.9 collective-permute-start.8
  74.3 14.0 %collective-permute-done.3.right = bf16[2,2,128,1024]{3,2,1,0:T(8,128)(2,1)} collective-permute-done((bf16[2,2,128,1024]{3,2,1,0:T(8,128)(2,1)}, bf16[2,2,128,1024]{3,2,1,0:T(8,128)(2,1)}, u32[]{:S(2)}, u32[]{:S(2)}) %collective-permute-start.3) | collective-permute-done | bytes 1048608 | tf_op jit(solution)/shard_map/Hb/ppermute | solution.py:72
  88.2 1.9 collective-permute-start.4
  90.1 0.0 copy-done.7
  90.1 8.7 %shard_map.124 = (bf16[4,2,128,256]{3,2,1,0:T(8,128)(2,1)}, bf16[2,128,1024]{2,1,0:T(8,128)(2,1)}) custom-call(s32[2]{0:T(128)} %pad_add_fusion.meta, bf16[2,2,128,1024]{3,2,1,0:T(8,128)(2,1)} %get-tuple-element.22.q_ref, bf16[2,2,128,1024]{3,2,1,0:T(8,128)(2,1)} %copy-done.7, bf16[2,2,128,1024]{3,2,1,0:T(8,128)(2,1)} %shard_map.123.mid, ...), custom_call_target="tpu_custom_call" | custom-call | flops 137438953472 | bytes 1 | tf_op jit(solution)/shard_map/pallas_call | solution.py:212
  98.9 4.1 %all-to-all-start = ((bf16[4,2,128,256]{3,2,1,0:T(8,128)(2,1)}), bf16[4,2,128,256]{3,2,1,0:T(8,128)(2,1)S(1)}, u32[]{:S(2)}, u32[]{:S(2)}) async-start(bf16[4,2,128,256]{3,2,1,0:T(8,128)(2,1)} %get-tuple-element.26), calls=%async_computation | async-start | bytes 1048576 | tf_op jit(solution)/shard_map/all_to_all | solution.py:410
  103.0 0.0 collective-permute-done.5.left_tan
  103.0 0.0 collective-permute-done.6.right_tan
  103.0 10.1 %all-to-all-done.att = bf16[4,2,128,256]{3,2,1,0:T(8,128)(2,1)S(1)} async-done(((bf16[4,2,128,256]{3,2,1,0:T(8,128)(2,1)}), bf16[4,2,128,256]{3,2,1,0:T(8,128)(2,1)S(1)}, u32[]{:S(2)}, u32[]{:S(2)}) %all-to-all-start) | async-done | bytes 524320 | tf_op jit(solution)/shard_map/all_to_all | solution.py:410
  113.1 0.0 collective-permute-done.4.w_sib
  113.1 0.8 copy-done.1
  114.0 1.2 copy-done.2
  115.2 4.7 %shard_map.125 = bf16[8,2,96,256]{3,2,1,0:T(8,128)(2,1)} custom-call(bf16[4,1536,128]{2,1,0:T(8,128)(2,1)} %bitcast.23, bf16[4,1536,128]{2,1,0:T(8,128)(2,1)} %copy-done.2, bf16[4,2,128,256]{3,2,1,0:T(8,128)(2,1)} %copy-done.1), custom_call_target="tpu_custom_call" | custom-call | flops 1 | bytes 1 | tf_op jit(solution)/shard_map/pallas_call | solution.py:359
  119.9 9.9 %all-to-all-start.1 = ((bf16[8,2,96,256]{3,2,1,0:T(8,128)(2,1)}), bf16[8,2,96,256]{3,2,1,0:T(8,128)(2,1)S(1)}, u32[]{:S(2)}, u32[]{:S(2)}) async-start(bf16[8,2,96,256]{3,2,1,0:T(8,128)(2,1)} %shard_map.125), calls=%async_computation.1 | async-start | bytes 1572864 | tf_op jit(solution)/shard_map/all_to_all | solution.py:413
  129.8 0.0 collective-permute-done.7.left_tan
  129.8 0.0 collective-permute-done.8.right_tan
  129.8 6.3 %shard_map.126.tan = bf16[2,128,512]{2,1,0:T(8,128)(2,1)} custom-call(s32[2]{0:T(128)} %pad_add_fusion.meta, bf16[2,2,128,1024]{3,2,1,0:T(8,128)(2,1)} %get-tuple-element.22.q_ref, bf16[2,2,128,1024]{3,2,1,0:T(8,128)(2,1)} %copy-done.7, bf16[2,2,128,1024]{3,2,1,0:T(8,128)(2,1)} %shard_map.123.mid, bf16[2,2,128,1024]{3,2,1,0:T(8,128)(2,1)} %collective-permute-done.3.right, ...), custom_call_target="tpu_custom_call" | custom-call | flops 8589934592 | bytes 1 | tf_op jit(solution)/shard_map/pallas_call | solution.py:257
  136.1 6.3 %shard_map.128.tan = bf16[2,128,512]{2,1,0:T(8,128)(2,1)} custom-call(s32[2]{0:T(128)} %pad_add_fusion.meta, bf16[2,2,128,1024]{3,2,1,0:T(8,128)(2,1)} %get-tuple-element.22.q_ref, bf16[2,2,128,1024]{3,2,1,0:T(8,128)(2,1)} %copy-done.7, bf16[2,2,128,1024]{3,2,1,0:T(8,128)(2,1)} %shard_map.123.mid, bf16[2,2,128,1024]{3,2,1,0:T(8,128)(2,1)} %collective-permute-done.3.right, ...), custom_call_target="tpu_custom_call" | custom-call | flops 8589934592 | bytes 1 | tf_op jit(solution)/shard_map/pallas_call | solution.py:257
  142.4 18.3 %all-to-all-done.1 = bf16[8,2,96,256]{3,2,1,0:T(8,128)(2,1)S(1)} async-done(((bf16[8,2,96,256]{3,2,1,0:T(8,128)(2,1)}), bf16[8,2,96,256]{3,2,1,0:T(8,128)(2,1)S(1)}, u32[]{:S(2)}, u32[]{:S(2)}) %all-to-all-start.1) | async-done | bytes 786464 | tf_op jit(solution)/shard_map/all_to_all | solution.py:413
  160.7 0.8 convert_reduce_fusion
  161.4 19.2 %all-to-all-start.2 = ((f32[8,24,256]{2,1,0:T(8,128)}), f32[8,24,256]{2,1,0:T(8,128)S(1)}, u32[]{:S(2)}, u32[]{:S(2)}) async-start(f32[8,24,256]{2,1,0:T(8,128)} %bitcast.8), calls=%async_computation.2 | async-start | bytes 393216 | tf_op jit(solution)/shard_map/all_to_all | solution.py:416
  180.6 5.6 %shard_map.127 = (f32[2,2,64,1536]{3,2,1,0:T(8,128)}, f32[2,2,64,1536]{3,2,1,0:T(8,128)}) custom-call(bf16[2,128,1024]{2,1,0:T(8,128)(2,1)} %get-tuple-element.29.att, bf16[2,128,512]{2,1,0:T(8,128)(2,1)} %shard_map.126.tan, bf16[1536,1024]{1,0:T(8,128)(2,1)} %bitcast.30, f32[2,1536]{1,0:T(2,128)} %gate.3, f32[2,1536]{1,0:T(2,128)} %gate_tan.1), custom_call_target="tpu_custom_call" | custom-call | flops 8589934592 | bytes 1 | tf_op jit(solution)/shard_map/pallas_call | solution.py:303
  186.2 1.9 collective-permute-start.9
  188.1 0.0 all-to-all-done.2
  188.1 0.0 copy-start.3
  188.1 4.1 %shard_map.129 = (f32[1,2,64,1536]{3,2,1,0:T(8,128)}, f32[1,2,64,1536]{3,2,1,0:T(8,128)}) custom-call(bf16[2,128,512]{2,1,0:T(8,128)(2,1)} %shard_map.128.tan, bf16[1536,1024]{1,0:T(8,128)(2,1)} %bitcast.31, f32[2,1536]{1,0:T(2,128)} %gate.3), custom_call_target="tpu_custom_call" | custom-call | flops 8589934592 | bytes 1 | tf_op jit(solution)/shard_map/pallas_call | solution.py:325
  192.3 2.4 %collective-permute-start.10 = (f32[1,2,64,1536]{3,2,1,0:T(8,128)}, f32[1,2,64,1536]{3,2,1,0:T(8,128)S(1)}, u32[]{:S(2)}, u32[]{:S(2)}) collective-permute-start(f32[1,2,64,1536]{3,2,1,0:T(8,128)} %get-tuple-element.38), channel_id=1, source_target_pairs={{0,1},{1,0},{2,3},{3,2},{4,5},{5,4},{6,7},{7,6},{8,9},{9,8},{10,11... | collective-permute-start | bytes 2359304 | tf_op jit(solution)/shard_map/Uswap/ppermute | solution.py:72
  194.7 1.9 collective-permute-start.11
  196.6 10.1 %collective-permute-done.11 = f32[24,256]{1,0:T(8,128)S(1)} collective-permute-done((f32[24,256]{1,0:T(8,128)S(1)}, f32[24,256]{1,0:T(8,128)S(1)}, u32[]{:S(2)}, u32[]{:S(2)}) %collective-permute-start.11) | collective-permute-done | bytes 24608 | tf_op jit(solution)/shard_map/Turn/ppermute | solution.py:72
  206.7 0.0 collective-permute-done.10
  206.7 0.0 collective-permute-done.9
  206.7 0.0 copy-done.3
  206.7 2.3 %fusion.4 = (bf16[2,64,1536]{2,1,0:T(8,128)(2,1)}, bf16[2,64,1536]{2,1,0:T(8,128)(2,1)}) fusion(f32[1,2,64,1536]{3,2,1,0:T(8,128)} %get-tuple-element.37, f32[1,2,64,1536]{3,2,1,0:T(8,128)S(1)} %collective-permute-done.10, f32[2,2,64,1536]{3,2,1,0:T(8,128)S(1)} %collective-permute-done.9, f32[2,2,64,1536]{3,2,1,0:T(8,128)S(1)} %copy-done.3), kind=kLoop, calls=%fused_computation.8 | loop fusion | flops 1179648 | bytes 5505024 | tf_op jit(solution)/shard_map/convert_element_type | solution.py:429
  209.1 0.6 copy.21
  (10 shorter events, 0.1 us)
Async XLA Ops:
  7.2 53.3 %all-gather.6.cloned.1.call-start = ((), (), s32[]{:S(2)}) async-start(), calls=%async_computation.4 | async-start | bytes 1966080 | tf_op jit(solution)/shard_map/all_gather | solution.py:401
  7.9 5.2 %copy-start.5 = (f32[2048,24]{0,1:T(8,128)S(1)}, f32[2048,24]{0,1:T(8,128)}, u32[]{:S(2)}) copy-start(f32[2048,24]{0,1:T(8,128)} %param.16) | copy-start | bytes 589828
  7.9 11.7 %copy-start.4 = (bf16[2,64,1536]{2,1,0:T(8,128)(2,1)S(1)}, bf16[2,64,1536]{2,1,0:T(8,128)(2,1)}, u32[]{:S(2)}) copy-start(bf16[2,64,1536]{2,1,0:T(8,128)(2,1)} %param.19) | copy-start | bytes 1179652
  7.9 11.7 %copy-start.6 = (f32[2,1536]{1,0:T(2,128)S(1)}, f32[2,1536]{1,0:T(2,128)}, u32[]{:S(2)}) copy-start(f32[2,1536]{1,0:T(2,128)} %gate.3) | copy-start | bytes 36868
  11.2 8.4 %collective-permute-start = (bf16[6,2,64,1024]{3,2,1,0:T(8,128)(2,1)}, bf16[6,2,64,1024]{3,2,1,0:T(8,128)(2,1)S(1)}, u32[]{:S(2)}, u32[]{:S(2)}) collective-permute-start(bf16[6,2,64,1024]{3,2,1,0:T(8,128)(2,1)} %shard_map.121), channel_id=1, source_target_pairs={{0,1},{1,0},{2,3},{3,2},{4,5},{5,4},{6,7},{7,6},{8,9},{9,8},{10,11... | collective-permute-start | bytes 4718600 | tf_op jit(solution)/shard_map/Sx/ppermute | solution.py:72
  13.5 6.0 %collective-permute-start.1 = (bf16[1,24,1024]{2,1,0:T(8,128)(2,1)S(1)}, bf16[1,24,1024]{2,1,0:T(8,128)(2,1)S(1)}, u32[]{:S(2)}, u32[]{:S(2)}) collective-permute-start(bf16[1,24,1024]{2,1,0:T(8,128)(2,1)S(1)} %bitcast.26), channel_id=1, source_target_pairs={{0,256},{1,257},{2,258},{3,259},{4,260},{5,261},{6,262},{7,263},{8... | collective-permute-start | bytes 147464 | tf_op jit(solution)/shard_map/Wy/ppermute | solution.py:72
  19.6 1.3 copy-start
  20.9 159.7 %all-gather.4.cloned.1.call-start = ((), (), s32[]{:S(2)}) async-start(), calls=%async_computation.3 | async-start | bytes 3538944 | tf_op jit(solution)/shard_map/all_gather | solution.py:406
  23.8 48.6 %collective-permute-start.2 = (bf16[2,2,128,1024]{3,2,1,0:T(8,128)(2,1)}, bf16[2,2,128,1024]{3,2,1,0:T(8,128)(2,1)S(1)}, u32[]{:S(2)}, u32[]{:S(2)}) collective-permute-start(bf16[2,2,128,1024]{3,2,1,0:T(8,128)(2,1)} %shard_map.123.mid), channel_id=1, source_target_pairs={{0,2},{1,3},{2,4},{3,5},{4,6},{5,7},{6,8},{7,9},{8,10},{9,11},{10,... | collective-permute-start | bytes 3145736 | tf_op jit(solution)/shard_map/Ha/ppermute | solution.py:72
  26.5 61.8 %collective-permute-start.3 = (bf16[2,2,128,1024]{3,2,1,0:T(8,128)(2,1)}, bf16[2,2,128,1024]{3,2,1,0:T(8,128)(2,1)}, u32[]{:S(2)}, u32[]{:S(2)}) collective-permute-start(bf16[2,2,128,1024]{3,2,1,0:T(8,128)(2,1)} %shard_map.123.mid), channel_id=1, source_target_pairs={{2,0},{3,1},{4,2},{5,3},{6,4},{7,5},{8,6},{9,7},{10,8},{11,9},{12,... | collective-permute-start | bytes 3145736 | tf_op jit(solution)/shard_map/Hb/ppermute | solution.py:72
  35.2 67.8 %collective-permute-start.5 = (bf16[2,2,128,512]{3,2,1,0:T(8,128)(2,1)}, bf16[2,2,128,512]{3,2,1,0:T(8,128)(2,1)}, u32[]{:S(2)}, u32[]{:S(2)}) collective-permute-start(bf16[2,2,128,512]{3,2,1,0:T(8,128)(2,1)} %get-tuple-element.27.mid_tan), channel_id=1, source_target_pairs={{0,2},{1,3},{2,4},{3,5},{4,6},{5,7},{6,8},{7,9},{8,10},{9,11},{10,... | collective-permute-start | bytes 1572872 | tf_op jit(solution)/shard_map/T1a/ppermute | solution.py:72
  37.1 65.9 %collective-permute-start.6 = (bf16[2,2,128,512]{3,2,1,0:T(8,128)(2,1)}, bf16[2,2,128,512]{3,2,1,0:T(8,128)(2,1)}, u32[]{:S(2)}, u32[]{:S(2)}) collective-permute-start(bf16[2,2,128,512]{3,2,1,0:T(8,128)(2,1)} %get-tuple-element.27.mid_tan), channel_id=1, source_target_pairs={{2,0},{3,1},{4,2},{5,3},{6,4},{7,5},{8,6},{9,7},{10,8},{11,9},{12,... | collective-permute-start | bytes 1572872 | tf_op jit(solution)/shard_map/T1b/ppermute | solution.py:72
  43.2 86.6 %collective-permute-start.7 = (bf16[2,2,128,512]{3,2,1,0:T(8,128)(2,1)}, bf16[2,2,128,512]{3,2,1,0:T(8,128)(2,1)}, u32[]{:S(2)}, u32[]{:S(2)}) collective-permute-start(bf16[2,2,128,512]{3,2,1,0:T(8,128)(2,1)} %get-tuple-element.30.mid_tan), channel_id=1, source_target_pairs={{0,2},{1,3},{2,4},{3,5},{4,6},{5,7},{6,8},{7,9},{8,10},{9,11},{10,... | collective-permute-start | bytes 1572872 | tf_op jit(solution)/shard_map/T0a/ppermute | solution.py:72
  72.3 17.8 %copy-start.7 = (bf16[2,2,128,1024]{3,2,1,0:T(8,128)(2,1)}, bf16[2,2,128,1024]{3,2,1,0:T(8,128)(2,1)S(1)}, u32[]{:S(2)}) copy-start(bf16[2,2,128,1024]{3,2,1,0:T(8,128)(2,1)S(1)} %collective-permute-done.2.left) | copy-start | bytes 3145732
  72.3 57.5 %collective-permute-start.8 = (bf16[2,2,128,512]{3,2,1,0:T(8,128)(2,1)}, bf16[2,2,128,512]{3,2,1,0:T(8,128)(2,1)}, u32[]{:S(2)}, u32[]{:S(2)}) collective-permute-start(bf16[2,2,128,512]{3,2,1,0:T(8,128)(2,1)} %get-tuple-element.30.mid_tan), channel_id=1, source_target_pairs={{2,0},{3,1},{4,2},{5,3},{6,4},{7,5},{8,6},{9,7},{10,8},{11,9},{12,... | collective-permute-start | bytes 1572872 | tf_op jit(solution)/shard_map/T0b/ppermute | solution.py:72
  88.2 24.9 %collective-permute-start.4 = (bf16[4,1536,128]{2,1,0:T(8,128)(2,1)}, bf16[4,1536,128]{2,1,0:T(8,128)(2,1)S(1)}, u32[]{:S(2)}, u32[]{:S(2)}) collective-permute-start(bf16[4,1536,128]{2,1,0:T(8,128)(2,1)} %bitcast.22), channel_id=1, source_target_pairs={{0,1},{1,0},{2,3},{3,2},{4,5},{5,4},{6,7},{7,6},{8,9},{9,8},{10,11... | collective-permute-start | bytes 4718600 | tf_op jit(solution)/shard_map/Cswap/ppermute | solution.py:72
  98.9 14.3 %all-to-all-start = ((bf16[4,2,128,256]{3,2,1,0:T(8,128)(2,1)}), bf16[4,2,128,256]{3,2,1,0:T(8,128)(2,1)S(1)}, u32[]{:S(2)}, u32[]{:S(2)}) async-start(bf16[4,2,128,256]{3,2,1,0:T(8,128)(2,1)} %get-tuple-element.26), calls=%async_computation | async-start | bytes 1048576 | tf_op jit(solution)/shard_map/all_to_all | solution.py:410
  113.1 0.8 copy-start.1
  114.0 1.2 copy-start.2
  119.9 40.8 %all-to-all-start.1 = ((bf16[8,2,96,256]{3,2,1,0:T(8,128)(2,1)}), bf16[8,2,96,256]{3,2,1,0:T(8,128)(2,1)S(1)}, u32[]{:S(2)}, u32[]{:S(2)}) async-start(bf16[8,2,96,256]{3,2,1,0:T(8,128)(2,1)} %shard_map.125), calls=%async_computation.1 | async-start | bytes 1572864 | tf_op jit(solution)/shard_map/all_to_all | solution.py:413
  161.4 26.7 %all-to-all-start.2 = ((f32[8,24,256]{2,1,0:T(8,128)}), f32[8,24,256]{2,1,0:T(8,128)S(1)}, u32[]{:S(2)}, u32[]{:S(2)}) async-start(f32[8,24,256]{2,1,0:T(8,128)} %bitcast.8), calls=%async_computation.2 | async-start | bytes 393216 | tf_op jit(solution)/shard_map/all_to_all | solution.py:416
  186.2 20.5 %collective-permute-start.9 = (f32[2,2,64,1536]{3,2,1,0:T(8,128)}, f32[2,2,64,1536]{3,2,1,0:T(8,128)S(1)}, u32[]{:S(2)}, u32[]{:S(2)}) collective-permute-start(f32[2,2,64,1536]{3,2,1,0:T(8,128)} %get-tuple-element.33), channel_id=1, source_target_pairs={{0,1},{1,0},{2,3},{3,2},{4,5},{5,4},{6,7},{7,6},{8,9},{9,8},{10,11... | collective-permute-start | bytes 4718600 | tf_op jit(solution)/shard_map/Pswap/ppermute | solution.py:72
  188.1 18.6 %copy-start.3 = (f32[2,2,64,1536]{3,2,1,0:T(8,128)S(1)}, f32[2,2,64,1536]{3,2,1,0:T(8,128)}, u32[]{:S(2)}) copy-start(f32[2,2,64,1536]{3,2,1,0:T(8,128)} %get-tuple-element.32) | copy-start | bytes 4718596
  192.3 14.4 %collective-permute-start.10 = (f32[1,2,64,1536]{3,2,1,0:T(8,128)}, f32[1,2,64,1536]{3,2,1,0:T(8,128)S(1)}, u32[]{:S(2)}, u32[]{:S(2)}) collective-permute-start(f32[1,2,64,1536]{3,2,1,0:T(8,128)} %get-tuple-element.38), channel_id=1, source_target_pairs={{0,1},{1,0},{2,3},{3,2},{4,5},{5,4},{6,7},{7,6},{8,9},{9,8},{10,11... | collective-permute-start | bytes 2359304 | tf_op jit(solution)/shard_map/Uswap/ppermute | solution.py:72
  194.7 12.0 %collective-permute-start.11 = (f32[24,256]{1,0:T(8,128)S(1)}, f32[24,256]{1,0:T(8,128)S(1)}, u32[]{:S(2)}, u32[]{:S(2)}) collective-permute-start(f32[24,256]{1,0:T(8,128)S(1)} %reduce_sum.19), channel_id=1, source_target_pairs={{0,0},{1,1},{2,8},{3,9},{4,16},{5,17},{6,24},{7,25},{8,2},{9,3},{1... | collective-permute-start | bytes 73736 | tf_op jit(solution)/shard_map/Turn/ppermute | solution.py:72
Sparse Core Ops, SparseCore 0:
  21.0 38.0 all-gather.5
  61.2 98.1 all-gather.3

commit v5 on v4

--- a/solution.py
+++ b/solution.py
@@ -106,9 +106,8 @@
     split=cost(1, 1),
     join=cost(1, 1),
     attend=cost(2**37, 1),
-    tangent=cost(2**33, 1),
-    project=cost(2**33, 1),
-    finish=cost(2**33, 1),
+    tangent=cost(1, 1),
+    project=cost(1, 1),
     grad=cost(1, 1),
 )
 
@@ -285,16 +284,17 @@
         other[at, s] = value[(2 * s + 1) * rows : (2 * s + 2) * rows]
 
 
-def project_body(att, tan, weight, gate, gate_tan, here, other):
+def project_body(att, first, last, weight, gate, gate_tan, here, other):
     rows = att.shape[1]
+    half = first.shape[2]
     proj = nt(flat2(att), weight[...])
-    proj_tan = nt(flat2(tan), weight[:, : tan.shape[2]])
+    proj_tan = nt(flat2(first), weight[:, :half]) + nt(flat2(last), weight[:, half:])
     g, gt = gate_rows(gate, rows), gate_rows(gate_tan, rows)
     put_halves(g * proj, here, other, 0)
     put_halves(gt * proj + g * proj_tan, here, other, 1)
 
 
-def project(att, tan, weight, gate, gate_tan):
+def project(att, first, last, weight, gate, gate_tan):
     seqs, rows, _ = att.shape
     width = gate.shape[1]
     step = 512
@@ -304,37 +304,12 @@
         project_body,
         grid=(width // step,),
         out_shape=[jax.ShapeDtypeStruct((2, seqs, rows // 2, width), F32)] * 2,
-        in_specs=[vmem_spec()] * 2
+        in_specs=[vmem_spec()] * 3
         + [pl.BlockSpec((step, GROUP), lambda i: (i, 0)), gates, gates],
         out_specs=[block, block],
         compiler_params=params("arbitrary"),
         cost_estimate=COSTS["project"],
-    )(att, tan, weight, gate, gate_tan)
-
-
-def finish_body(tan, weight, gate, here, other):
-    proj_tan = nt(flat2(tan), weight[...])
-    put_halves(gate_rows(gate, tan.shape[1]) * proj_tan, here, other, 0)
-
-
-def finish(tan, weight, gate):
-    seqs, rows, half = tan.shape
-    width = gate.shape[1]
-    step = 512
-    block = pl.BlockSpec((1, seqs, rows // 2, step), lambda i: (0, 0, 0, i))
-    return pl.pallas_call(
-        finish_body,
-        grid=(width // step,),
-        out_shape=[jax.ShapeDtypeStruct((1, seqs, rows // 2, width), F32)] * 2,
-        in_specs=[
-            vmem_spec(),
-            pl.BlockSpec((step, half), lambda i: (i, 1)),
-            pl.BlockSpec((2, step), lambda i: (0, i)),
-        ],
-        out_specs=[block, block],
-        compiler_params=params("arbitrary"),
-        cost_estimate=COSTS["finish"],
-    )(tan, weight, gate)
+    )(att, first, last, weight, gate, gate_tan)
 
 
 def grad_body(w_own, w_sib, att, out):
@@ -393,6 +368,8 @@
     q_rows, *tans = join_rows(
         meta, arrays[2:], got, (((0, 1), (0, NJ)),) + tuple(((2, 3), p) for p in PIECES), 2
     )
+    low = lax.all_gather(low, AXES, axis_index_groups=GROUPS_X, axis=1, tiled=True)
+    *tans, _ = after((*tans, low))
     tans = [[send(t, TO_NEXT, "T%da" % n), t, send(t, TO_PREV, "T%db" % n)] for n, t in enumerate(tans)]
 
     cotangent, _ = after((cotangent, got))
@@ -402,31 +379,25 @@
     w_own, _ = after((w_own, kv))
     w_sib = send(w_own, SWAP_CORE, "Cswap")
 
-    low = lax.all_gather(low, AXES, axis_index_groups=GROUPS_X, axis=1, tiled=True)
     weight = lax.all_gather(low, AXES, axis_index_groups=GROUPS_Z, axis=1, tiled=True)
     weight = weight.reshape(-1, GROUP)
 
     quarter, att = attend(meta, q_rows, keyed)
     quarter = lax.all_to_all(quarter, AXES, 0, 0, axis_index_groups=GROUPS_X, tiled=True)
-    (quarter, tans[1][0], tans[1][2]) = after((quarter, tans[1][0], tans[1][2]))
+    (quarter, tans[0][0], tans[0][2]) = after((quarter, tans[0][0], tans[0][2]))
     terms = grad_terms(w_own, w_sib, quarter)
     terms = lax.all_to_all(terms, AXES, 0, 0, axis_index_groups=GROUPS_Z, tiled=True)
     terms = jnp.sum(terms.astype(F32), axis=0).reshape(NYL * NYH, -1, PAIR)
-    summed = terms
     terms = lax.all_to_all(terms, AXES, 0, 0, axis_index_groups=GROUPS_Y, tiled=True)
     terms = jnp.sum(terms, axis=0)
     weight_grad = send(terms, TURN, "Turn").T
 
-    tan_first = attend_tangent(meta, q_rows, keyed, tans[0], 0)
-    att, _ = after((att, summed))
-    here, other = project(att, tan_first, weight, gate, gate_tan)
+    first = attend_tangent(meta, q_rows, keyed, tans[0], 0)
+    last = attend_tangent(meta, q_rows, keyed, tans[1], 1)
+    here, other = project(att, first, last, weight, gate, gate_tan)
     other = send(other, SWAP_CORE, "Pswap")
-    tan_last = attend_tangent(meta, q_rows, keyed, tans[1], 1)
-    tan_last, _ = after((tan_last, terms))
-    rest, rest_other = finish(tan_last, weight, gate)
-    rest_other = send(rest_other, SWAP_CORE, "Uswap")
     mixed = (here[0] + other[0]).astype(BF)
-    mixed_tan = ((here[1] + other[1]) + (rest[0] + rest_other[0])).astype(BF)
+    mixed_tan = (here[1] + other[1]).astype(BF)
     return mixed, mixed_tan, weight_grad
 
 

time: 217 us -> 220 us (1.014)
  the two profiles are of different devices: /device:TPU:96 before, /device:TPU:40 now
where the time goes in v5:
time: 220 us; the launch traced here: 219 us
  starting transfers between devices  64 us (29%)
  waiting for transfers between devices  47 us (21%)
  blocking collectives  43.1 us (20%)
  Pallas kernels  41.5 us (19%)
  between operations  14.3 us (6%)
  local copies, waits for them, and re-layouts  5.96 us (3%)
  other arithmetic  3.3 us (2%)
    ppermute x11, starting transfers between devices, send(): return lax.ppermute(array, AXES, pairs)  43.6 us
    ppermute x11, waiting for transfers between devices, send(): return lax.ppermute(array, AXES, pairs)  30.1 us
    all_to_all x1, blocking collectives, on_device(): lax.all_to_all(terms, AXES, 0, 0, axis_index_groups=GROUPS_Y, tiled=True)  28.3 us
    all_gather x1, waiting for transfers between devices, on_device(): lax.all_gather(low, AXES, axis_index_groups=GROUPS_Z, axis=1, tiled=True)  16.8 us
    all_gather x1, blocking collectives, on_device(): lax.all_gather(low, AXES, axis_index_groups=GROUPS_X, axis=1, tiled=True)  14.8 us
    pallas_call x2, Pallas kernels, attend_tangent(): pl.pallas_call(tangent_body, out_shape=jax.ShapeDtypeStruct((seqs, rows,...  12.5 us
    all_to_all x1, starting transfers between devices, on_device(): lax.all_to_all(terms, AXES, 0, 0, axis_index_groups=GROUPS_Z, tiled=True)  11.7 us
    pallas_call x1, Pallas kernels, attend(): pl.pallas_call(attend_body, out_shape=[jax.ShapeDtypeStruct((NJ, seqs, ro...  8.88 us
  transfers between devices with their start and end apart: 15, of which 5 were waited for; matrix products, arithmetic and copies ran while one was open for 0% of the time, Pallas kernels for 17%

profile of v5, /device:TPU:40, one launch (start us, length us, event | category | flops | bytes accessed | tf_op | source)
XLA Modules:
  0.0 219.1 jit_solution(4505872145614943312)
XLA Ops:
  7.2 0.0 all-gather.6.cloned.1.call-start
  7.2 0.6 pad_add_fusion.meta
  7.9 3.3 %shard_map.121 = bf16[6,2,64,1024]{3,2,1,0:T(8,128)(2,1)} custom-call(s32[2]{0:T(128)} %pad_add_fusion.meta, bf16[2,64,2048]{2,1,0:T(8,128)(2,1)} %refs_0_.5, bf16[2,64,2048]{2,1,0:T(8,128)(2,1)} %refs_1_.5, bf16[2,64,2048]{2,1,0:T(8,128)(2,1)} %refs_0_.4, bf16[2,64,2048]{2,1,0:T(8,128)(2,1)} %refs_1_.4, bf16[2,64,2048]{2,1,0:T(8,128)(2,1)} %refs_2_.3, ...), custom_call_target="tpu_custom_call" | custom-call | flops 1 | bytes 1 | tf_op jit(solution)/shard_map/pallas_call | solution.py:131
  11.2 1.9 collective-permute-start
  13.1 0.0 copy-done.10
  13.2 0.3 dynamic-slice_reduce_fusion
  13.5 3.3 %collective-permute-start.1 = (bf16[1,24,1024]{2,1,0:T(8,128)(2,1)S(1)}, bf16[1,24,1024]{2,1,0:T(8,128)(2,1)S(1)}, u32[]{:S(2)}, u32[]{:S(2)}) collective-permute-start(bf16[1,24,1024]{2,1,0:T(8,128)(2,1)S(1)} %bitcast.28), channel_id=1, source_target_pairs={{0,256},{1,257},{2,258},{3,259},{4,260},{5,261},{6,262},{7,263},{8... | collective-permute-start | bytes 147464 | tf_op jit(solution)/shard_map/Wy/ppermute | solution.py:72
  16.8 2.8 %collective-permute-done.1 = bf16[1,24,1024]{2,1,0:T(8,128)(2,1)S(1)} collective-permute-done((bf16[1,24,1024]{2,1,0:T(8,128)(2,1)S(1)}, bf16[1,24,1024]{2,1,0:T(8,128)(2,1)S(1)}, u32[]{:S(2)}, u32[]{:S(2)}) %collective-permute-start.1) | collective-permute-done | bytes 49184 | tf_op jit(solution)/shard_map/Wy/ppermute | solution.py:72
  19.6 0.0 collective-permute-done.refs_4_.refs_2_
  19.6 0.0 copy-done.9
  19.6 0.0 copy-done.11
  19.6 0.0 copy-start
  19.6 0.1 multiply_convert_fusion
  19.7 1.2 copy.17
  20.8 0.0 all-gather.6.cloned.1.call-update
  20.9 0.0 all-gather.4.cloned.1.call-start
  20.9 0.0 copy-done
  20.9 2.8 %shard_map.123.mid = bf16[2,2,128,1024]{3,2,1,0:T(8,128)(2,1)} custom-call(s32[2]{0:T(128)} %pad_add_fusion.meta, bf16[2,64,2048]{2,1,0:T(8,128)(2,1)} %refs_0_.5, bf16[2,64,2048]{2,1,0:T(8,128)(2,1)} %refs_1_.5, bf16[6,2,64,1024]{3,2,1,0:T(8,128)(2,1)} %copy-done), custom_call_target="tpu_custom_call" | custom-call | flops 1 | bytes 1 | tf_op jit(solution)/shard_map/pallas_call | solution.py:159
  23.7 2.7 %collective-permute-start.2 = (bf16[2,2,128,1024]{3,2,1,0:T(8,128)(2,1)}, bf16[2,2,128,1024]{3,2,1,0:T(8,128)(2,1)S(1)}, u32[]{:S(2)}, u32[]{:S(2)}) collective-permute-start(bf16[2,2,128,1024]{3,2,1,0:T(8,128)(2,1)} %shard_map.123.mid), channel_id=1, source_target_pairs={{0,2},{1,3},{2,4},{3,5},{4,6},{5,7},{6,8},{7,9},{8,10},{9,11},{10,... | collective-permute-start | bytes 3145736 | tf_op jit(solution)/shard_map/Ha/ppermute | solution.py:72
  26.4 5.3 %collective-permute-start.3 = (bf16[2,2,128,1024]{3,2,1,0:T(8,128)(2,1)}, bf16[2,2,128,1024]{3,2,1,0:T(8,128)(2,1)S(1)}, u32[]{:S(2)}, u32[]{:S(2)}) collective-permute-start(bf16[2,2,128,1024]{3,2,1,0:T(8,128)(2,1)} %shard_map.123.mid), channel_id=1, source_target_pairs={{2,0},{3,1},{4,2},{5,3},{6,4},{7,5},{8,6},{9,7},{10,8},{11,9},{12,... | collective-permute-start | bytes 3145736 | tf_op jit(solution)/shard_map/Hb/ppermute | solution.py:72
  31.7 3.6 %shard_map.122 = (bf16[2,2,128,1024]{3,2,1,0:T(8,128)(2,1)}, bf16[2,2,128,512]{3,2,1,0:T(8,128)(2,1)}, bf16[2,2,128,512]{3,2,1,0:T(8,128)(2,1)}) custom-call(s32[2]{0:T(128)} %pad_add_fusion.meta, bf16[2,64,2048]{2,1,0:T(8,128)(2,1)} %refs_0_.4, bf16[2,64,2048]{2,1,0:T(8,128)(2,1)} %refs_1_.4, bf16[2,64,2048]{2,1,0:T(8,128)(2,1)} %refs_2_.3, ...), custom_call_target="tpu_custom_call" | custom-call | flops 1 | bytes 1 | tf_op jit(solution)/shard_map/pallas_call | solution.py:159
  35.3 14.8 %all_gather.12 = bf16[2,96,1024]{2,1,0:T(8,128)(2,1)} all-gather(bf16[2,24,1024]{2,1,0:T(8,128)(2,1)S(1)} %maximum_select_fusion), channel_id=1, replica_groups={{0,8,16,24},{1,9,17,25},{32,40,48,56},{33,41,49,57},{64,72,80,88},{65,7..., dimensions={1}, use_global_device_ids=true | all-gather | bytes 491520 | tf_op jit(solution)/shard_map/all_gather | solution.py:371
  50.0 14.4 %collective-permute-start.4 = (bf16[2,2,128,512]{3,2,1,0:T(8,128)(2,1)}, bf16[2,2,128,512]{3,2,1,0:T(8,128)(2,1)S(1)}, u32[]{:S(2)}, u32[]{:S(2)}) collective-permute-start(bf16[2,2,128,512]{3,2,1,0:T(8,128)(2,1)} %get-tuple-element.26.mid_tan), channel_id=1, source_target_pairs={{0,2},{1,3},{2,4},{3,5},{4,6},{5,7},{6,8},{7,9},{8,10},{9,11},{10,... | collective-permute-start | bytes 1572872 | tf_op jit(solution)/shard_map/T0a/ppermute | solution.py:72
  64.4 1.9 collective-permute-start.5
  66.3 0.0 all-gather.4.cloned.1.call-update
  66.3 0.0 all-gather.6.cloned.1.call-done
  66.4 1.9 collective-permute-start.9
  68.3 15.3 %collective-permute-done.2.left = bf16[2,2,128,1024]{3,2,1,0:T(8,128)(2,1)S(1)} collective-permute-done((bf16[2,2,128,1024]{3,2,1,0:T(8,128)(2,1)}, bf16[2,2,128,1024]{3,2,1,0:T(8,128)(2,1)S(1)}, u32[]{:S(2)}, u32[]{:S(2)}) %collective-permute-start.2) | collective-permute-done | bytes 1048608 | tf_op jit(solution)/shard_map/Ha/ppermute | solution.py:72
  83.6 0.0 collective-permute-done.3.right
  83.6 1.1 copy-done.1
  84.6 0.3 copy-done.2
  85.0 8.9 %shard_map.124 = (bf16[4,2,128,256]{3,2,1,0:T(8,128)(2,1)}, bf16[2,128,1024]{2,1,0:T(8,128)(2,1)}) custom-call(s32[2]{0:T(128)} %pad_add_fusion.meta, bf16[2,2,128,1024]{3,2,1,0:T(8,128)(2,1)} %get-tuple-element.20.q_ref, bf16[2,2,128,1024]{3,2,1,0:T(8,128)(2,1)} %copy-done.1, bf16[2,2,128,1024]{3,2,1,0:T(8,128)(2,1)} %shard_map.123.mid, ...), custom_call_target="tpu_custom_call" | custom-call | flops 137438953472 | bytes 1 | tf_op jit(solution)/shard_map/pallas_call | solution.py:211
  93.9 8.5 %all-to-all-start = ((bf16[4,2,128,256]{3,2,1,0:T(8,128)(2,1)}), bf16[4,2,128,256]{3,2,1,0:T(8,128)(2,1)S(1)}, u32[]{:S(2)}, u32[]{:S(2)}) async-start(bf16[4,2,128,256]{3,2,1,0:T(8,128)(2,1)} %get-tuple-element.22), calls=%async_computation | async-start | bytes 1048576 | tf_op jit(solution)/shard_map/all_to_all | solution.py:386
  102.4 0.0 copy-done.5
  102.4 1.9 collective-permute-start.6
  104.3 6.5 %collective-permute-start.7 = (bf16[2,2,128,512]{3,2,1,0:T(8,128)(2,1)S(1)}, bf16[2,2,128,512]{3,2,1,0:T(8,128)(2,1)S(1)}, u32[]{:S(2)}, u32[]{:S(2)}) collective-permute-start(bf16[2,2,128,512]{3,2,1,0:T(8,128)(2,1)S(1)} %copy-done.5), channel_id=1, source_target_pairs={{2,0},{3,1},{4,2},{5,3},{6,4},{7,5},{8,6},{9,7},{10,8},{11,9},{12,... | collective-permute-start | bytes 1572872 | tf_op jit(solution)/shard_map/T1b/ppermute | solution.py:72
  110.8 0.0 collective-permute-done.4.left_tan
  110.8 0.0 copy-start.6
  110.8 0.0 collective-permute-done.5.right_tan
  110.8 0.0 all-to-all-done.att
  110.8 0.0 copy-start.3
  110.8 0.0 collective-permute-done.9.w_sib
  110.8 0.8 copy-done.3
  111.7 4.7 %shard_map.128 = bf16[8,2,96,256]{3,2,1,0:T(8,128)(2,1)} custom-call(bf16[4,1536,128]{2,1,0:T(8,128)(2,1)} %bitcast.24, bf16[4,1536,128]{2,1,0:T(8,128)(2,1)} %collective-permute-done.9.w_sib, bf16[4,2,128,256]{3,2,1,0:T(8,128)(2,1)} %copy-done.3), custom_call_target="tpu_custom_call" | custom-call | flops 1 | bytes 1 | tf_op jit(solution)/shard_map/pallas_call | solution.py:334
  116.3 11.7 %all-to-all-start.1 = ((bf16[8,2,96,256]{3,2,1,0:T(8,128)(2,1)}), bf16[8,2,96,256]{3,2,1,0:T(8,128)(2,1)S(1)}, u32[]{:S(2)}, u32[]{:S(2)}) async-start(bf16[8,2,96,256]{3,2,1,0:T(8,128)(2,1)} %shard_map.128), calls=%async_computation.1 | async-start | bytes 1572864 | tf_op jit(solution)/shard_map/all_to_all | solution.py:389
  128.1 1.9 collective-permute-done.6.left_tan
  130.0 0.0 collective-permute-done.7.right_tan
  130.0 0.8 copy-done.7
  130.8 0.8 copy-done.8
  131.6 6.3 %shard_map.126.last = bf16[2,128,512]{2,1,0:T(8,128)(2,1)} custom-call(s32[2]{0:T(128)} %pad_add_fusion.meta, bf16[2,2,128,1024]{3,2,1,0:T(8,128)(2,1)} %get-tuple-element.20.q_ref, bf16[2,2,128,1024]{3,2,1,0:T(8,128)(2,1)} %copy-done.1, bf16[2,2,128,1024]{3,2,1,0:T(8,128)(2,1)} %shard_map.123.mid, bf16[2,2,128,1024]{3,2,1,0:T(8,128)(2,1)} %copy-done.2, ...), custom_call_target="tpu_custom_call" | custom-call | flops 1 | bytes 1 | tf_op jit(solution)/shard_map/pallas_call | solution.py:256
  137.9 0.0 copy-done.6
  137.9 6.3 %shard_map.125.first = bf16[2,128,512]{2,1,0:T(8,128)(2,1)} custom-call(s32[2]{0:T(128)} %pad_add_fusion.meta, bf16[2,2,128,1024]{3,2,1,0:T(8,128)(2,1)} %get-tuple-element.20.q_ref, bf16[2,2,128,1024]{3,2,1,0:T(8,128)(2,1)} %copy-done.1, bf16[2,2,128,1024]{3,2,1,0:T(8,128)(2,1)} %shard_map.123.mid, bf16[2,2,128,1024]{3,2,1,0:T(8,128)(2,1)} %copy-done.2, ...), custom_call_target="tpu_custom_call" | custom-call | flops 1 | bytes 1 | tf_op jit(solution)/shard_map/pallas_call | solution.py:256
  144.1 16.8 %all-gather.4.cloned.1.call-done = bf16[2,768,1024]{2,1,0:T(8,128)(2,1)} async-done(((bf16[2,96,1024]{2,1,0:T(8,128)(2,1)}), bf16[2,768,1024]{2,1,0:T(8,128)(2,1)}) %all-gather.4.cloned.1.call-update) | async-done | bytes 3145744 | tf_op jit(solution)/shard_map/all_gather | solution.py:382
  161.0 5.7 %shard_map.127 = (f32[2,2,64,1536]{3,2,1,0:T(8,128)}, f32[2,2,64,1536]{3,2,1,0:T(8,128)}) custom-call(bf16[2,128,1024]{2,1,0:T(8,128)(2,1)} %get-tuple-element.21.att, bf16[2,128,512]{2,1,0:T(8,128)(2,1)} %shard_map.125.first, bf16[2,128,512]{2,1,0:T(8,128)(2,1)} %shard_map.126.last, bf16[1536,1024]{1,0:T(8,128)(2,1)} %bitcast.22, f32[2,1536]{1,0:T(2,128)} %gate.1, ...), custom_call_target="tpu_custom_call" | custom-call | flops 1 | bytes 1 | tf_op jit(solution)/shard_map/pallas_call | solution.py:303
  166.7 2.0 collective-permute-start.8
  168.8 0.0 all-to-all-done.1
  168.8 0.1 convert_reduce_fusion
  168.9 28.3 %all_to_all.15 = f32[8,24,256]{2,1,0:T(8,128)S(1)} all-to-all(f32[8,24,256]{2,1,0:T(8,128)S(1)} %bitcast.27), channel_id=1, replica_groups={{0,2,4,6,256,258,260,262},{1,3,5,7,257,259,261,263},{8,10,12,14,264,266..., dimensions={0} | all-to-all | bytes 393216 | tf_op jit(solution)/shard_map/all_to_all | solution.py:391
  197.2 1.9 collective-permute-start.10
  199.2 10.1 %collective-permute-done.10 = f32[24,256]{1,0:T(8,128)S(1)} collective-permute-done((f32[24,256]{1,0:T(8,128)S(1)}, f32[24,256]{1,0:T(8,128)S(1)}, u32[]{:S(2)}, u32[]{:S(2)}) %collective-permute-start.10) | collective-permute-done | bytes 24608 | tf_op jit(solution)/shard_map/Turn/ppermute | solution.py:72
  209.3 0.0 collective-permute-done.8
  209.3 0.0 copy-done.4
  209.3 2.4 %fusion.3 = (bf16[2,64,1536]{2,1,0:T(8,128)(2,1)}, bf16[2,64,1536]{2,1,0:T(8,128)(2,1)}) fusion(f32[2,2,64,1536]{3,2,1,0:T(8,128)} %collective-permute-done.8, f32[2,2,64,1536]{3,2,1,0:T(8,128)S(1)} %copy-done.4), kind=kLoop, calls=%fused_computation.7 | loop fusion | flops 786432 | bytes 3932160 | tf_op jit(solution)/shard_map/convert_element_type | solution.py:400
  211.7 0.6 copy.21
  (14 shorter events, 0.1 us)
Async XLA Ops:
  7.2 59.2 %all-gather.6.cloned.1.call-start = ((), (), s32[]{:S(2)}) async-start(), calls=%async_computation.4 | async-start | bytes 1966080 | tf_op jit(solution)/shard_map/all_gather | solution.py:378
  7.9 5.2 %copy-start.10 = (f32[2048,24]{0,1:T(8,128)S(1)}, f32[2048,24]{0,1:T(8,128)}, u32[]{:S(2)}) copy-start(f32[2048,24]{0,1:T(8,128)} %param.16) | copy-start | bytes 589828
  7.9 11.7 %copy-start.9 = (bf16[2,64,1536]{2,1,0:T(8,128)(2,1)S(1)}, bf16[2,64,1536]{2,1,0:T(8,128)(2,1)}, u32[]{:S(2)}) copy-start(bf16[2,64,1536]{2,1,0:T(8,128)(2,1)} %param.19) | copy-start | bytes 1179652
  7.9 11.7 %copy-start.11 = (f32[2,1536]{1,0:T(2,128)S(1)}, f32[2,1536]{1,0:T(2,128)}, u32[]{:S(2)}) copy-start(f32[2,1536]{1,0:T(2,128)} %gate.1) | copy-start | bytes 36868
  11.2 8.4 %collective-permute-start = (bf16[6,2,64,1024]{3,2,1,0:T(8,128)(2,1)}, bf16[6,2,64,1024]{3,2,1,0:T(8,128)(2,1)S(1)}, u32[]{:S(2)}, u32[]{:S(2)}) collective-permute-start(bf16[6,2,64,1024]{3,2,1,0:T(8,128)(2,1)} %shard_map.121), channel_id=1, source_target_pairs={{0,1},{1,0},{2,3},{3,2},{4,5},{5,4},{6,7},{7,6},{8,9},{9,8},{10,11... | collective-permute-start | bytes 4718600 | tf_op jit(solution)/shard_map/Sx/ppermute | solution.py:72
  13.5 6.0 %collective-permute-start.1 = (bf16[1,24,1024]{2,1,0:T(8,128)(2,1)S(1)}, bf16[1,24,1024]{2,1,0:T(8,128)(2,1)S(1)}, u32[]{:S(2)}, u32[]{:S(2)}) collective-permute-start(bf16[1,24,1024]{2,1,0:T(8,128)(2,1)S(1)} %bitcast.28), channel_id=1, source_target_pairs={{0,256},{1,257},{2,258},{3,259},{4,260},{5,261},{6,262},{7,263},{8... | collective-permute-start | bytes 147464 | tf_op jit(solution)/shard_map/Wy/ppermute | solution.py:72
  19.6 1.3 copy-start
  20.9 140.1 %all-gather.4.cloned.1.call-start = ((), (), s32[]{:S(2)}) async-start(), calls=%async_computation.3 | async-start | bytes 3538944 | tf_op jit(solution)/shard_map/all_gather | solution.py:382
  23.7 59.8 %collective-permute-start.2 = (bf16[2,2,128,1024]{3,2,1,0:T(8,128)(2,1)}, bf16[2,2,128,1024]{3,2,1,0:T(8,128)(2,1)S(1)}, u32[]{:S(2)}, u32[]{:S(2)}) collective-permute-start(bf16[2,2,128,1024]{3,2,1,0:T(8,128)(2,1)} %shard_map.123.mid), channel_id=1, source_target_pairs={{0,2},{1,3},{2,4},{3,5},{4,6},{5,7},{6,8},{7,9},{8,10},{9,11},{10,... | collective-permute-start | bytes 3145736 | tf_op jit(solution)/shard_map/Ha/ppermute | solution.py:72
  26.4 57.1 %collective-permute-start.3 = (bf16[2,2,128,1024]{3,2,1,0:T(8,128)(2,1)}, bf16[2,2,128,1024]{3,2,1,0:T(8,128)(2,1)S(1)}, u32[]{:S(2)}, u32[]{:S(2)}) collective-permute-start(bf16[2,2,128,1024]{3,2,1,0:T(8,128)(2,1)} %shard_map.123.mid), channel_id=1, source_target_pairs={{2,0},{3,1},{4,2},{5,3},{6,4},{7,5},{8,6},{9,7},{10,8},{11,9},{12,... | collective-permute-start | bytes 3145736 | tf_op jit(solution)/shard_map/Hb/ppermute | solution.py:72
  50.0 60.7 %collective-permute-start.4 = (bf16[2,2,128,512]{3,2,1,0:T(8,128)(2,1)}, bf16[2,2,128,512]{3,2,1,0:T(8,128)(2,1)S(1)}, u32[]{:S(2)}, u32[]{:S(2)}) collective-permute-start(bf16[2,2,128,512]{3,2,1,0:T(8,128)(2,1)} %get-tuple-element.26.mid_tan), channel_id=1, source_target_pairs={{0,2},{1,3},{2,4},{3,5},{4,6},{5,7},{6,8},{7,9},{8,10},{9,11},{10,... | collective-permute-start | bytes 1572872 | tf_op jit(solution)/shard_map/T0a/ppermute | solution.py:72
  64.4 46.4 %collective-permute-start.5 = (bf16[2,2,128,512]{3,2,1,0:T(8,128)(2,1)}, bf16[2,2,128,512]{3,2,1,0:T(8,128)(2,1)}, u32[]{:S(2)}, u32[]{:S(2)}) collective-permute-start(bf16[2,2,128,512]{3,2,1,0:T(8,128)(2,1)} %get-tuple-element.26.mid_tan), channel_id=1, source_target_pairs={{2,0},{3,1},{4,2},{5,3},{6,4},{7,5},{8,6},{9,7},{10,8},{11,9},{12,... | collective-permute-start | bytes 1572872 | tf_op jit(solution)/shard_map/T0b/ppermute | solution.py:72
  66.4 44.4 %collective-permute-start.9 = (bf16[4,1536,128]{2,1,0:T(8,128)(2,1)}, bf16[4,1536,128]{2,1,0:T(8,128)(2,1)}, u32[]{:S(2)}, u32[]{:S(2)}) collective-permute-start(bf16[4,1536,128]{2,1,0:T(8,128)(2,1)} %bitcast.23), channel_id=1, source_target_pairs={{0,1},{1,0},{2,3},{3,2},{4,5},{5,4},{6,7},{7,6},{8,9},{9,8},{10,11... | collective-permute-start | bytes 4718600 | tf_op jit(solution)/shard_map/Cswap/ppermute | solution.py:72
  83.6 1.1 copy-start.1
  83.6 1.4 copy-start.2
  85.0 17.4 %copy-start.5 = (bf16[2,2,128,512]{3,2,1,0:T(8,128)(2,1)S(1)}, bf16[2,2,128,512]{3,2,1,0:T(8,128)(2,1)}, u32[]{:S(2)}) copy-start(bf16[2,2,128,512]{3,2,1,0:T(8,128)(2,1)} %get-tuple-element.29.mid_tan) | copy-start | bytes 1572868
  93.9 16.9 %all-to-all-start = ((bf16[4,2,128,256]{3,2,1,0:T(8,128)(2,1)}), bf16[4,2,128,256]{3,2,1,0:T(8,128)(2,1)S(1)}, u32[]{:S(2)}, u32[]{:S(2)}) async-start(bf16[4,2,128,256]{3,2,1,0:T(8,128)(2,1)} %get-tuple-element.22), calls=%async_computation | async-start | bytes 1048576 | tf_op jit(solution)/shard_map/all_to_all | solution.py:386
  102.4 27.6 %collective-permute-start.6 = (bf16[2,2,128,512]{3,2,1,0:T(8,128)(2,1)S(1)}, bf16[2,2,128,512]{3,2,1,0:T(8,128)(2,1)S(1)}, u32[]{:S(2)}, u32[]{:S(2)}) collective-permute-start(bf16[2,2,128,512]{3,2,1,0:T(8,128)(2,1)S(1)} %copy-done.5), channel_id=1, source_target_pairs={{0,2},{1,3},{2,4},{3,5},{4,6},{5,7},{6,8},{7,9},{8,10},{9,11},{10,... | collective-permute-start | bytes 1572872 | tf_op jit(solution)/shard_map/T1a/ppermute | solution.py:72
  104.3 25.7 %collective-permute-start.7 = (bf16[2,2,128,512]{3,2,1,0:T(8,128)(2,1)S(1)}, bf16[2,2,128,512]{3,2,1,0:T(8,128)(2,1)S(1)}, u32[]{:S(2)}, u32[]{:S(2)}) collective-permute-start(bf16[2,2,128,512]{3,2,1,0:T(8,128)(2,1)S(1)} %copy-done.5), channel_id=1, source_target_pairs={{2,0},{3,1},{4,2},{5,3},{6,4},{7,5},{8,6},{9,7},{10,8},{11,9},{12,... | collective-permute-start | bytes 1572872 | tf_op jit(solution)/shard_map/T1b/ppermute | solution.py:72
  110.8 27.1 %copy-start.6 = (bf16[2,2,128,512]{3,2,1,0:T(8,128)(2,1)}, bf16[2,2,128,512]{3,2,1,0:T(8,128)(2,1)S(1)}, u32[]{:S(2)}) copy-start(bf16[2,2,128,512]{3,2,1,0:T(8,128)(2,1)S(1)} %collective-permute-done.4.left_tan) | copy-start | bytes 1572868
  110.8 0.8 copy-start.3
  116.3 52.4 %all-to-all-start.1 = ((bf16[8,2,96,256]{3,2,1,0:T(8,128)(2,1)}), bf16[8,2,96,256]{3,2,1,0:T(8,128)(2,1)S(1)}, u32[]{:S(2)}, u32[]{:S(2)}) async-start(bf16[8,2,96,256]{3,2,1,0:T(8,128)(2,1)} %shard_map.128), calls=%async_computation.1 | async-start | bytes 1572864 | tf_op jit(solution)/shard_map/all_to_all | solution.py:389
  130.0 0.8 copy-start.7
  130.8 0.8 copy-start.8
  166.7 42.5 %copy-start.4 = (f32[2,2,64,1536]{3,2,1,0:T(8,128)S(1)}, f32[2,2,64,1536]{3,2,1,0:T(8,128)}, u32[]{:S(2)}) copy-start(f32[2,2,64,1536]{3,2,1,0:T(8,128)} %get-tuple-element.30) | copy-start | bytes 4718596
  166.7 42.5 %collective-permute-start.8 = (f32[2,2,64,1536]{3,2,1,0:T(8,128)}, f32[2,2,64,1536]{3,2,1,0:T(8,128)}, u32[]{:S(2)}, u32[]{:S(2)}) collective-permute-start(f32[2,2,64,1536]{3,2,1,0:T(8,128)} %get-tuple-element.31), channel_id=1, source_target_pairs={{0,1},{1,0},{2,3},{3,2},{4,5},{5,4},{6,7},{7,6},{8,9},{9,8},{10,11... | collective-permute-start | bytes 4718600 | tf_op jit(solution)/shard_map/Pswap/ppermute | solution.py:72
  197.2 12.0 %collective-permute-start.10 = (f32[24,256]{1,0:T(8,128)S(1)}, f32[24,256]{1,0:T(8,128)S(1)}, u32[]{:S(2)}, u32[]{:S(2)}) collective-permute-start(f32[24,256]{1,0:T(8,128)S(1)} %reduce_sum.19), channel_id=1, source_target_pairs={{0,0},{1,1},{2,8},{3,9},{4,16},{5,17},{6,24},{7,25},{8,2},{9,3},{1... | collective-permute-start | bytes 73736 | tf_op jit(solution)/shard_map/Turn/ppermute | solution.py:72
Sparse Core Ops, SparseCore 0:
  21.0 37.6 all-gather.5
  66.5 94.4 all-gather.3

commit v6 on v5

--- a/solution.py
+++ b/solution.py
@@ -387,13 +387,15 @@
     (quarter, tans[0][0], tans[0][2]) = after((quarter, tans[0][0], tans[0][2]))
     terms = grad_terms(w_own, w_sib, quarter)
     terms = lax.all_to_all(terms, AXES, 0, 0, axis_index_groups=GROUPS_Z, tiled=True)
+    first = attend_tangent(meta, q_rows, keyed, tans[0], 0)
+    last = attend_tangent(meta, q_rows, keyed, tans[1], 1)
+    terms, first = after((terms, first))
     terms = jnp.sum(terms.astype(F32), axis=0).reshape(NYL * NYH, -1, PAIR)
     terms = lax.all_to_all(terms, AXES, 0, 0, axis_index_groups=GROUPS_Y, tiled=True)
     terms = jnp.sum(terms, axis=0)
     weight_grad = send(terms, TURN, "Turn").T
 
-    first = attend_tangent(meta, q_rows, keyed, tans[0], 0)
-    last = attend_tangent(meta, q_rows, keyed, tans[1], 1)
+    att, _ = after((att, terms))
     here, other = project(att, first, last, weight, gate, gate_tan)
     other = send(other, SWAP_CORE, "Pswap")
     mixed = (here[0] + other[0]).astype(BF)

time: 220 us -> 216 us (0.982)
  the two profiles are of different devices: /device:TPU:40 before, /device:TPU:96 now
where the time goes in v6:
time: 216 us; the launch traced here: 215 us
  starting transfers between devices  89.9 us (42%)
  waiting for transfers between devices  45.9 us (21%)
  Pallas kernels  41.3 us (19%)
  blocking collectives  15 us (7%)
  between operations  14.3 us (7%)
  local copies, waits for them, and re-layouts  4.73 us (2%)
  other arithmetic  3.97 us (2%)
    ppermute x11, starting transfers between devices, send(): return lax.ppermute(array, AXES, pairs)  43.6 us
    ppermute x11, waiting for transfers between devices, send(): return lax.ppermute(array, AXES, pairs)  37.5 us
    all_to_all x1, starting transfers between devices, on_device(): lax.all_to_all(terms, AXES, 0, 0, axis_index_groups=GROUPS_Y, tiled=True)  27.6 us
    all_gather x1, blocking collectives, on_device(): lax.all_gather(low, AXES, axis_index_groups=GROUPS_X, axis=1, tiled=True)  15 us
    all_to_all x1, starting transfers between devices, on_device(): lax.all_to_all(terms, AXES, 0, 0, axis_index_groups=GROUPS_Z, tiled=True)  14.4 us
    pallas_call x2, Pallas kernels, attend_tangent(): pl.pallas_call(tangent_body, out_shape=jax.ShapeDtypeStruct((seqs, rows,...  12.5 us
    pallas_call x1, Pallas kernels, attend(): pl.pallas_call(attend_body, out_shape=[jax.ShapeDtypeStruct((NJ, seqs, ro...  8.77 us
    pallas_call x2, Pallas kernels, join_rows(): pl.pallas_call(functools.partial(join_body, pieces=pieces, first=first),...  6.35 us
  transfers between devices with their start and end apart: 16, of which 7 were waited for; matrix products, arithmetic and copies ran while one was open for 1% of the time, Pallas kernels for 15%

profile of v6, /device:TPU:96, one launch (start us, length us, event | category | flops | bytes accessed | tf_op | source)
XLA Modules:
  0.0 215.1 jit_solution(2170380060143615010)
XLA Ops:
  7.2 0.0 all-gather.6.cloned.1.call-start
  7.2 0.6 pad_add_fusion.meta
  7.8 0.0 copy-start.8
  7.8 0.0 copy-start.10
  7.8 3.3 %shard_map.121 = bf16[6,2,64,1024]{3,2,1,0:T(8,128)(2,1)} custom-call(s32[2]{0:T(128)} %pad_add_fusion.meta, bf16[2,64,2048]{2,1,0:T(8,128)(2,1)} %refs_0_.5, bf16[2,64,2048]{2,1,0:T(8,128)(2,1)} %refs_1_.5, bf16[2,64,2048]{2,1,0:T(8,128)(2,1)} %refs_0_.4, bf16[2,64,2048]{2,1,0:T(8,128)(2,1)} %refs_1_.4, bf16[2,64,2048]{2,1,0:T(8,128)(2,1)} %refs_2_.3, ...), custom_call_target="tpu_custom_call" | custom-call | flops 1 | bytes 1 | tf_op jit(solution)/shard_map/pallas_call | solution.py:131
  11.1 1.9 collective-permute-start
  13.0 0.0 copy-done.9
  13.1 0.3 dynamic-slice_reduce_fusion
  13.5 2.6 %collective-permute-start.1 = (bf16[1,24,1024]{2,1,0:T(8,128)(2,1)S(1)}, bf16[1,24,1024]{2,1,0:T(8,128)(2,1)S(1)}, u32[]{:S(2)}, u32[]{:S(2)}) collective-permute-start(bf16[1,24,1024]{2,1,0:T(8,128)(2,1)S(1)} %bitcast.27), channel_id=1, source_target_pairs={{0,256},{1,257},{2,258},{3,259},{4,260},{5,261},{6,262},{7,263},{8... | collective-permute-start | bytes 147464 | tf_op jit(solution)/shard_map/Wy/ppermute | solution.py:72
  16.1 3.4 %collective-permute-done.1 = bf16[1,24,1024]{2,1,0:T(8,128)(2,1)S(1)} collective-permute-done((bf16[1,24,1024]{2,1,0:T(8,128)(2,1)S(1)}, bf16[1,24,1024]{2,1,0:T(8,128)(2,1)S(1)}, u32[]{:S(2)}, u32[]{:S(2)}) %collective-permute-start.1) | collective-permute-done | bytes 49184 | tf_op jit(solution)/shard_map/Wy/ppermute | solution.py:72
  19.5 0.0 collective-permute-done.refs_4_.refs_2_
  19.5 0.0 copy-done.8
  19.5 0.0 copy-done.10
  19.6 0.0 copy-start
  19.6 0.1 multiply_convert_fusion
  19.6 1.2 copy.17
  20.8 0.0 all-gather.6.cloned.1.call-update
  20.8 0.0 all-gather.4.cloned.1.call-start
  20.9 0.0 copy-done
  20.9 2.8 %shard_map.123.mid = bf16[2,2,128,1024]{3,2,1,0:T(8,128)(2,1)} custom-call(s32[2]{0:T(128)} %pad_add_fusion.meta, bf16[2,64,2048]{2,1,0:T(8,128)(2,1)} %refs_0_.5, bf16[2,64,2048]{2,1,0:T(8,128)(2,1)} %refs_1_.5, bf16[6,2,64,1024]{3,2,1,0:T(8,128)(2,1)} %copy-done), custom_call_target="tpu_custom_call" | custom-call | flops 1 | bytes 1 | tf_op jit(solution)/shard_map/pallas_call | solution.py:159
  23.7 2.7 %collective-permute-start.2 = (bf16[2,2,128,1024]{3,2,1,0:T(8,128)(2,1)}, bf16[2,2,128,1024]{3,2,1,0:T(8,128)(2,1)S(1)}, u32[]{:S(2)}, u32[]{:S(2)}) collective-permute-start(bf16[2,2,128,1024]{3,2,1,0:T(8,128)(2,1)} %shard_map.123.mid), channel_id=1, source_target_pairs={{0,2},{1,3},{2,4},{3,5},{4,6},{5,7},{6,8},{7,9},{8,10},{9,11},{10,... | collective-permute-start | bytes 3145736 | tf_op jit(solution)/shard_map/Ha/ppermute | solution.py:72
  26.4 5.3 %collective-permute-start.3 = (bf16[2,2,128,1024]{3,2,1,0:T(8,128)(2,1)}, bf16[2,2,128,1024]{3,2,1,0:T(8,128)(2,1)S(1)}, u32[]{:S(2)}, u32[]{:S(2)}) collective-permute-start(bf16[2,2,128,1024]{3,2,1,0:T(8,128)(2,1)} %shard_map.123.mid), channel_id=1, source_target_pairs={{2,0},{3,1},{4,2},{5,3},{6,4},{7,5},{8,6},{9,7},{10,8},{11,9},{12,... | collective-permute-start | bytes 3145736 | tf_op jit(solution)/shard_map/Hb/ppermute | solution.py:72
  31.6 3.5 %shard_map.122 = (bf16[2,2,128,1024]{3,2,1,0:T(8,128)(2,1)}, bf16[2,2,128,512]{3,2,1,0:T(8,128)(2,1)}, bf16[2,2,128,512]{3,2,1,0:T(8,128)(2,1)}) custom-call(s32[2]{0:T(128)} %pad_add_fusion.meta, bf16[2,64,2048]{2,1,0:T(8,128)(2,1)} %refs_0_.4, bf16[2,64,2048]{2,1,0:T(8,128)(2,1)} %refs_1_.4, bf16[2,64,2048]{2,1,0:T(8,128)(2,1)} %refs_2_.3, ...), custom_call_target="tpu_custom_call" | custom-call | flops 1 | bytes 1 | tf_op jit(solution)/shard_map/pallas_call | solution.py:159
  35.2 15.0 %all_gather.14 = bf16[2,96,1024]{2,1,0:T(8,128)(2,1)} all-gather(bf16[2,24,1024]{2,1,0:T(8,128)(2,1)S(1)} %maximum_select_fusion), channel_id=1, replica_groups={{0,8,16,24},{1,9,17,25},{32,40,48,56},{33,41,49,57},{64,72,80,88},{65,7..., dimensions={1}, use_global_device_ids=true | all-gather | bytes 491520 | tf_op jit(solution)/shard_map/all_gather | solution.py:371
  50.1 2.2 %collective-permute-start.5 = (bf16[2,2,128,512]{3,2,1,0:T(8,128)(2,1)}, bf16[2,2,128,512]{3,2,1,0:T(8,128)(2,1)S(1)}, u32[]{:S(2)}, u32[]{:S(2)}) collective-permute-start(bf16[2,2,128,512]{3,2,1,0:T(8,128)(2,1)} %get-tuple-element.31.mid_tan), channel_id=1, source_target_pairs={{0,2},{1,3},{2,4},{3,5},{4,6},{5,7},{6,8},{7,9},{8,10},{9,11},{10,... | collective-permute-start | bytes 1572872 | tf_op jit(solution)/shard_map/T0a/ppermute | solution.py:72
  52.4 5.7 %collective-permute-start.6 = (bf16[2,2,128,512]{3,2,1,0:T(8,128)(2,1)}, bf16[2,2,128,512]{3,2,1,0:T(8,128)(2,1)S(1)}, u32[]{:S(2)}, u32[]{:S(2)}) collective-permute-start(bf16[2,2,128,512]{3,2,1,0:T(8,128)(2,1)} %get-tuple-element.31.mid_tan), channel_id=1, source_target_pairs={{2,0},{3,1},{4,2},{5,3},{6,4},{7,5},{8,6},{9,7},{10,8},{11,9},{12,... | collective-permute-start | bytes 1572872 | tf_op jit(solution)/shard_map/T0b/ppermute | solution.py:72
  58.1 0.0 all-gather.4.cloned.1.call-update
  58.1 0.0 all-gather.6.cloned.1.call-done
  58.2 1.9 collective-permute-start.4
  60.1 12.2 %collective-permute-done.2.left = bf16[2,2,128,1024]{3,2,1,0:T(8,128)(2,1)S(1)} collective-permute-done((bf16[2,2,128,1024]{3,2,1,0:T(8,128)(2,1)}, bf16[2,2,128,1024]{3,2,1,0:T(8,128)(2,1)S(1)}, u32[]{:S(2)}, u32[]{:S(2)}) %collective-permute-start.2) | collective-permute-done | bytes 1048608 | tf_op jit(solution)/shard_map/Ha/ppermute | solution.py:72
  72.3 4.6 %collective-permute-done.3.right = bf16[2,2,128,1024]{3,2,1,0:T(8,128)(2,1)S(1)} collective-permute-done((bf16[2,2,128,1024]{3,2,1,0:T(8,128)(2,1)}, bf16[2,2,128,1024]{3,2,1,0:T(8,128)(2,1)S(1)}, u32[]{:S(2)}, u32[]{:S(2)}) %collective-permute-start.3) | collective-permute-done | bytes 1048608 | tf_op jit(solution)/shard_map/Hb/ppermute | solution.py:72
  76.8 0.0 copy-done.1
  76.8 1.0 copy-done.2
  77.8 8.8 %shard_map.124 = (bf16[4,2,128,256]{3,2,1,0:T(8,128)(2,1)}, bf16[2,128,1024]{2,1,0:T(8,128)(2,1)}) custom-call(s32[2]{0:T(128)} %pad_add_fusion.meta, bf16[2,2,128,1024]{3,2,1,0:T(8,128)(2,1)} %get-tuple-element.23.q_ref, bf16[2,2,128,1024]{3,2,1,0:T(8,128)(2,1)} %copy-done.1, bf16[2,2,128,1024]{3,2,1,0:T(8,128)(2,1)} %shard_map.123.mid, ...), custom_call_target="tpu_custom_call" | custom-call | flops 137438953472 | bytes 1 | tf_op jit(solution)/shard_map/pallas_call | solution.py:211
  86.6 4.2 %all-to-all-start = ((bf16[4,2,128,256]{3,2,1,0:T(8,128)(2,1)}), bf16[4,2,128,256]{3,2,1,0:T(8,128)(2,1)S(1)}, u32[]{:S(2)}, u32[]{:S(2)}) async-start(bf16[4,2,128,256]{3,2,1,0:T(8,128)(2,1)} %get-tuple-element.27), calls=%async_computation | async-start | bytes 1048576 | tf_op jit(solution)/shard_map/all_to_all | solution.py:386
  90.8 7.2 %collective-permute-done.5.left_tan = bf16[2,2,128,512]{3,2,1,0:T(8,128)(2,1)S(1)} collective-permute-done((bf16[2,2,128,512]{3,2,1,0:T(8,128)(2,1)}, bf16[2,2,128,512]{3,2,1,0:T(8,128)(2,1)S(1)}, u32[]{:S(2)}, u32[]{:S(2)}) %collective-permute-start.5) | collective-permute-done | bytes 524320 | tf_op jit(solution)/shard_map/T0a/ppermute | solution.py:72
  98.0 0.0 collective-permute-done.6.right_tan
  98.1 2.1 all-to-all-done.att
  100.2 0.0 collective-permute-done.4.w_sib
  100.2 0.8 copy-done.3
  100.9 4.7 %shard_map.125 = bf16[8,2,96,256]{3,2,1,0:T(8,128)(2,1)} custom-call(bf16[4,1536,128]{2,1,0:T(8,128)(2,1)} %bitcast.24, bf16[4,1536,128]{2,1,0:T(8,128)(2,1)} %collective-permute-done.4.w_sib, bf16[4,2,128,256]{3,2,1,0:T(8,128)(2,1)} %copy-done.3), custom_call_target="tpu_custom_call" | custom-call | flops 1 | bytes 1 | tf_op jit(solution)/shard_map/pallas_call | solution.py:334
  105.6 14.4 %all-to-all-start.1 = ((bf16[8,2,96,256]{3,2,1,0:T(8,128)(2,1)}), bf16[8,2,96,256]{3,2,1,0:T(8,128)(2,1)S(1)}, u32[]{:S(2)}, u32[]{:S(2)}) async-start(bf16[8,2,96,256]{3,2,1,0:T(8,128)(2,1)} %shard_map.125), calls=%async_computation.1 | async-start | bytes 1572864 | tf_op jit(solution)/shard_map/all_to_all | solution.py:389
  120.0 0.0 copy-done.4
  120.0 15.6 %collective-permute-start.7 = (bf16[2,2,128,512]{3,2,1,0:T(8,128)(2,1)S(1)}, bf16[2,2,128,512]{3,2,1,0:T(8,128)(2,1)S(1)}, u32[]{:S(2)}, u32[]{:S(2)}) collective-permute-start(bf16[2,2,128,512]{3,2,1,0:T(8,128)(2,1)S(1)} %copy-done.4), channel_id=1, source_target_pairs={{0,2},{1,3},{2,4},{3,5},{4,6},{5,7},{6,8},{7,9},{8,10},{9,11},{10,... | collective-permute-start | bytes 1572872 | tf_op jit(solution)/shard_map/T1a/ppermute | solution.py:72
  135.6 1.9 collective-permute-start.8
  137.5 0.0 copy-done.5
  137.5 0.0 copy-done.6
  137.5 6.3 %shard_map.126.first = bf16[2,128,512]{2,1,0:T(8,128)(2,1)} custom-call(s32[2]{0:T(128)} %pad_add_fusion.meta, bf16[2,2,128,1024]{3,2,1,0:T(8,128)(2,1)} %get-tuple-element.23.q_ref, bf16[2,2,128,1024]{3,2,1,0:T(8,128)(2,1)} %copy-done.1, bf16[2,2,128,1024]{3,2,1,0:T(8,128)(2,1)} %shard_map.123.mid, bf16[2,2,128,1024]{3,2,1,0:T(8,128)(2,1)} %copy-done.2, ...), custom_call_target="tpu_custom_call" | custom-call | flops 1 | bytes 1 | tf_op jit(solution)/shard_map/pallas_call | solution.py:256
  143.8 6.2 %all-to-all-done.1 = bf16[8,2,96,256]{3,2,1,0:T(8,128)(2,1)S(1)} async-done(((bf16[8,2,96,256]{3,2,1,0:T(8,128)(2,1)}), bf16[8,2,96,256]{3,2,1,0:T(8,128)(2,1)S(1)}, u32[]{:S(2)}, u32[]{:S(2)}) %all-to-all-start.1) | async-done | bytes 786464 | tf_op jit(solution)/shard_map/all_to_all | solution.py:389
  150.0 0.8 convert_reduce_fusion
  150.8 27.6 %all-to-all-start.2 = ((f32[8,24,256]{2,1,0:T(8,128)}), f32[8,24,256]{2,1,0:T(8,128)S(1)}, u32[]{:S(2)}, u32[]{:S(2)}) async-start(f32[8,24,256]{2,1,0:T(8,128)} %bitcast.8), calls=%async_computation.2 | async-start | bytes 393216 | tf_op jit(solution)/shard_map/all_to_all | solution.py:394
  178.4 0.0 collective-permute-done.7.left_tan
  178.4 0.0 collective-permute-done.8.right_tan
  178.4 0.8 copy-done.7
  179.2 6.3 %shard_map.127.last = bf16[2,128,512]{2,1,0:T(8,128)(2,1)} custom-call(s32[2]{0:T(128)} %pad_add_fusion.meta, bf16[2,2,128,1024]{3,2,1,0:T(8,128)(2,1)} %get-tuple-element.23.q_ref, bf16[2,2,128,1024]{3,2,1,0:T(8,128)(2,1)} %copy-done.1, bf16[2,2,128,1024]{3,2,1,0:T(8,128)(2,1)} %shard_map.123.mid, bf16[2,2,128,1024]{3,2,1,0:T(8,128)(2,1)} %copy-done.2, ...), custom_call_target="tpu_custom_call" | custom-call | flops 1 | bytes 1 | tf_op jit(solution)/shard_map/pallas_call | solution.py:256
  185.5 0.0 all-to-all-done.2
  185.5 0.0 all-gather.4.cloned.1.call-done
  185.5 5.7 %shard_map.128 = (f32[2,2,64,1536]{3,2,1,0:T(8,128)}, f32[2,2,64,1536]{3,2,1,0:T(8,128)}) custom-call(bf16[2,128,1024]{2,1,0:T(8,128)(2,1)} %get-tuple-element.36.att, bf16[2,128,512]{2,1,0:T(8,128)(2,1)} %shard_map.126.first, bf16[2,128,512]{2,1,0:T(8,128)(2,1)} %shard_map.127.last, bf16[1536,1024]{1,0:T(8,128)(2,1)} %bitcast.22, f32[2,1536]{1,0:T(2,128)} %gate.1, ...), custom_call_target="tpu_custom_call" | custom-call | flops 1 | bytes 1 | tf_op jit(solution)/shard_map/pallas_call | solution.py:303
  191.2 1.9 collective-permute-start.9
  193.1 1.9 collective-permute-start.10
  195.0 10.1 %collective-permute-done.10 = f32[24,256]{1,0:T(8,128)S(1)} collective-permute-done((f32[24,256]{1,0:T(8,128)S(1)}, f32[24,256]{1,0:T(8,128)S(1)}, u32[]{:S(2)}, u32[]{:S(2)}) %collective-permute-start.10) | collective-permute-done | bytes 24608 | tf_op jit(solution)/shard_map/Turn/ppermute | solution.py:72
  205.1 0.0 collective-permute-done.9
  205.1 2.5 %fusion.3 = (bf16[2,64,1536]{2,1,0:T(8,128)(2,1)}, bf16[2,64,1536]{2,1,0:T(8,128)(2,1)}) fusion(f32[2,2,64,1536]{3,2,1,0:T(8,128)S(1)} %collective-permute-done.9, f32[2,2,64,1536]{3,2,1,0:T(8,128)} %get-tuple-element.39), kind=kLoop, calls=%fused_computation.7 | loop fusion | flops 786432 | bytes 3932160 | tf_op jit(solution)/shard_map/convert_element_type | solution.py:402
  207.6 0.6 copy.21
  (13 shorter events, 0.1 us)
Async XLA Ops:
  7.2 51.0 %all-gather.6.cloned.1.call-start = ((), (), s32[]{:S(2)}) async-start(), calls=%async_computation.4 | async-start | bytes 1966080 | tf_op jit(solution)/shard_map/all_gather | solution.py:378
  7.8 5.2 %copy-start.9 = (f32[2048,24]{0,1:T(8,128)S(1)}, f32[2048,24]{0,1:T(8,128)}, u32[]{:S(2)}) copy-start(f32[2048,24]{0,1:T(8,128)} %param.16) | copy-start | bytes 589828
  7.8 11.7 %copy-start.8 = (bf16[2,64,1536]{2,1,0:T(8,128)(2,1)S(1)}, bf16[2,64,1536]{2,1,0:T(8,128)(2,1)}, u32[]{:S(2)}) copy-start(bf16[2,64,1536]{2,1,0:T(8,128)(2,1)} %param.19) | copy-start | bytes 1179652
  7.8 11.7 %copy-start.10 = (f32[2,1536]{1,0:T(2,128)S(1)}, f32[2,1536]{1,0:T(2,128)}, u32[]{:S(2)}) copy-start(f32[2,1536]{1,0:T(2,128)} %gate.1) | copy-start | bytes 36868
  11.1 8.4 %collective-permute-start = (bf16[6,2,64,1024]{3,2,1,0:T(8,128)(2,1)}, bf16[6,2,64,1024]{3,2,1,0:T(8,128)(2,1)S(1)}, u32[]{:S(2)}, u32[]{:S(2)}) collective-permute-start(bf16[6,2,64,1024]{3,2,1,0:T(8,128)(2,1)} %shard_map.121), channel_id=1, source_target_pairs={{0,1},{1,0},{2,3},{3,2},{4,5},{5,4},{6,7},{7,6},{8,9},{9,8},{10,11... | collective-permute-start | bytes 4718600 | tf_op jit(solution)/shard_map/Sx/ppermute | solution.py:72
  13.5 6.0 %collective-permute-start.1 = (bf16[1,24,1024]{2,1,0:T(8,128)(2,1)S(1)}, bf16[1,24,1024]{2,1,0:T(8,128)(2,1)S(1)}, u32[]{:S(2)}, u32[]{:S(2)}) collective-permute-start(bf16[1,24,1024]{2,1,0:T(8,128)(2,1)S(1)} %bitcast.27), channel_id=1, source_target_pairs={{0,256},{1,257},{2,258},{3,259},{4,260},{5,261},{6,262},{7,263},{8... | collective-permute-start | bytes 147464 | tf_op jit(solution)/shard_map/Wy/ppermute | solution.py:72
  19.6 1.3 copy-start
  20.8 164.7 %all-gather.4.cloned.1.call-start = ((), (), s32[]{:S(2)}) async-start(), calls=%async_computation.3 | async-start | bytes 3538944 | tf_op jit(solution)/shard_map/all_gather | solution.py:382
  23.7 48.6 %collective-permute-start.2 = (bf16[2,2,128,1024]{3,2,1,0:T(8,128)(2,1)}, bf16[2,2,128,1024]{3,2,1,0:T(8,128)(2,1)S(1)}, u32[]{:S(2)}, u32[]{:S(2)}) collective-permute-start(bf16[2,2,128,1024]{3,2,1,0:T(8,128)(2,1)} %shard_map.123.mid), channel_id=1, source_target_pairs={{0,2},{1,3},{2,4},{3,5},{4,6},{5,7},{6,8},{7,9},{8,10},{9,11},{10,... | collective-permute-start | bytes 3145736 | tf_op jit(solution)/shard_map/Ha/ppermute | solution.py:72
  26.4 50.5 %collective-permute-start.3 = (bf16[2,2,128,1024]{3,2,1,0:T(8,128)(2,1)}, bf16[2,2,128,1024]{3,2,1,0:T(8,128)(2,1)S(1)}, u32[]{:S(2)}, u32[]{:S(2)}) collective-permute-start(bf16[2,2,128,1024]{3,2,1,0:T(8,128)(2,1)} %shard_map.123.mid), channel_id=1, source_target_pairs={{2,0},{3,1},{4,2},{5,3},{6,4},{7,5},{8,6},{9,7},{10,8},{11,9},{12,... | collective-permute-start | bytes 3145736 | tf_op jit(solution)/shard_map/Hb/ppermute | solution.py:72
  50.1 47.9 %collective-permute-start.5 = (bf16[2,2,128,512]{3,2,1,0:T(8,128)(2,1)}, bf16[2,2,128,512]{3,2,1,0:T(8,128)(2,1)S(1)}, u32[]{:S(2)}, u32[]{:S(2)}) collective-permute-start(bf16[2,2,128,512]{3,2,1,0:T(8,128)(2,1)} %get-tuple-element.31.mid_tan), channel_id=1, source_target_pairs={{0,2},{1,3},{2,4},{3,5},{4,6},{5,7},{6,8},{7,9},{8,10},{9,11},{10,... | collective-permute-start | bytes 1572872 | tf_op jit(solution)/shard_map/T0a/ppermute | solution.py:72
  52.4 45.7 %collective-permute-start.6 = (bf16[2,2,128,512]{3,2,1,0:T(8,128)(2,1)}, bf16[2,2,128,512]{3,2,1,0:T(8,128)(2,1)S(1)}, u32[]{:S(2)}, u32[]{:S(2)}) collective-permute-start(bf16[2,2,128,512]{3,2,1,0:T(8,128)(2,1)} %get-tuple-element.31.mid_tan), channel_id=1, source_target_pairs={{2,0},{3,1},{4,2},{5,3},{6,4},{7,5},{8,6},{9,7},{10,8},{11,9},{12,... | collective-permute-start | bytes 1572872 | tf_op jit(solution)/shard_map/T0b/ppermute | solution.py:72
  58.2 42.0 %collective-permute-start.4 = (bf16[4,1536,128]{2,1,0:T(8,128)(2,1)}, bf16[4,1536,128]{2,1,0:T(8,128)(2,1)}, u32[]{:S(2)}, u32[]{:S(2)}) collective-permute-start(bf16[4,1536,128]{2,1,0:T(8,128)(2,1)} %bitcast.23), channel_id=1, source_target_pairs={{0,1},{1,0},{2,3},{3,2},{4,5},{5,4},{6,7},{7,6},{8,9},{9,8},{10,11... | collective-permute-start | bytes 4718600 | tf_op jit(solution)/shard_map/Cswap/ppermute | solution.py:72
  72.3 4.6 %copy-start.1 = (bf16[2,2,128,1024]{3,2,1,0:T(8,128)(2,1)}, bf16[2,2,128,1024]{3,2,1,0:T(8,128)(2,1)S(1)}, u32[]{:S(2)}) copy-start(bf16[2,2,128,1024]{3,2,1,0:T(8,128)(2,1)S(1)} %collective-permute-done.2.left) | copy-start | bytes 3145732
  76.8 1.0 copy-start.2
  86.6 13.5 %all-to-all-start = ((bf16[4,2,128,256]{3,2,1,0:T(8,128)(2,1)}), bf16[4,2,128,256]{3,2,1,0:T(8,128)(2,1)S(1)}, u32[]{:S(2)}, u32[]{:S(2)}) async-start(bf16[4,2,128,256]{3,2,1,0:T(8,128)(2,1)} %get-tuple-element.27), calls=%async_computation | async-start | bytes 1048576 | tf_op jit(solution)/shard_map/all_to_all | solution.py:386
  90.8 29.1 %copy-start.4 = (bf16[2,2,128,512]{3,2,1,0:T(8,128)(2,1)S(1)}, bf16[2,2,128,512]{3,2,1,0:T(8,128)(2,1)}, u32[]{:S(2)}) copy-start(bf16[2,2,128,512]{3,2,1,0:T(8,128)(2,1)} %get-tuple-element.38.mid_tan) | copy-start | bytes 1572868
  98.0 39.4 %copy-start.5 = (bf16[2,2,128,512]{3,2,1,0:T(8,128)(2,1)}, bf16[2,2,128,512]{3,2,1,0:T(8,128)(2,1)S(1)}, u32[]{:S(2)}) copy-start(bf16[2,2,128,512]{3,2,1,0:T(8,128)(2,1)S(1)} %collective-permute-done.5.left_tan) | copy-start | bytes 1572868
  98.0 39.5 %copy-start.6 = (bf16[2,2,128,512]{3,2,1,0:T(8,128)(2,1)}, bf16[2,2,128,512]{3,2,1,0:T(8,128)(2,1)S(1)}, u32[]{:S(2)}) copy-start(bf16[2,2,128,512]{3,2,1,0:T(8,128)(2,1)S(1)} %collective-permute-done.6.right_tan) | copy-start | bytes 1572868
  100.1 0.8 copy-start.3
  105.6 44.4 %all-to-all-start.1 = ((bf16[8,2,96,256]{3,2,1,0:T(8,128)(2,1)}), bf16[8,2,96,256]{3,2,1,0:T(8,128)(2,1)S(1)}, u32[]{:S(2)}, u32[]{:S(2)}) async-start(bf16[8,2,96,256]{3,2,1,0:T(8,128)(2,1)} %shard_map.125), calls=%async_computation.1 | async-start | bytes 1572864 | tf_op jit(solution)/shard_map/all_to_all | solution.py:389
  120.0 58.4 %collective-permute-start.7 = (bf16[2,2,128,512]{3,2,1,0:T(8,128)(2,1)S(1)}, bf16[2,2,128,512]{3,2,1,0:T(8,128)(2,1)S(1)}, u32[]{:S(2)}, u32[]{:S(2)}) collective-permute-start(bf16[2,2,128,512]{3,2,1,0:T(8,128)(2,1)S(1)} %copy-done.4), channel_id=1, source_target_pairs={{0,2},{1,3},{2,4},{3,5},{4,6},{5,7},{6,8},{7,9},{8,10},{9,11},{10,... | collective-permute-start | bytes 1572872 | tf_op jit(solution)/shard_map/T1a/ppermute | solution.py:72
  135.6 42.8 %collective-permute-start.8 = (bf16[2,2,128,512]{3,2,1,0:T(8,128)(2,1)S(1)}, bf16[2,2,128,512]{3,2,1,0:T(8,128)(2,1)}, u32[]{:S(2)}, u32[]{:S(2)}) collective-permute-start(bf16[2,2,128,512]{3,2,1,0:T(8,128)(2,1)S(1)} %copy-done.4), channel_id=1, source_target_pairs={{2,0},{3,1},{4,2},{5,3},{6,4},{7,5},{8,6},{9,7},{10,8},{11,9},{12,... | collective-permute-start | bytes 1572872 | tf_op jit(solution)/shard_map/T1b/ppermute | solution.py:72
  150.8 34.7 %all-to-all-start.2 = ((f32[8,24,256]{2,1,0:T(8,128)}), f32[8,24,256]{2,1,0:T(8,128)S(1)}, u32[]{:S(2)}, u32[]{:S(2)}) async-start(f32[8,24,256]{2,1,0:T(8,128)} %bitcast.8), calls=%async_computation.2 | async-start | bytes 393216 | tf_op jit(solution)/shard_map/all_to_all | solution.py:394
  178.4 0.8 copy-start.7
  191.2 13.9 %collective-permute-start.9 = (f32[2,2,64,1536]{3,2,1,0:T(8,128)}, f32[2,2,64,1536]{3,2,1,0:T(8,128)S(1)}, u32[]{:S(2)}, u32[]{:S(2)}) collective-permute-start(f32[2,2,64,1536]{3,2,1,0:T(8,128)} %get-tuple-element.40), channel_id=1, source_target_pairs={{0,1},{1,0},{2,3},{3,2},{4,5},{5,4},{6,7},{7,6},{8,9},{9,8},{10,11... | collective-permute-start | bytes 4718600 | tf_op jit(solution)/shard_map/Pswap/ppermute | solution.py:72
  193.1 12.0 %collective-permute-start.10 = (f32[24,256]{1,0:T(8,128)S(1)}, f32[24,256]{1,0:T(8,128)S(1)}, u32[]{:S(2)}, u32[]{:S(2)}) collective-permute-start(f32[24,256]{1,0:T(8,128)S(1)} %reduce_sum.19), channel_id=1, source_target_pairs={{0,0},{1,1},{2,8},{3,9},{4,16},{5,17},{6,24},{7,25},{8,2},{9,3},{1... | collective-permute-start | bytes 73736 | tf_op jit(solution)/shard_map/Turn/ppermute | solution.py:72
Sparse Core Ops, SparseCore 0:
  20.9 37.0 all-gather.5
  60.1 99.4 all-gather.3

commit v7 on v5

--- a/solution.py
+++ b/solution.py
@@ -60,6 +60,10 @@
 GROUPS_Z = [
     [device_of(x, yl, yh, z, c) for z in range(NZ)]
     for yl in range(NYL) for yh in range(NYH) for x in range(NX) for c in range(NC)
+]
+GROUPS_ZYL = [
+    [device_of(x, yl, yh, z, c) for yl in range(NYL) for z in range(NZ)]
+    for yh in range(NYH) for x in range(NX) for c in range(NC)
 ]
 GROUPS_Y = [
     [device_of(x, yl, yh, z, c) for yl in range(NYL) for yh in range(NYH)]
@@ -361,14 +365,13 @@
     got = send(split_groups(meta, arrays), SWAP_CORE, "Sx")
     low = weight_out.astype(BF).reshape(NJ, NC, PAIR, -1)
     low = lax.dynamic_index_in_dim(low, core, 1, keepdims=False).reshape(GROUP, -1).T
-    low = in_order(low[None], send(low[None], SWAP_YLO, "Wy"), yl_at)
-    got, low = after((got, low))
+    low = jnp.broadcast_to(low[None], (NYL * NZ,) + low.shape)
+    low = lax.all_to_all(low, AXES, 0, 0, axis_index_groups=GROUPS_ZYL, tiled=True)
     (kv,) = join_rows(meta, arrays[:2], got, (((0, 1), (0, NJ)),), 0)
     keyed = (send(kv, TO_NEXT, "Ha"), kv, send(kv, TO_PREV, "Hb"))
     q_rows, *tans = join_rows(
         meta, arrays[2:], got, (((0, 1), (0, NJ)),) + tuple(((2, 3), p) for p in PIECES), 2
     )
-    low = lax.all_gather(low, AXES, axis_index_groups=GROUPS_X, axis=1, tiled=True)
     *tans, _ = after((*tans, low))
     tans = [[send(t, TO_NEXT, "T%da" % n), t, send(t, TO_PREV, "T%db" % n)] for n, t in enumerate(tans)]
 
@@ -379,7 +382,7 @@
     w_own, _ = after((w_own, kv))
     w_sib = send(w_own, SWAP_CORE, "Cswap")
 
-    weight = lax.all_gather(low, AXES, axis_index_groups=GROUPS_Z, axis=1, tiled=True)
+    weight = lax.all_gather(low, AXES, axis_index_groups=GROUPS_X, axis=1, tiled=True)
     weight = weight.reshape(-1, GROUP)
 
     quarter, att = attend(meta, q_rows, keyed)

time: 220 us -> 210 us (0.955)
  the two profiles are of different devices: /device:TPU:40 before, /device:TPU:30 now
where the time goes in v7:
time: 210 us; the launch traced here: 209 us
  starting transfers between devices  67.9 us (32%)
  waiting for transfers between devices  52.5 us (25%)
  Pallas kernels  41.4 us (20%)
  blocking collectives  22.3 us (11%)
  between operations  14.3 us (7%)
  local copies, waits for them, and re-layouts  7.5 us (4%)
  other arithmetic  3.25 us (2%)
    ppermute x10, starting transfers between devices, send(): return lax.ppermute(array, AXES, pairs)  42 us
    all_to_all x1, waiting for transfers between devices, on_device(): lax.all_to_all(low, AXES, 0, 0, axis_index_groups=GROUPS_ZYL, tiled=True)  27.2 us
    all_to_all x1, blocking collectives, on_device(): lax.all_to_all(terms, AXES, 0, 0, axis_index_groups=GROUPS_Y, tiled=True)  22.3 us
    ppermute x10, waiting for transfers between devices, send(): return lax.ppermute(array, AXES, pairs)  19.1 us
    pallas_call x2, Pallas kernels, attend_tangent(): pl.pallas_call(tangent_body, out_shape=jax.ShapeDtypeStruct((seqs, rows,...  12.5 us
    all_to_all x1, starting transfers between devices, on_device(): lax.all_to_all(low, AXES, 0, 0, axis_index_groups=GROUPS_ZYL, tiled=True)  11.8 us
    all_to_all x1, starting transfers between devices, on_device(): lax.all_to_all(terms, AXES, 0, 0, axis_index_groups=GROUPS_Z, tiled=True)  9.19 us
    pallas_call x1, Pallas kernels, attend(): pl.pallas_call(attend_body, out_shape=[jax.ShapeDtypeStruct((NJ, seqs, ro...  8.91 us
  transfers between devices with their start and end apart: 15, of which 6 were waited for; matrix products, arithmetic and copies ran while one was open for 1% of the time, Pallas kernels for 18%

profile of v7, /device:TPU:30, one launch (start us, length us, event | category | flops | bytes accessed | tf_op | source)
XLA Modules:
  0.0 209.0 jit_solution(12253952399761284352)
XLA Ops:
  7.2 0.0 all-gather.6.cloned.1.call-start
  7.2 0.6 pad_add_fusion.meta
  7.9 3.3 %shard_map.121 = bf16[6,2,64,1024]{3,2,1,0:T(8,128)(2,1)} custom-call(s32[2]{0:T(128)} %pad_add_fusion.meta, bf16[2,64,2048]{2,1,0:T(8,128)(2,1)} %refs_0_.5, bf16[2,64,2048]{2,1,0:T(8,128)(2,1)} %refs_1_.5, bf16[2,64,2048]{2,1,0:T(8,128)(2,1)} %refs_0_.4, bf16[2,64,2048]{2,1,0:T(8,128)(2,1)} %refs_1_.4, bf16[2,64,2048]{2,1,0:T(8,128)(2,1)} %refs_2_.3, ...), custom_call_target="tpu_custom_call" | custom-call | flops 1 | bytes 1 | tf_op jit(solution)/shard_map/pallas_call | solution.py:135
  11.2 2.0 collective-permute-start
  13.2 3.6 %collective-permute-done.refs_4_.refs_2_ = bf16[6,2,64,1024]{3,2,1,0:T(8,128)(2,1)S(1)} collective-permute-done((bf16[6,2,64,1024]{3,2,1,0:T(8,128)(2,1)}, bf16[6,2,64,1024]{3,2,1,0:T(8,128)(2,1)S(1)}, u32[]{:S(2)}, u32[]{:S(2)}) %collective-permute-start) | collective-permute-done | bytes 1572896 | tf_op jit(solution)/shard_map/Sx/ppermute | solution.py:76
  16.8 0.0 copy-done.10
  16.8 0.0 copy-done.12
  16.8 0.1 multiply_convert_fusion
  16.9 1.2 copy.17
  18.1 0.0 all-gather.6.cloned.1.call-update
  18.1 0.0 copy-done.11
  18.2 0.3 dynamic-slice_reduce_fusion
  18.5 1.0 broadcast_in_dim.2
  19.5 0.0 copy-done
  19.5 11.8 %all-to-all-start.1 = ((bf16[16,24,1024]{2,1,0:T(8,128)(2,1)}), bf16[16,24,1024]{2,1,0:T(8,128)(2,1)S(1)}, u32[]{:S(2)}, u32[]{:S(2)}) async-start(bf16[16,24,1024]{2,1,0:T(8,128)(2,1)} %broadcast_in_dim.2), calls=%async_computation.1 | async-start | bytes 1572864 | tf_op jit(solution)/shard_map/all_to_all | solution.py:369
  31.3 0.0 all-gather.4.cloned.1.call-start
  31.4 2.8 %shard_map.123.mid = bf16[2,2,128,1024]{3,2,1,0:T(8,128)(2,1)} custom-call(s32[2]{0:T(128)} %pad_add_fusion.meta, bf16[2,64,2048]{2,1,0:T(8,128)(2,1)} %refs_0_.5, bf16[2,64,2048]{2,1,0:T(8,128)(2,1)} %refs_1_.5, bf16[6,2,64,1024]{3,2,1,0:T(8,128)(2,1)} %copy-done), custom_call_target="tpu_custom_call" | custom-call | flops 1 | bytes 1 | tf_op jit(solution)/shard_map/pallas_call | solution.py:163
  34.2 4.8 %collective-permute-start.1 = (bf16[2,2,128,1024]{3,2,1,0:T(8,128)(2,1)}, bf16[2,2,128,1024]{3,2,1,0:T(8,128)(2,1)S(1)}, u32[]{:S(2)}, u32[]{:S(2)}) collective-permute-start(bf16[2,2,128,1024]{3,2,1,0:T(8,128)(2,1)} %shard_map.123.mid), channel_id=1, source_target_pairs={{0,2},{1,3},{2,4},{3,5},{4,6},{5,7},{6,8},{7,9},{8,10},{9,11},{10,... | collective-permute-start | bytes 3145736 | tf_op jit(solution)/shard_map/Ha/ppermute | solution.py:76
  39.0 1.9 collective-permute-start.2
  40.9 27.2 %all-to-all-done.1 = bf16[16,24,1024]{2,1,0:T(8,128)(2,1)S(1)} async-done(((bf16[16,24,1024]{2,1,0:T(8,128)(2,1)}), bf16[16,24,1024]{2,1,0:T(8,128)(2,1)S(1)}, u32[]{:S(2)}, u32[]{:S(2)}) %all-to-all-start.1) | async-done | bytes 786464 | tf_op jit(solution)/shard_map/all_to_all | solution.py:369
  68.1 0.9 copy-done.3
  69.0 0.0 all-gather.4.cloned.1.call-update
  69.0 3.5 %shard_map.122 = (bf16[2,2,128,1024]{3,2,1,0:T(8,128)(2,1)}, bf16[2,2,128,512]{3,2,1,0:T(8,128)(2,1)}, bf16[2,2,128,512]{3,2,1,0:T(8,128)(2,1)}) custom-call(s32[2]{0:T(128)} %pad_add_fusion.meta, bf16[2,64,2048]{2,1,0:T(8,128)(2,1)} %refs_0_.4, bf16[2,64,2048]{2,1,0:T(8,128)(2,1)} %refs_1_.4, bf16[2,64,2048]{2,1,0:T(8,128)(2,1)} %refs_2_.3, ...), custom_call_target="tpu_custom_call" | custom-call | flops 1 | bytes 1 | tf_op jit(solution)/shard_map/pallas_call | solution.py:163
  72.6 4.8 %collective-permute-start.3 = (bf16[2,2,128,512]{3,2,1,0:T(8,128)(2,1)}, bf16[2,2,128,512]{3,2,1,0:T(8,128)(2,1)S(1)}, u32[]{:S(2)}, u32[]{:S(2)}) collective-permute-start(bf16[2,2,128,512]{3,2,1,0:T(8,128)(2,1)} %get-tuple-element.22.mid_tan), channel_id=1, source_target_pairs={{0,2},{1,3},{2,4},{3,5},{4,6},{5,7},{6,8},{7,9},{8,10},{9,11},{10,... | collective-permute-start | bytes 1572872 | tf_op jit(solution)/shard_map/T0a/ppermute | solution.py:76
  77.4 12.9 %collective-permute-start.4 = (bf16[2,2,128,512]{3,2,1,0:T(8,128)(2,1)}, bf16[2,2,128,512]{3,2,1,0:T(8,128)(2,1)}, u32[]{:S(2)}, u32[]{:S(2)}) collective-permute-start(bf16[2,2,128,512]{3,2,1,0:T(8,128)(2,1)} %get-tuple-element.22.mid_tan), channel_id=1, source_target_pairs={{2,0},{3,1},{4,2},{5,3},{6,4},{7,5},{8,6},{9,7},{10,8},{11,9},{12,... | collective-permute-start | bytes 1572872 | tf_op jit(solution)/shard_map/T0b/ppermute | solution.py:76
  90.3 0.0 all-gather.6.cloned.1.call-done
  90.3 1.9 collective-permute-start.8
  92.2 0.0 collective-permute-done.1.left
  92.2 0.0 copy-start.1
  92.2 8.4 %collective-permute-done.2.right = bf16[2,2,128,1024]{3,2,1,0:T(8,128)(2,1)S(1)} collective-permute-done((bf16[2,2,128,1024]{3,2,1,0:T(8,128)(2,1)}, bf16[2,2,128,1024]{3,2,1,0:T(8,128)(2,1)S(1)}, u32[]{:S(2)}, u32[]{:S(2)}) %collective-permute-start.2) | collective-permute-done | bytes 1048608 | tf_op jit(solution)/shard_map/Hb/ppermute | solution.py:76
  100.6 0.0 copy-done.1
  100.6 1.0 copy-done.2
  101.6 8.9 %shard_map.124 = (bf16[4,2,128,256]{3,2,1,0:T(8,128)(2,1)}, bf16[2,128,1024]{2,1,0:T(8,128)(2,1)}) custom-call(s32[2]{0:T(128)} %pad_add_fusion.meta, bf16[2,2,128,1024]{3,2,1,0:T(8,128)(2,1)} %get-tuple-element.17.q_ref, bf16[2,2,128,1024]{3,2,1,0:T(8,128)(2,1)} %copy-done.1, bf16[2,2,128,1024]{3,2,1,0:T(8,128)(2,1)} %shard_map.123.mid, ...), custom_call_target="tpu_custom_call" | custom-call | flops 137438953472 | bytes 1 | tf_op jit(solution)/shard_map/pallas_call | solution.py:215
  110.6 4.8 %all-to-all-start = ((bf16[4,2,128,256]{3,2,1,0:T(8,128)(2,1)}), bf16[4,2,128,256]{3,2,1,0:T(8,128)(2,1)S(1)}, u32[]{:S(2)}, u32[]{:S(2)}) async-start(bf16[4,2,128,256]{3,2,1,0:T(8,128)(2,1)} %get-tuple-element.19), calls=%async_computation | async-start | bytes 1048576 | tf_op jit(solution)/shard_map/all_to_all | solution.py:389
  115.3 0.0 copy-done.7
  115.3 3.3 %collective-permute-start.5 = (bf16[2,2,128,512]{3,2,1,0:T(8,128)(2,1)S(1)}, bf16[2,2,128,512]{3,2,1,0:T(8,128)(2,1)S(1)}, u32[]{:S(2)}, u32[]{:S(2)}) collective-permute-start(bf16[2,2,128,512]{3,2,1,0:T(8,128)(2,1)S(1)} %copy-done.7), channel_id=1, source_target_pairs={{0,2},{1,3},{2,4},{3,5},{4,6},{5,7},{6,8},{7,9},{8,10},{9,11},{10,... | collective-permute-start | bytes 1572872 | tf_op jit(solution)/shard_map/T1a/ppermute | solution.py:76
  118.6 3.4 %collective-permute-start.6 = (bf16[2,2,128,512]{3,2,1,0:T(8,128)(2,1)S(1)}, bf16[2,2,128,512]{3,2,1,0:T(8,128)(2,1)S(1)}, u32[]{:S(2)}, u32[]{:S(2)}) collective-permute-start(bf16[2,2,128,512]{3,2,1,0:T(8,128)(2,1)S(1)} %copy-done.7), channel_id=1, source_target_pairs={{2,0},{3,1},{4,2},{5,3},{6,4},{7,5},{8,6},{9,7},{10,8},{11,9},{12,... | collective-permute-start | bytes 1572872 | tf_op jit(solution)/shard_map/T1b/ppermute | solution.py:76
  122.1 0.0 collective-permute-done.3.left_tan
  122.1 0.0 copy-start.6
  122.1 0.0 collective-permute-done.4.right_tan
  122.1 5.1 %all-to-all-done.att = bf16[4,2,128,256]{3,2,1,0:T(8,128)(2,1)S(1)} async-done(((bf16[4,2,128,256]{3,2,1,0:T(8,128)(2,1)}), bf16[4,2,128,256]{3,2,1,0:T(8,128)(2,1)S(1)}, u32[]{:S(2)}, u32[]{:S(2)}) %all-to-all-start) | async-done | bytes 524320 | tf_op jit(solution)/shard_map/all_to_all | solution.py:389
  127.2 0.0 collective-permute-done.8.w_sib
  127.2 0.8 copy-done.4
  128.0 4.7 %shard_map.128 = bf16[8,2,96,256]{3,2,1,0:T(8,128)(2,1)} custom-call(bf16[4,1536,128]{2,1,0:T(8,128)(2,1)} %bitcast.22, bf16[4,1536,128]{2,1,0:T(8,128)(2,1)} %collective-permute-done.8.w_sib, bf16[4,2,128,256]{3,2,1,0:T(8,128)(2,1)} %copy-done.4), custom_call_target="tpu_custom_call" | custom-call | flops 1 | bytes 1 | tf_op jit(solution)/shard_map/pallas_call | solution.py:338
  132.7 9.2 %all-to-all-start.2 = ((bf16[8,2,96,256]{3,2,1,0:T(8,128)(2,1)}), bf16[8,2,96,256]{3,2,1,0:T(8,128)(2,1)S(1)}, u32[]{:S(2)}, u32[]{:S(2)}) async-start(bf16[8,2,96,256]{3,2,1,0:T(8,128)(2,1)} %shard_map.128), calls=%async_computation.2 | async-start | bytes 1572864 | tf_op jit(solution)/shard_map/all_to_all | solution.py:392
  141.9 0.0 collective-permute-done.5.left_tan
  141.9 0.0 copy-start.8
  141.9 0.0 collective-permute-done.6.right_tan
  141.9 0.8 copy-done.8
  142.7 0.8 copy-done.9
  143.5 6.3 %shard_map.126.last = bf16[2,128,512]{2,1,0:T(8,128)(2,1)} custom-call(s32[2]{0:T(128)} %pad_add_fusion.meta, bf16[2,2,128,1024]{3,2,1,0:T(8,128)(2,1)} %get-tuple-element.17.q_ref, bf16[2,2,128,1024]{3,2,1,0:T(8,128)(2,1)} %copy-done.1, bf16[2,2,128,1024]{3,2,1,0:T(8,128)(2,1)} %shard_map.123.mid, bf16[2,2,128,1024]{3,2,1,0:T(8,128)(2,1)} %copy-done.2, ...), custom_call_target="tpu_custom_call" | custom-call | flops 1 | bytes 1 | tf_op jit(solution)/shard_map/pallas_call | solution.py:260
  149.8 0.0 copy-done.6
  149.8 6.3 %shard_map.125.first = bf16[2,128,512]{2,1,0:T(8,128)(2,1)} custom-call(s32[2]{0:T(128)} %pad_add_fusion.meta, bf16[2,2,128,1024]{3,2,1,0:T(8,128)(2,1)} %get-tuple-element.17.q_ref, bf16[2,2,128,1024]{3,2,1,0:T(8,128)(2,1)} %copy-done.1, bf16[2,2,128,1024]{3,2,1,0:T(8,128)(2,1)} %shard_map.123.mid, bf16[2,2,128,1024]{3,2,1,0:T(8,128)(2,1)} %copy-done.2, ...), custom_call_target="tpu_custom_call" | custom-call | flops 1 | bytes 1 | tf_op jit(solution)/shard_map/pallas_call | solution.py:260
  156.0 5.7 %shard_map.127 = (f32[2,2,64,1536]{3,2,1,0:T(8,128)}, f32[2,2,64,1536]{3,2,1,0:T(8,128)}) custom-call(bf16[2,128,1024]{2,1,0:T(8,128)(2,1)} %get-tuple-element.18.att, bf16[2,128,512]{2,1,0:T(8,128)(2,1)} %shard_map.125.first, bf16[2,128,512]{2,1,0:T(8,128)(2,1)} %shard_map.126.last, bf16[1536,1024]{1,0:T(8,128)(2,1)} %bitcast.20, f32[2,1536]{1,0:T(2,128)} %gate.1, ...), custom_call_target="tpu_custom_call" | custom-call | flops 1 | bytes 1 | tf_op jit(solution)/shard_map/pallas_call | solution.py:307
  161.7 2.0 collective-permute-start.7
  163.8 1.0 all-to-all-done.2
  164.7 0.1 convert_reduce_fusion
  164.8 22.3 %all_to_all.20 = f32[8,24,256]{2,1,0:T(8,128)S(1)} all-to-all(f32[8,24,256]{2,1,0:T(8,128)S(1)} %bitcast.25), channel_id=1, replica_groups={{0,2,4,6,256,258,260,262},{1,3,5,7,257,259,261,263},{8,10,12,14,264,266..., dimensions={0} | all-to-all | bytes 393216 | tf_op jit(solution)/shard_map/all_to_all | solution.py:394
  187.1 4.9 %collective-permute-start.9 = (f32[24,256]{1,0:T(8,128)S(1)}, f32[24,256]{1,0:T(8,128)S(1)}, u32[]{:S(2)}, u32[]{:S(2)}) collective-permute-start(f32[24,256]{1,0:T(8,128)S(1)} %reduce_sum.19), channel_id=1, source_target_pairs={{0,0},{1,1},{2,8},{3,9},{4,16},{5,17},{6,24},{7,25},{8,2},{9,3},{1... | collective-permute-start | bytes 73736 | tf_op jit(solution)/shard_map/Turn/ppermute | solution.py:76
  192.0 7.1 %collective-permute-done.9 = f32[24,256]{1,0:T(8,128)S(1)} collective-permute-done((f32[24,256]{1,0:T(8,128)S(1)}, f32[24,256]{1,0:T(8,128)S(1)}, u32[]{:S(2)}, u32[]{:S(2)}) %collective-permute-start.9) | collective-permute-done | bytes 24608 | tf_op jit(solution)/shard_map/Turn/ppermute | solution.py:76
  199.2 0.0 collective-permute-done.7
  199.2 0.0 copy-done.5
  199.2 2.4 %fusion.3 = (bf16[2,64,1536]{2,1,0:T(8,128)(2,1)}, bf16[2,64,1536]{2,1,0:T(8,128)(2,1)}) fusion(f32[2,2,64,1536]{3,2,1,0:T(8,128)} %collective-permute-done.7, f32[2,2,64,1536]{3,2,1,0:T(8,128)S(1)} %copy-done.5), kind=kLoop, calls=%fused_computation.7 | loop fusion | flops 786432 | bytes 3932160 | tf_op jit(solution)/shard_map/convert_element_type | solution.py:403
  201.6 0.6 copy.21
  (15 shorter events, 0.1 us)
Async XLA Ops:
  7.2 83.1 %all-gather.6.cloned.1.call-start = ((), (), s32[]{:S(2)}) async-start(), calls=%async_computation.5 | async-start | bytes 1966080 | tf_op jit(solution)/shard_map/all_gather | solution.py:381
  7.8 8.9 %copy-start.10 = (bf16[2,64,1536]{2,1,0:T(8,128)(2,1)S(1)}, bf16[2,64,1536]{2,1,0:T(8,128)(2,1)}, u32[]{:S(2)}) copy-start(bf16[2,64,1536]{2,1,0:T(8,128)(2,1)} %param.19) | copy-start | bytes 1179652
  7.9 8.9 %copy-start.12 = (f32[2,1536]{1,0:T(2,128)S(1)}, f32[2,1536]{1,0:T(2,128)}, u32[]{:S(2)}) copy-start(f32[2,1536]{1,0:T(2,128)} %gate.1) | copy-start | bytes 36868
  11.2 6.9 %copy-start.11 = (f32[2048,24]{0,1:T(8,128)S(1)}, f32[2048,24]{0,1:T(8,128)}, u32[]{:S(2)}) copy-start(f32[2048,24]{0,1:T(8,128)} %param.16) | copy-start | bytes 589828
  11.2 5.6 %collective-permute-start = (bf16[6,2,64,1024]{3,2,1,0:T(8,128)(2,1)}, bf16[6,2,64,1024]{3,2,1,0:T(8,128)(2,1)S(1)}, u32[]{:S(2)}, u32[]{:S(2)}) collective-permute-start(bf16[6,2,64,1024]{3,2,1,0:T(8,128)(2,1)} %shard_map.121), channel_id=1, source_target_pairs={{0,1},{1,0},{2,3},{3,2},{4,5},{5,4},{6,7},{7,6},{8,9},{9,8},{10,11... | collective-permute-start | bytes 4718600 | tf_op jit(solution)/shard_map/Sx/ppermute | solution.py:76
  16.8 2.7 %copy-start = (bf16[6,2,64,1024]{3,2,1,0:T(8,128)(2,1)}, bf16[6,2,64,1024]{3,2,1,0:T(8,128)(2,1)S(1)}, u32[]{:S(2)}) copy-start(bf16[6,2,64,1024]{3,2,1,0:T(8,128)(2,1)S(1)} %collective-permute-done.refs_4_.refs_2_) | copy-start | bytes 4718596
  19.5 48.6 %all-to-all-start.1 = ((bf16[16,24,1024]{2,1,0:T(8,128)(2,1)}), bf16[16,24,1024]{2,1,0:T(8,128)(2,1)S(1)}, u32[]{:S(2)}, u32[]{:S(2)}) async-start(bf16[16,24,1024]{2,1,0:T(8,128)(2,1)} %broadcast_in_dim.2), calls=%async_computation.1 | async-start | bytes 1572864 | tf_op jit(solution)/shard_map/all_to_all | solution.py:369
  31.3 124.7 %all-gather.4.cloned.1.call-start = ((), (), s32[]{:S(2)}) async-start(), calls=%async_computation.4 | async-start | bytes 3932160 | tf_op jit(solution)/shard_map/all_gather | solution.py:385
  34.2 58.1 %collective-permute-start.1 = (bf16[2,2,128,1024]{3,2,1,0:T(8,128)(2,1)}, bf16[2,2,128,1024]{3,2,1,0:T(8,128)(2,1)S(1)}, u32[]{:S(2)}, u32[]{:S(2)}) collective-permute-start(bf16[2,2,128,1024]{3,2,1,0:T(8,128)(2,1)} %shard_map.123.mid), channel_id=1, source_target_pairs={{0,2},{1,3},{2,4},{3,5},{4,6},{5,7},{6,8},{7,9},{8,10},{9,11},{10,... | collective-permute-start | bytes 3145736 | tf_op jit(solution)/shard_map/Ha/ppermute | solution.py:76
  39.0 61.7 %collective-permute-start.2 = (bf16[2,2,128,1024]{3,2,1,0:T(8,128)(2,1)}, bf16[2,2,128,1024]{3,2,1,0:T(8,128)(2,1)S(1)}, u32[]{:S(2)}, u32[]{:S(2)}) collective-permute-start(bf16[2,2,128,1024]{3,2,1,0:T(8,128)(2,1)} %shard_map.123.mid), channel_id=1, source_target_pairs={{2,0},{3,1},{4,2},{5,3},{6,4},{7,5},{8,6},{9,7},{10,8},{11,9},{12,... | collective-permute-start | bytes 3145736 | tf_op jit(solution)/shard_map/Hb/ppermute | solution.py:76
  68.1 0.9 copy-start.3
  72.6 49.5 %collective-permute-start.3 = (bf16[2,2,128,512]{3,2,1,0:T(8,128)(2,1)}, bf16[2,2,128,512]{3,2,1,0:T(8,128)(2,1)S(1)}, u32[]{:S(2)}, u32[]{:S(2)}) collective-permute-start(bf16[2,2,128,512]{3,2,1,0:T(8,128)(2,1)} %get-tuple-element.22.mid_tan), channel_id=1, source_target_pairs={{0,2},{1,3},{2,4},{3,5},{4,6},{5,7},{6,8},{7,9},{8,10},{9,11},{10,... | collective-permute-start | bytes 1572872 | tf_op jit(solution)/shard_map/T0a/ppermute | solution.py:76
  77.4 44.7 %collective-permute-start.4 = (bf16[2,2,128,512]{3,2,1,0:T(8,128)(2,1)}, bf16[2,2,128,512]{3,2,1,0:T(8,128)(2,1)}, u32[]{:S(2)}, u32[]{:S(2)}) collective-permute-start(bf16[2,2,128,512]{3,2,1,0:T(8,128)(2,1)} %get-tuple-element.22.mid_tan), channel_id=1, source_target_pairs={{2,0},{3,1},{4,2},{5,3},{6,4},{7,5},{8,6},{9,7},{10,8},{11,9},{12,... | collective-permute-start | bytes 1572872 | tf_op jit(solution)/shard_map/T0b/ppermute | solution.py:76
  90.3 36.9 %collective-permute-start.8 = (bf16[4,1536,128]{2,1,0:T(8,128)(2,1)}, bf16[4,1536,128]{2,1,0:T(8,128)(2,1)}, u32[]{:S(2)}, u32[]{:S(2)}) collective-permute-start(bf16[4,1536,128]{2,1,0:T(8,128)(2,1)} %bitcast.21), channel_id=1, source_target_pairs={{0,1},{1,0},{2,3},{3,2},{4,5},{5,4},{6,7},{7,6},{8,9},{9,8},{10,11... | collective-permute-start | bytes 4718600 | tf_op jit(solution)/shard_map/Cswap/ppermute | solution.py:76
  92.2 8.4 %copy-start.1 = (bf16[2,2,128,1024]{3,2,1,0:T(8,128)(2,1)}, bf16[2,2,128,1024]{3,2,1,0:T(8,128)(2,1)S(1)}, u32[]{:S(2)}) copy-start(bf16[2,2,128,1024]{3,2,1,0:T(8,128)(2,1)S(1)} %collective-permute-done.1.left) | copy-start | bytes 3145732
  100.6 1.0 copy-start.2
  101.6 13.7 %copy-start.7 = (bf16[2,2,128,512]{3,2,1,0:T(8,128)(2,1)S(1)}, bf16[2,2,128,512]{3,2,1,0:T(8,128)(2,1)}, u32[]{:S(2)}) copy-start(bf16[2,2,128,512]{3,2,1,0:T(8,128)(2,1)} %get-tuple-element.25.mid_tan) | copy-start | bytes 1572868
  110.6 16.7 %all-to-all-start = ((bf16[4,2,128,256]{3,2,1,0:T(8,128)(2,1)}), bf16[4,2,128,256]{3,2,1,0:T(8,128)(2,1)S(1)}, u32[]{:S(2)}, u32[]{:S(2)}) async-start(bf16[4,2,128,256]{3,2,1,0:T(8,128)(2,1)} %get-tuple-element.19), calls=%async_computation | async-start | bytes 1048576 | tf_op jit(solution)/shard_map/all_to_all | solution.py:389
  115.3 26.6 %collective-permute-start.5 = (bf16[2,2,128,512]{3,2,1,0:T(8,128)(2,1)S(1)}, bf16[2,2,128,512]{3,2,1,0:T(8,128)(2,1)S(1)}, u32[]{:S(2)}, u32[]{:S(2)}) collective-permute-start(bf16[2,2,128,512]{3,2,1,0:T(8,128)(2,1)S(1)} %copy-done.7), channel_id=1, source_target_pairs={{0,2},{1,3},{2,4},{3,5},{4,6},{5,7},{6,8},{7,9},{8,10},{9,11},{10,... | collective-permute-start | bytes 1572872 | tf_op jit(solution)/shard_map/T1a/ppermute | solution.py:76
  118.6 23.3 %collective-permute-start.6 = (bf16[2,2,128,512]{3,2,1,0:T(8,128)(2,1)S(1)}, bf16[2,2,128,512]{3,2,1,0:T(8,128)(2,1)S(1)}, u32[]{:S(2)}, u32[]{:S(2)}) collective-permute-start(bf16[2,2,128,512]{3,2,1,0:T(8,128)(2,1)S(1)} %copy-done.7), channel_id=1, source_target_pairs={{2,0},{3,1},{4,2},{5,3},{6,4},{7,5},{8,6},{9,7},{10,8},{11,9},{12,... | collective-permute-start | bytes 1572872 | tf_op jit(solution)/shard_map/T1b/ppermute | solution.py:76
  122.1 27.7 %copy-start.6 = (bf16[2,2,128,512]{3,2,1,0:T(8,128)(2,1)}, bf16[2,2,128,512]{3,2,1,0:T(8,128)(2,1)S(1)}, u32[]{:S(2)}) copy-start(bf16[2,2,128,512]{3,2,1,0:T(8,128)(2,1)S(1)} %collective-permute-done.3.left_tan) | copy-start | bytes 1572868
  127.2 0.8 copy-start.4
  132.7 32.0 %all-to-all-start.2 = ((bf16[8,2,96,256]{3,2,1,0:T(8,128)(2,1)}), bf16[8,2,96,256]{3,2,1,0:T(8,128)(2,1)S(1)}, u32[]{:S(2)}, u32[]{:S(2)}) async-start(bf16[8,2,96,256]{3,2,1,0:T(8,128)(2,1)} %shard_map.128), calls=%async_computation.2 | async-start | bytes 1572864 | tf_op jit(solution)/shard_map/all_to_all | solution.py:392
  141.9 0.8 copy-start.8
  142.7 0.8 copy-start.9
  161.7 37.4 %copy-start.5 = (f32[2,2,64,1536]{3,2,1,0:T(8,128)S(1)}, f32[2,2,64,1536]{3,2,1,0:T(8,128)}, u32[]{:S(2)}) copy-start(f32[2,2,64,1536]{3,2,1,0:T(8,128)} %get-tuple-element.26) | copy-start | bytes 4718596
  161.7 37.4 %collective-permute-start.7 = (f32[2,2,64,1536]{3,2,1,0:T(8,128)}, f32[2,2,64,1536]{3,2,1,0:T(8,128)}, u32[]{:S(2)}, u32[]{:S(2)}) collective-permute-start(f32[2,2,64,1536]{3,2,1,0:T(8,128)} %get-tuple-element.27), channel_id=1, source_target_pairs={{0,1},{1,0},{2,3},{3,2},{4,5},{5,4},{6,7},{7,6},{8,9},{9,8},{10,11... | collective-permute-start | bytes 4718600 | tf_op jit(solution)/shard_map/Pswap/ppermute | solution.py:76
  187.1 12.0 %collective-permute-start.9 = (f32[24,256]{1,0:T(8,128)S(1)}, f32[24,256]{1,0:T(8,128)S(1)}, u32[]{:S(2)}, u32[]{:S(2)}) collective-permute-start(f32[24,256]{1,0:T(8,128)S(1)} %reduce_sum.19), channel_id=1, source_target_pairs={{0,0},{1,1},{2,8},{3,9},{4,16},{5,17},{6,24},{7,25},{8,2},{9,3},{1... | collective-permute-start | bytes 73736 | tf_op jit(solution)/shard_map/Turn/ppermute | solution.py:76
Sparse Core Ops, SparseCore 0:
  18.2 35.0 all-gather.5
  69.2 60.3 all-gather.3
